TPU v7x, 256 devices: a whole 4x4x8 slice. The times are simulated.
256 devices in a mesh: section: 32 (over x, z_hi, y), dp: 8 (over z_lo, core).
Axes of the slice: x: 4, y: 4, z: 8 (z_hi: 2, z_lo: 4; z = z_hi * 4 + z_lo), core: 2. Of those that a mesh axis runs over, the one named last changes fastest.
Arguments:
- saved_entering_lanes: bfloat16 [32, 2, 1024, 4, 1024], P('section', None, 'dp'), may hold values from -6 to 6
- opening_adjoint: bfloat16 [32, 1024, 4, 1024], P('section', 'dp'), may hold values from -6 to 6
- final_later_adjoint: bfloat16 [1, 1024, 4, 1024], P(None, 'dp'), may hold values from -6 to 6
- document_labels: int32 [32, 2, 1024], P('section', None, 'dp'), may hold values from 0 to 63, never falling along the last dimension, each value on 1 to 48 neighbouring positions
- blend_linear_map: float32 [32, 4096, 24], P('section'), may hold values from -0.1875 to 0.1875
- rescale_amplitude: float32 [32, 1024], P('section'), may hold values from 0.5 to 1.5
- attend_entry_maps: bfloat16 [32, 1024, 1536], P('section'), may hold values from -0.1875 to 0.1875
- attend_exit_map: bfloat16 [32, 512, 1024], P('section'), may hold values from -0.25 to 0.25
Outputs:
- sent: bfloat16 [32, 2, 1024, 4, 1024], P('section', None, 'dp')
- grad_qkv: float32 [32, 1024, 1536], P('section', 'dp')
- grad_out: float32 [32, 512, 1024], P('section', 'dp')
- grad_proj: float32 [32, 4096, 24], P('section', 'dp')
- grad_gain: float32 [32, 1024], P('section', 'dp')
Inputs may be any that keep to these rules, and one draw needn't show every extreme that they name: `document_labels`: along a microbatch's row of 1024 tokens the segment ids never fall.
All inputs are finite; a program needn't handle non-finite values.
Results may differ from a plain program's by a relative error of at most 0.03.
Values may be sent and summed in bfloat16 or wider, within the bound.
No kernel may reach another device: no remote copies, remote signals or barrier semaphores. Data moves between devices by JAX's collectives and lax.ppermute only.
A program may use at most 128 MiB of HBM per device.

v0:
```python
import jax
import jax.numpy as jnp
from jax import lax
from jax.experimental import pallas as pl
from jax.experimental.pallas import tpu as pltpu
from jax.sharding import PartitionSpec as P

F32 = jnp.float32
BF16 = jnp.bfloat16
LANES = 4
D = 1024
T = 128
HEADS = 8
PAIRS = HEADS // 2
INNER = 512
SINK = 20
EPS = 1e-6
ROWS = 16
SHARD_ROWS = 288
QKV_TAIL = 128
OUT_AT = 192
PROJ_AT = 256
GAIN_AT = 272
NN = (((1,), (0,)), ((), ()))
NT = (((1,), (1,)), ((), ()))
TN = (((0,), (0,)), ((), ()))


def dot(a, b, dims=NN):
    return lax.dot_general(a, b, dims, preferred_element_type=F32)


def split(value):
    high = value.astype(BF16)
    return high, (value - high.astype(F32)).astype(BF16)


def iota(shape, axis):
    return lax.broadcasted_iota(jnp.int32, shape, axis)


def group_sum(block):
    block = block + pltpu.roll(block, 1, 0)
    return block + pltpu.roll(block, 2, 0)


def doubled(block):
    lower = iota(block.shape, 0) < 4
    turned = pltpu.roll(block, 4, 0)
    return jnp.where(lower, block, turned), jnp.where(lower, turned, block)


def tokens_first(rows):
    short = 128 - rows.shape[0]
    if short:
        rows = jnp.concatenate([rows, jnp.zeros((short, T), F32)], axis=0)
    return rows.T


def head_ones():
    return (iota((128, 128), 0) // 64 == iota((128, 128), 1) // 64).astype(BF16)


def head_mean(value, ones):
    high, low = split(value)
    return (dot(high, ones) + dot(low, ones)) * (1.0 / 64.0)


def half_masks():
    low = iota((1, 128), 1) < 64
    return low, [low.astype(F32).astype(BF16), (~low).astype(F32).astype(BF16)]


def stacked_map(bt_ref, bhl):
    high, low = split(jnp.concatenate([bt_ref[...], jnp.zeros((8, LANES * D), F32)], axis=0))
    bhl[0:32, :] = high
    bhl[32:64, :] = low


def forward(x, bhl, gain, w, wo, seg, s):
    eye = iota((T, T), 0) == iota((T, T), 1)
    raw = jnp.zeros((64, T), F32)
    square = jnp.zeros((T, T), F32)
    for j in range(LANES):
        raw = raw + dot(bhl[:, j * D : (j + 1) * D], x[j], NT)
        square = square + dot(x[j], x[j], NT)
    mean = jnp.sum(jnp.where(eye, square, 0.0), axis=0, keepdims=True) * (1.0 / (LANES * D))
    inv = lax.rsqrt(mean + EPS)
    mc = (raw[0:24] + raw[32:56]) * inv
    s["mc"][...] = jnp.concatenate([mc, jnp.broadcast_to(inv, (8, T))], axis=0)
    lower = iota((8, T), 0) < 4
    gates = jax.nn.sigmoid(mc[0:8])
    gates = jnp.where(lower, gates, 2.0 * gates)
    first = doubled(jnp.exp(mc[8:16]))
    second = doubled(jnp.exp(mc[16:24]))

    def one_round(index, current):
        sums = [1.0 / group_sum(a) for a in current]
        current = [a * b for a, b in zip(current, sums)]
        for i in range(LANES):
            s["sink"][index, i] = current[i]
            s["sink"][index, 4 + i] = sums[i]
        total = 1.0 / ((current[0] + current[1]) + (current[2] + current[3]))
        current = [a * total for a in current]
        for i in range(LANES):
            s["sink"][index, 8 + i] = current[i]
        s["sink"][index, 12] = total
        return tuple(current)

    settled = lax.fori_loop(0, SINK, one_round, first + second)
    s["coef"][...] = tokens_first(
        jnp.concatenate(
            [
                gates,
                jnp.where(lower, settled[0], settled[1]),
                jnp.where(lower, settled[2], settled[3]),
            ],
            axis=0,
        )
    )

    def join_rows(block, _):
        rows = pl.ds(pl.multiple_of(block * ROWS, ROWS), ROWS)
        c = s["coef"][rows, :]
        joined = c[:, 0:1] * x[0, rows, :].astype(F32)
        for i in range(1, LANES):
            joined = joined + c[:, i : i + 1] * x[i, rows, :].astype(F32)
        r = lax.rsqrt(jnp.mean(joined * joined, axis=-1, keepdims=True) + EPS)
        s["joined"][rows, :] = joined
        s["r"][rows, :] = jnp.broadcast_to(r, (ROWS, 128))
        s["normed"][rows, :] = (joined * r * gain[...]).astype(BF16)
        return 0

    lax.fori_loop(0, T // ROWS, join_rows, 0)
    projected = dot(s["normed"][...], w[...]).astype(BF16)
    s["proj"][...] = projected
    ones = head_ones()
    for at in range(2 * PAIRS):
        lanes = slice(at * 128, at * 128 + 128)
        wide = projected[:, lanes].astype(F32)
        scale = lax.rsqrt(head_mean(wide * wide, ones) + EPS)
        s["scale"][:, lanes] = scale
        s["qk"][:, lanes] = (wide * scale).astype(BF16)
    ids = jnp.broadcast_to(seg[...].astype(F32), (T, T))
    allowed = (ids == ids.T) & (iota((T, T), 1) <= iota((T, T), 0))
    low, masks = half_masks()
    for pair in range(PAIRS):
        lanes = slice(pair * 128, pair * 128 + 128)
        q = s["qk"][:, lanes]
        k = s["qk"][:, pl.ds(INNER + pair * 128, 128)]
        v = s["proj"][:, pl.ds(2 * INNER + pair * 128, 128)]
        parts = []
        for half in range(2):
            scores = dot(q * masks[half], k, NT) * 0.125
            free = jnp.where(allowed, jnp.exp(scores), 0.0)
            weights = free / jnp.sum(free, axis=-1, keepdims=True)
            s["weights"][2 * pair + half] = weights
            parts.append(dot(weights.astype(BF16), v))
        s["ctx"][:, lanes] = jnp.where(low, parts[0], parts[1]).astype(BF16)
    s["att"][...] = dot(s["ctx"][...], wo[...]).astype(BF16)


def diagonal(product, eye):
    return jnp.sum(jnp.where(eye, product, 0.0), axis=0, keepdims=True)


def by_sublane(rows):
    at = iota((8, T), 0) % 4
    block = jnp.broadcast_to(rows[3], (8, T))
    for k in range(3):
        block = jnp.where(at == k, jnp.broadcast_to(rows[k], (8, T)), block)
    return block


def backward(x, g, bhl, gain, w, wo, s, o, t):
    eye = iota((T, T), 0) == iota((T, T), 1)

    def att_rows(block, _):
        rows = pl.ds(pl.multiple_of(block * ROWS, ROWS), ROWS)
        c = s["coef"][rows, :]
        total = c[:, 4:5] * g[0, rows, :].astype(F32)
        for i in range(1, LANES):
            total = total + c[:, 4 + i : 5 + i] * g[i, rows, :].astype(F32)
        o["datt"][rows, :] = total.astype(BF16)
        return 0

    lax.fori_loop(0, T // ROWS, att_rows, 0)
    dctx = dot(o["datt"][...], wo[...], NT).astype(BF16)
    low, masks = half_masks()
    ones = head_ones()

    def norm_back(dn, at):
        lanes = pl.ds(at * 128, 128)
        wide = s["proj"][:, lanes].astype(F32)
        scale = s["scale"][:, lanes]
        dn = dn.astype(BF16).astype(F32)
        moment = head_mean(dn * wide, ones)
        o["dproj"][:, lanes] = (scale * (dn - wide * (scale * scale * moment))).astype(BF16)

    for pair in range(PAIRS):
        lanes = slice(pair * 128, pair * 128 + 128)
        q = s["qk"][:, lanes]
        k = s["qk"][:, pl.ds(INNER + pair * 128, 128)]
        v = s["proj"][:, pl.ds(2 * INNER + pair * 128, 128)]
        dc = dctx[:, lanes]
        dq, dk, dv = [], [], []
        for half in range(2):
            weights = s["weights"][2 * pair + half]
            dw = dot(dc * masks[half], v, NT).astype(BF16).astype(F32)
            dscore = weights * (dw - jnp.sum(dw * weights, axis=-1, keepdims=True)) * 0.125
            dq.append(dot(dscore.astype(BF16), k))
            dk.append(dot(dscore.T.astype(BF16), q))
            dv.append(dot(weights.T.astype(BF16), dc))
        o["dproj"][:, pl.ds(2 * INNER + pair * 128, 128)] = jnp.where(low, dv[0], dv[1]).astype(BF16)
        norm_back(jnp.where(low, dq[0], dq[1]), pair)
        norm_back(jnp.where(low, dk[0], dk[1]), PAIRS + pair)
    t["dn"][...] = dot(o["dproj"][...], w[...], NT).astype(BF16)

    def joined_rows(block, total):
        rows = pl.ds(pl.multiple_of(block * ROWS, ROWS), ROWS)
        r = s["r"][rows, 0:1]
        joined = s["joined"][rows, :]
        dn = t["dn"][rows, :].astype(F32)
        total = total + jnp.sum(dn * (joined * r), axis=0, keepdims=True)
        scaled = dn * gain[...]
        moment = jnp.mean(scaled * joined, axis=-1, keepdims=True)
        t["dj"][rows, :] = r * scaled - joined * (r * r * r * moment)
        return total

    o["dgain"][...] = lax.fori_loop(0, T // ROWS, joined_rows, jnp.zeros((1, D), F32))

    dj = t["dj"][...].astype(BF16)
    pre = [diagonal(dot(dj, x[j], NT), eye) for j in range(LANES)]
    post = [diagonal(dot(g[i], s["att"][...], NT), eye) for i in range(LANES)]
    dmix = tuple(
        by_sublane([diagonal(dot(g[i], x[j], NT), eye) for j in range(LANES)])
        for i in range(LANES)
    )

    def one_round(step, current):
        index = SINK - 1 - step
        after = [s["sink"][index, 8 + i] for i in range(LANES)]
        pull = [a * b for a, b in zip(current, after)]
        pull = (pull[0] + pull[1]) + (pull[2] + pull[3])
        total = s["sink"][index, 12]
        current = [(a - pull) * total for a in current]
        between = [s["sink"][index, i] for i in range(LANES)]
        sums = [s["sink"][index, 4 + i] for i in range(LANES)]
        return tuple(
            (a - group_sum(a * b)) * c for a, b, c in zip(current, between, sums)
        )

    dmix = lax.fori_loop(0, SINK, one_round, dmix)
    lower = iota((8, T), 0) < 4
    mc = s["mc"][...]
    inv = mc[24:32]
    gates = jax.nn.sigmoid(mc[0:8])
    dgates = jnp.where(lower, by_sublane(pre), 2.0 * by_sublane(post))
    dmc = [
        dgates * gates * (1.0 - gates),
        jnp.where(lower, dmix[0], dmix[1]) * jnp.exp(mc[8:16]),
        jnp.where(lower, dmix[2], dmix[3]) * jnp.exp(mc[16:24]),
    ]
    dot_mc = dmc[0] * mc[0:8] + dmc[1] * mc[8:16] + dmc[2] * mc[16:24]
    dot_mc = jnp.sum(dot_mc, axis=0, keepdims=True)
    kappa = inv * inv * dot_mc * (1.0 / (LANES * D))
    scaled = jnp.concatenate([a * inv for a in dmc] + [jnp.zeros((8, T), F32)], axis=0)
    back = tokens_first(jnp.concatenate([scaled, scaled, kappa], axis=0))
    t["back"][...] = back
    lead = back[:, 0:64].astype(BF16)
    rows_first = scaled.astype(BF16)
    for j in range(LANES):
        cols = slice(j * D, (j + 1) * D)
        o["dproj_map"][:, cols] = dot(rows_first, x[j])
        t["f"][j] = dot(lead, bhl[:, cols])

    def stream_rows(block, _):
        rows = pl.ds(pl.multiple_of(block * ROWS, ROWS), ROWS)
        c = s["coef"][rows, :]
        kap = t["back"][rows, 64:65]
        dj = t["dj"][rows, :]
        gs = [g[i, rows, :].astype(F32) for i in range(LANES)]
        for j in range(LANES):
            total = t["f"][j, rows, :] + c[:, j : j + 1] * dj - kap * x[j, rows, :].astype(F32)
            for i in range(LANES):
                at = 8 + LANES * i + j
                total = total + c[:, at : at + 1] * gs[i]
            o["dx"][j, rows, :] = total.astype(BF16)
        return 0

    lax.fori_loop(0, T // ROWS, stream_rows, 0)


SAVED = (
    ("mc", (32, T), F32),
    ("sink", (SINK, 13, 8, T), F32),
    ("coef", (T, 128), F32),
    ("joined", (T, D), F32),
    ("r", (T, 128), F32),
    ("normed", (T, D), BF16),
    ("proj", (T, 3 * INNER), BF16),
    ("scale", (T, 2 * INNER), F32),
    ("qk", (T, 2 * INNER), BF16),
    ("weights", (HEADS, T, T), F32),
    ("ctx", (T, INNER), BF16),
    ("att", (T, D), BF16),
)
BACK = (
    ("dx", (LANES, T, D), BF16),
    ("dproj", (T, 3 * INNER), BF16),
    ("datt", (T, D), BF16),
    ("dproj_map", (32, LANES * D), F32),
    ("dgain", (1, D), F32),
)
TEMPS = (
    ("dn", (T, D), BF16),
    ("dj", (T, D), F32),
    ("back", (T, 128), F32),
    ("f", (LANES, T, D), F32),
)
KEPT = ("normed", "ctx")
BHL = (64, LANES * D)


def shapes(table):
    return [jax.ShapeDtypeStruct(shape, dtype) for _, shape, dtype in table]


def scratch(table):
    return [pltpu.VMEM(shape, dtype) for _, shape, dtype in table]


def named(table, refs):
    return {name: ref for (name, _, _), ref in zip(table, refs)}


def call(body, outs, scratches, args, flops, name):
    moved = sum(a.size * a.dtype.itemsize for a in args)
    moved += sum(a.size * a.dtype.itemsize for a in outs)
    whole = pl.BlockSpec(memory_space=pltpu.VMEM)
    return pl.pallas_call(
        body,
        out_shape=outs,
        in_specs=[whole] * len(args),
        out_specs=[whole] * len(outs),
        scratch_shapes=scratches,
        compiler_params=pltpu.CompilerParams(vmem_limit_bytes=56 * 1024 * 1024),
        cost_estimate=pl.CostEstimate(flops=flops, bytes_accessed=moved, transcendentals=0),
        name=name,
    )(*args)


SAVED_IN = [e for e in SAVED if e[0] not in KEPT]
SAVED_OUT = [e for e in SAVED if e[0] in KEPT]


def whole_tick(x, g, seg, bt, gain, w, wo):
    def body(x, g, seg, bt, gain, w, wo, *rest):
        outs = rest[: len(BACK) + len(KEPT)]
        rest = rest[len(outs) :]
        o = named(BACK, outs)
        s = named(SAVED_OUT, outs[len(BACK) :])
        s.update(named(SAVED_IN, rest))
        rest = rest[len(SAVED_IN) :]
        t = named(TEMPS, rest)
        bhl = rest[len(TEMPS)]
        stacked_map(bt, bhl)
        forward(x, bhl, gain, w, wo, seg, s)
        backward(x, g, bhl, gain, w, wo, s, o, t)

    return call(
        body,
        shapes(BACK) + shapes(SAVED_OUT),
        scratch(SAVED_IN) + scratch(TEMPS) + [pltpu.VMEM(BHL, BF16)],
        (x, g, seg, bt, gain, w, wo),
        4_000_000_000,
        "whole_tick",
    )


def forward_tick(x, seg, bt, gain, w, wo):
    def body(x, seg, bt, gain, w, wo, *outs):
        bhl = outs[len(SAVED)]
        stacked_map(bt, bhl)
        forward(x, bhl, gain, w, wo, seg, named(SAVED, outs))

    saved = call(
        body,
        shapes(SAVED) + [jax.ShapeDtypeStruct(BHL, BF16)],
        [],
        (x, seg, bt, gain, w, wo),
        1_000_000_000,
        "forward_tick",
    )
    return saved


def fill_shards(first, second, out, n):
    rows = D // n
    normed = jnp.concatenate([first["normed"][...], second["normed"][...]], axis=0)
    for at in range(6):
        cols = slice(at * 256, at * 256 + 256)
        right = jnp.concatenate([first["dproj"][:, cols], second["dproj"][:, cols]], axis=0)
        product = dot(normed, right, TN).astype(BF16)
        for d in range(n):
            part = product[d * rows : (d + 1) * rows]
            if at < 4:
                out[d, 0:rows, cols] = part
            else:
                left = (at - 4) * 256
                half = rows // 2
                out[d, QKV_TAIL : QKV_TAIL + half, left : left + 256] = part[0:half]
                out[d, QKV_TAIL : QKV_TAIL + half, 512 + left : 768 + left] = part[half:]
    ctx = jnp.concatenate([first["ctx"][...], second["ctx"][...]], axis=0)
    rows = INNER // n
    for at in range(4):
        cols = slice(at * 256, at * 256 + 256)
        right = jnp.concatenate([first["datt"][:, cols], second["datt"][:, cols]], axis=0)
        product = dot(ctx, right, TN).astype(BF16)
        for d in range(n):
            out[d, OUT_AT : OUT_AT + rows, cols] = product[d * rows : (d + 1) * rows]
    for d in range(n):
        cols = slice(d * 512, d * 512 + 512)
        proj = first["dproj_map"][:, cols] + second["dproj_map"][:, cols]
        out[d, PROJ_AT : PROJ_AT + 16, 0:512] = proj[0:16].astype(BF16)
        out[d, PROJ_AT : PROJ_AT + 16, 512:1024] = proj[16:32].astype(BF16)
        gain = first["dgain"][:, d * 128 : d * 128 + 128] + second["dgain"][:, d * 128 : d * 128 + 128]
        out[d, GAIN_AT : GAIN_AT + 16, 0:128] = jnp.broadcast_to(gain, (16, 128)).astype(BF16)
        out[d, GAIN_AT : GAIN_AT + 16, 128:1024] = jnp.zeros((16, 896), BF16)


EARLIER = ("dproj", "datt", "dproj_map", "dgain", "normed", "ctx")


def backward_tick(x, g, gain, w, wo, saved, earlier, n):
    def body(x, g, gain, w, wo, *rest):
        s = named(SAVED, rest)
        bhl = rest[len(SAVED)]
        rest = rest[len(SAVED) + 1 :]
        first = dict(zip(EARLIER, rest))
        rest = rest[len(EARLIER) :]
        o = {"dx": rest[0]}
        out = rest[1]
        rest = rest[2:]
        o.update(named(BACK[1:], rest))
        t = named(TEMPS, rest[len(BACK) - 1 :])
        backward(x, g, bhl, gain, w, wo, s, o, t)
        second = dict(o)
        second["normed"] = s["normed"]
        second["ctx"] = s["ctx"]
        fill_shards(first, second, out, n)

    return call(
        body,
        shapes(BACK[:1]) + [jax.ShapeDtypeStruct((n, SHARD_ROWS, D), BF16)],
        scratch(BACK[1:]) + scratch(TEMPS),
        (x, g, gain, w, wo, *saved, *[earlier[k] for k in EARLIER]),
        4_000_000_000,
        "backward_tick",
    )


def shards(
    saved_entering_lanes,
    opening_adjoint,
    final_later_adjoint,
    document_labels,
    blend_linear_map,
    rescale_amplitude,
    attend_entry_maps,
    attend_exit_map,
):
    n = lax.axis_size("dp")
    layers = lax.axis_size("section")
    last = lax.axis_index("section") == layers - 1
    lanes_first = lambda a: jnp.transpose(a, (1, 0, 2))
    x0 = lanes_first(saved_entering_lanes[0, 0])
    x1 = lanes_first(saved_entering_lanes[0, 1])
    opening = lanes_first(opening_adjoint[0])
    final = lanes_first(final_later_adjoint[0])
    bt = blend_linear_map[0].T
    gain = rescale_amplitude
    w = attend_entry_maps[0]
    wo = attend_exit_map[0]
    outs = whole_tick(x0, opening, document_labels[0, 0:1], bt, gain, w, wo)
    earlier = dict(zip([e[0] for e in BACK] + [e[0] for e in SAVED_OUT], outs))
    dx0 = earlier["dx"]
    received = lax.ppermute(dx0, "section", [(i + 1, i) for i in range(layers - 1)])
    saved = forward_tick(x1, document_labels[0, 1:2], bt, gain, w, wo)
    later = jnp.where(last, final, received)
    dx1, terms = backward_tick(x1, later, gain, w, wo, saved, earlier, n)
    mine = lax.psum_scatter(terms, "dp", scatter_dimension=0, tiled=False)
    sent = jnp.stack([jnp.transpose(dx0, (1, 0, 2)), jnp.transpose(dx1, (1, 0, 2))])[None]
    mine = mine.astype(F32)
    rows = D // n
    half = rows // 2
    tail = mine[QKV_TAIL : QKV_TAIL + half]
    tail = jnp.concatenate([tail[:, :512], tail[:, 512:]], axis=0)
    grad_qkv = jnp.concatenate([mine[:rows], tail], axis=1)
    grad_out = mine[OUT_AT : OUT_AT + INNER // n]
    proj = jnp.concatenate(
        [mine[PROJ_AT : PROJ_AT + 16, :512], mine[PROJ_AT : PROJ_AT + 8, 512:]], axis=0
    )
    return (
        sent,
        grad_qkv[None],
        grad_out[None],
        proj.T[None],
        mine[GAIN_AT : GAIN_AT + 1, :rows],
    )


def solution(mesh):
    return jax.shard_map(
        shards,
        mesh=mesh,
        in_specs=(
            P("section", None, "dp", None, None),
            P("section", "dp", None, None),
            P(None, "dp", None, None),
            P("section", None, "dp"),
            P("section", None, None),
            P("section", None),
            P("section", None, None),
            P("section", None, None),
        ),
        out_specs=(
            P("section", None, "dp", None, None),
            P("section", "dp", None),
            P("section", "dp", None),
            P("section", "dp", None),
            P("section", "dp"),
        ),
        check_vma=False,
    )
```

profile of v0, /device:TPU:30, one launch (start us, length us, event | category | flops | bytes accessed | tf_op | source)
XLA Modules:
  0.0 185.9 jit_solution(10114871404849746309)
XLA Ops:
  7.2 0.0 copy-start
  7.2 0.0 reduce-scatter.2.cloned.1.call-start
  7.2 1.4 slice_bitcast_fusion.1
  8.6 2.5 %copy.26 = bf16[1,128,4,1024]{3,1,2,0:T(8,128)(2,1)} copy(bf16[1,128,4,1024]{3,2,1,0:T(4,128)(2,1)} %param.9) | data formatting | bytes 2097152 | tf_op args[1]
  11.1 0.0 copy-done
  11.1 0.7 fusion
  11.8 1.3 copy.25
  13.1 20.9 %whole_tick.1 = (bf16[4,128,1024]{2,1,0:T(8,128)(2,1)}, bf16[128,1536]{1,0:T(8,128)(2,1)}, bf16[128,1024]{1,0:T(8,128)(2,1)}, f32[32,4096]{1,0:T(8,128)}, f32[1,...) custom-call(bf16[4,128,1024]{2,1,0:T(8,128)(2,1)} %bitcast.55, bf16[4,128,1024]{2,1,0:T(8,128)(2,1)} %bitcast.54, ...), custom_call_target="tpu_custom_call" | custom-call | flops 4000000000 | bytes 9314816 | tf_op jit(solution)/shard_map/whole_tick/pallas_call | solution.py:341
  34.0 2.8 %collective-permute-start = (bf16[4,128,1024]{2,1,0:T(8,128)(2,1)}, bf16[4,128,1024]{2,1,0:T(8,128)(2,1)S(1)}, u32[]{:S(2)}, u32[]{:S(2)}) collective-permute-start(bf16[4,128,1024]{2,1,0:T(8,128)(2,1)} %get-tuple-element.27), channel_id=1, source_target_pairs={{8,0},{16,8},{24,16},{32,24},{40,32},{48,40},{56,48},{64,56},{72,6... | collective-permute-start | bytes 3145736 | tf_op jit(solution)/shard_map/ppermute | solution.py:488
  36.9 1.3 copy.24
  38.2 0.0 copy-start.1
  38.2 9.5 %forward_tick.1 = (f32[32,128]{1,0:T(8,128)}, f32[20,13,8,128]{3,2,1,0:T(8,128)}, f32[128,128]{1,0:T(8,128)}, f32[128,1024]{1,0:T(8,128)}, f32[128,128]{1,0:T(8,...) custom-call(bf16[4,128,1024]{2,1,0:T(8,128)(2,1)} %bitcast.46, ...), custom_call_target="tpu_custom_call" | custom-call | flops 1000000000 | bytes 10260992 | tf_op jit(solution)/shard_map/forward_tick/pallas_call | solution.py:341
  47.7 25.6 %collective-permute-done = bf16[4,128,1024]{2,1,0:T(8,128)(2,1)S(1)} collective-permute-done((bf16[4,128,1024]{2,1,0:T(8,128)(2,1)}, bf16[4,128,1024]{2,1,0:T(8,128)(2,1)S(1)}, u32[]{:S(2)}, u32[]{:S(2)}) %collective-permute-start) | collective-permute-done | bytes 1048608 | tf_op jit(solution)/shard_map/ppermute | solution.py:488
  73.2 0.0 copy-done.1
  73.2 1.7 bitcast_select_fusion.g
  74.9 18.8 %backward_tick.1 = (bf16[4,128,1024]{2,1,0:T(8,128)(2,1)}, bf16[8,288,1024]{2,1,0:T(8,128)(2,1)}) custom-call(bf16[4,128,1024]{2,1,0:T(8,128)(2,1)} %bitcast.47, bf16[4,128,1024]{2,1,0:T(8,128)(2,1)} %bitcast_select_fusion.g, f32[1,1024]{1,0:T(1,128)} %gain.5, bf16[1024,1536]{1,0:T(8,128)(2,1)} %bitcast.50, bf16[512,1024]{1,0:T(8,128)(2,1)} %bitcast.53, ...), custom_call_target="tpu_custom_call" | custom-call | flops 4000000000 | bytes 18259968 | tf_op jit(solution)/shard_map/backward_tick/pallas_call | solution.py:341
  93.7 0.0 copy-start.2
  93.7 0.0 copy-start.3
  93.7 0.0 reduce-scatter.2.cloned.1.call-update
  93.7 1.2 copy-done.2
  94.9 0.3 copy-done.3
  95.2 0.2 maximum_bitcast_fusion
  95.4 2.9 %copy.17 = bf16[1,2,128,4,1024]{4,3,2,1,0:T(4,128)(2,1)} copy(bf16[1,2,128,4,1024]{4,2,3,1,0:T(8,128)(2,1)S(1)} %maximum_bitcast_fusion) | data formatting | bytes 4194304
  98.3 75.5 %reduce-scatter.2.cloned.1.call-done = bf16[1,288,1024]{2,1,0:T(8,128)(2,1)} async-done(((bf16[8,288,1024]{2,1,0:T(8,128)(2,1)}), bf16[1,288,1024]{2,1,0:T(8,128)(2,1)}) %reduce-scatter.2.cloned.1.call-update) | async-done | bytes 589840 | tf_op jit(solution)/shard_map/reduce_scatter | solution.py:492
  173.9 1.3 fusion.2
  175.2 0.5 slice.58
  175.8 0.6 maximum_bitcast_fusion.2
  176.5 0.9 maximum_bitcast_fusion.1
  177.4 1.6 slice.55
  (4 shorter events, 0.1 us)
Async XLA Ops:
  7.2 3.9 %copy-start = (bf16[1,2,128,4,1024]{4,3,2,1,0:T(4,128)(2,1)S(1)}, bf16[1,2,128,4,1024]{4,3,2,1,0:T(4,128)(2,1)}, u32[]{:S(2)}) copy-start(bf16[1,2,128,4,1024]{4,3,2,1,0:T(4,128)(2,1)} %param.8) | copy-start | bytes 6291460
  7.2 166.7 %reduce-scatter.2.cloned.1.call-start = ((), (), s32[]{:S(2)}) async-start(), calls=%async_computation.1 | async-start | bytes 5308416 | tf_op jit(solution)/shard_map/reduce_scatter | solution.py:492
  34.0 39.2 %collective-permute-start = (bf16[4,128,1024]{2,1,0:T(8,128)(2,1)}, bf16[4,128,1024]{2,1,0:T(8,128)(2,1)S(1)}, u32[]{:S(2)}, u32[]{:S(2)}) collective-permute-start(bf16[4,128,1024]{2,1,0:T(8,128)(2,1)} %get-tuple-element.27), channel_id=1, source_target_pairs={{8,0},{16,8},{24,16},{32,24},{40,32},{48,40},{56,48},{64,56},{72,6... | collective-permute-start | bytes 3145736 | tf_op jit(solution)/shard_map/ppermute | solution.py:488
  38.2 35.0 %copy-start.1 = (bf16[1,128,4,1024]{3,2,1,0:T(4,128)(2,1)S(1)}, bf16[1,128,4,1024]{3,2,1,0:T(4,128)(2,1)}, u32[]{:S(2)}) copy-start(bf16[1,128,4,1024]{3,2,1,0:T(4,128)(2,1)} %param.10) | copy-start | bytes 3145732
  93.7 1.2 copy-start.2
  93.7 1.5 copy-start.3
Sparse Core Ops, SparseCore 0:
  93.8 80.0 reduce-scatter.1
where the time goes:
time: 186 us
  waiting for transfers between devices  101 us (54%)
  Pallas kernels  49.2 us (26%)
  between operations  14.1 us (8%)
  local copies, waits for them, and re-layouts  13.8 us (7%)
  other arithmetic  4.77 us (3%)
  starting transfers between devices  2.86 us (2%)
    reduce_scatter x1, waiting for transfers between devices, shards(): mine = lax.psum_scatter(terms, 'dp', scatter_dimension=0, tiled=False)  75.5 us
    pallas_call x3, Pallas kernels, call(): pl.pallas_call(body, out_shape=outs, in_specs=[whole] * len(args), out_sp...  49.2 us
    ppermute x1, waiting for transfers between devices, shards(): lax.ppermute(dx0, 'section', [(i + 1, i) for i in range(layers - 1)])  25.6 us
    unnamed x12, local copies, waits for them, and re-layouts  9.54 us
  transfers between devices with their start and end apart: 2, of which 2 were waited for; matrix products, arithmetic and copies ran while one was open for 2% of the time, Pallas kernels for 5%

commit v1 on v0

--- a/solution.py
+++ b/solution.py
@@ -1,3 +1,5 @@
+import functools
+
 import jax
 import jax.numpy as jnp
 from jax import lax
@@ -16,11 +18,12 @@
 SINK = 20
 EPS = 1e-6
 ROWS = 16
-SHARD_ROWS = 288
-QKV_TAIL = 128
-OUT_AT = 192
-PROJ_AT = 256
-GAIN_AT = 272
+RUN = 4
+FORWARD_COST = 1
+FINISH_COST = 100
+RIGHT = 3 * INNER + D
+LEFT = D + INNER
+FRONT = 80
 NN = (((1,), (0,)), ((), ()))
 NT = (((1,), (1,)), ((), ()))
 TN = (((0,), (0,)), ((), ()))
@@ -172,20 +175,21 @@
     return block
 
 
-def backward(x, g, bhl, gain, w, wo, s, o, t):
-    eye = iota((T, T), 0) == iota((T, T), 1)
-
+def adjoint_rows(g, s, out):
     def att_rows(block, _):
         rows = pl.ds(pl.multiple_of(block * ROWS, ROWS), ROWS)
         c = s["coef"][rows, :]
         total = c[:, 4:5] * g[0, rows, :].astype(F32)
         for i in range(1, LANES):
             total = total + c[:, 4 + i : 5 + i] * g[i, rows, :].astype(F32)
-        o["datt"][rows, :] = total.astype(BF16)
+        out[rows, :] = total.astype(BF16)
         return 0
 
     lax.fori_loop(0, T // ROWS, att_rows, 0)
-    dctx = dot(o["datt"][...], wo[...], NT).astype(BF16)
+
+
+def attention_back(datt, wo, s, out):
+    dctx = dot(datt[...], wo[...], NT).astype(BF16)
     low, masks = half_masks()
     ones = head_ones()
 
@@ -195,25 +199,29 @@
         scale = s["scale"][:, lanes]
         dn = dn.astype(BF16).astype(F32)
         moment = head_mean(dn * wide, ones)
-        o["dproj"][:, lanes] = (scale * (dn - wide * (scale * scale * moment))).astype(BF16)
+        out[:, lanes] = (scale * (dn - wide * (scale * scale * moment))).astype(BF16)
 
     for pair in range(PAIRS):
         lanes = slice(pair * 128, pair * 128 + 128)
-        q = s["qk"][:, lanes]
-        k = s["qk"][:, pl.ds(INNER + pair * 128, 128)]
+        q = s["qk"][:, pl.ds(pair * 128, 128)]
+        key = s["qk"][:, pl.ds(INNER + pair * 128, 128)]
         v = s["proj"][:, pl.ds(2 * INNER + pair * 128, 128)]
         dc = dctx[:, lanes]
         dq, dk, dv = [], [], []
-        for half in range(2):
-            weights = s["weights"][2 * pair + half]
-            dw = dot(dc * masks[half], v, NT).astype(BF16).astype(F32)
+        for side in range(2):
+            weights = s["weights"][2 * pair + side]
+            dw = dot(dc * masks[side], v, NT).astype(BF16).astype(F32)
             dscore = weights * (dw - jnp.sum(dw * weights, axis=-1, keepdims=True)) * 0.125
-            dq.append(dot(dscore.astype(BF16), k))
+            dq.append(dot(dscore.astype(BF16), key))
             dk.append(dot(dscore.T.astype(BF16), q))
             dv.append(dot(weights.T.astype(BF16), dc))
-        o["dproj"][:, pl.ds(2 * INNER + pair * 128, 128)] = jnp.where(low, dv[0], dv[1]).astype(BF16)
+        out[:, pl.ds(2 * INNER + pair * 128, 128)] = jnp.where(low, dv[0], dv[1]).astype(BF16)
         norm_back(jnp.where(low, dq[0], dq[1]), pair)
         norm_back(jnp.where(low, dk[0], dk[1]), PAIRS + pair)
+
+
+def stream_back(x, g, bhl, gain, w, s, o, t, put):
+    eye = iota((T, T), 0) == iota((T, T), 1)
     t["dn"][...] = dot(o["dproj"][...], w[...], NT).astype(BF16)
 
     def joined_rows(block, total):
@@ -274,7 +282,7 @@
         o["dproj_map"][:, cols] = dot(rows_first, x[j])
         t["f"][j] = dot(lead, bhl[:, cols])
 
-    def stream_rows(block, _):
+    def stream_rows(put, block, _):
         rows = pl.ds(pl.multiple_of(block * ROWS, ROWS), ROWS)
         c = s["coef"][rows, :]
         kap = t["back"][rows, 64:65]
@@ -285,10 +293,11 @@
             for i in range(LANES):
                 at = 8 + LANES * i + j
                 total = total + c[:, at : at + 1] * gs[i]
-            o["dx"][j, rows, :] = total.astype(BF16)
+            put(block, j, total.astype(BF16))
         return 0
 
-    lax.fori_loop(0, T // ROWS, stream_rows, 0)
+    for first, last, place in put:
+        lax.fori_loop(first, last, functools.partial(stream_rows, place), 0)
 
 
 SAVED = (
@@ -297,166 +306,327 @@
     ("coef", (T, 128), F32),
     ("joined", (T, D), F32),
     ("r", (T, 128), F32),
-    ("normed", (T, D), BF16),
     ("proj", (T, 3 * INNER), BF16),
     ("scale", (T, 2 * INNER), F32),
     ("qk", (T, 2 * INNER), BF16),
     ("weights", (HEADS, T, T), F32),
-    ("ctx", (T, INNER), BF16),
     ("att", (T, D), BF16),
+    ("bhl", (64, LANES * D), BF16),
 )
-BACK = (
-    ("dx", (LANES, T, D), BF16),
-    ("dproj", (T, 3 * INNER), BF16),
-    ("datt", (T, D), BF16),
-    ("dproj_map", (32, LANES * D), F32),
-    ("dgain", (1, D), F32),
-)
+LEFT_OUT = (("left", (T, LEFT), BF16),)
+MAP = (("dproj_map", (32, LANES * D), F32), ("dgain", (1, D), F32))
 TEMPS = (
     ("dn", (T, D), BF16),
     ("dj", (T, D), F32),
     ("back", (T, 128), F32),
     ("f", (LANES, T, D), F32),
 )
-KEPT = ("normed", "ctx")
-BHL = (64, LANES * D)
+STREAMS = (("g", (LANES, T, D), BF16),)
+VMEM = pl.BlockSpec(memory_space=pltpu.VMEM)
+ANY = pl.BlockSpec(memory_space=pl.ANY)
+SMEM = pl.BlockSpec(memory_space=pltpu.SMEM)
+
+
+def struct(shape, dtype):
+    return jax.ShapeDtypeStruct(shape, dtype)
 
 
 def shapes(table):
-    return [jax.ShapeDtypeStruct(shape, dtype) for _, shape, dtype in table]
+    return [struct(shape, dtype) for _, shape, dtype in table]
 
 
 def scratch(table):
     return [pltpu.VMEM(shape, dtype) for _, shape, dtype in table]
 
 
+def names(table):
+    return [name for name, _, _ in table]
+
+
 def named(table, refs):
-    return {name: ref for (name, _, _), ref in zip(table, refs)}
-
-
-def call(body, outs, scratches, args, flops, name):
-    moved = sum(a.size * a.dtype.itemsize for a in args)
-    moved += sum(a.size * a.dtype.itemsize for a in outs)
-    whole = pl.BlockSpec(memory_space=pltpu.VMEM)
+    return dict(zip(names(table), refs))
+
+
+def call(body, outs, scratches, args, micros, name, specs=None):
     return pl.pallas_call(
         body,
         out_shape=outs,
-        in_specs=[whole] * len(args),
-        out_specs=[whole] * len(outs),
+        in_specs=specs or [VMEM] * len(args),
+        out_specs=[VMEM] * len(outs),
         scratch_shapes=scratches,
         compiler_params=pltpu.CompilerParams(vmem_limit_bytes=56 * 1024 * 1024),
-        cost_estimate=pl.CostEstimate(flops=flops, bytes_accessed=moved, transcendentals=0),
+        cost_estimate=pl.CostEstimate(
+            flops=micros * 1_000_000_000, bytes_accessed=micros * 2_000_000, transcendentals=0
+        ),
         name=name,
     )(*args)
 
 
-SAVED_IN = [e for e in SAVED if e[0] not in KEPT]
-SAVED_OUT = [e for e in SAVED if e[0] in KEPT]
+def factors(refs, right, left):
+    if right is not None:
+        refs["dproj"] = right.at[:, pl.ds(0, 3 * INNER)]
+        refs["datt"] = right.at[:, pl.ds(3 * INNER, D)]
+    if left is not None:
+        refs["normed"] = left.at[:, pl.ds(0, D)]
+        refs["ctx"] = left.at[:, pl.ds(D, INNER)]
+    return refs
 
 
 def whole_tick(x, g, seg, bt, gain, w, wo):
+    outs = [
+        ("dx_front", (LANES, FRONT, D), BF16),
+        ("dx_back", (LANES, T - FRONT, D), BF16),
+        ("factors", (T, RIGHT + LEFT), BF16),
+        *MAP,
+    ]
+
     def body(x, g, seg, bt, gain, w, wo, *rest):
-        outs = rest[: len(BACK) + len(KEPT)]
+        o = named(outs, rest)
+        right = o["factors"].at[:, pl.ds(0, RIGHT)]
+        s = factors({}, None, o["factors"].at[:, pl.ds(RIGHT, LEFT)])
+        factors(o, right, None)
         rest = rest[len(outs) :]
-        o = named(BACK, outs)
-        s = named(SAVED_OUT, outs[len(BACK) :])
-        s.update(named(SAVED_IN, rest))
-        rest = rest[len(SAVED_IN) :]
-        t = named(TEMPS, rest)
-        bhl = rest[len(TEMPS)]
-        stacked_map(bt, bhl)
-        forward(x, bhl, gain, w, wo, seg, s)
-        backward(x, g, bhl, gain, w, wo, s, o, t)
-
+        s.update(named(SAVED, rest))
+        t = named(TEMPS, rest[len(SAVED) :])
+        stacked_map(bt, s["bhl"])
+        forward(x, s["bhl"], gain, w, wo, seg, s)
+        adjoint_rows(g, s, o["datt"])
+        attention_back(o["datt"], wo, s, o["dproj"])
+
+        def put_front(block, j, value):
+            o["dx_front"][j, pl.ds(pl.multiple_of(block * ROWS, ROWS), ROWS), :] = value
+
+        def put_back(block, j, value):
+            at = pl.multiple_of(block * ROWS - FRONT, ROWS)
+            o["dx_back"][j, pl.ds(at, ROWS), :] = value
+
+        cut = FRONT // ROWS
+        put = ((0, cut, put_front), (cut, T // ROWS, put_back))
+        stream_back(x, g, s["bhl"], gain, w, s, o, t, put)
+
+    got = call(
+        body,
+        shapes(outs),
+        scratch(SAVED) + scratch(TEMPS),
+        (x, g, seg, bt, gain, w, wo),
+        20,
+        "whole_tick",
+    )
+    return named(outs, got)
+
+
+def forward_tick(x, seg, bt, gain, w, wo):
+    table = SAVED + LEFT_OUT
+
+    def body(x, seg, bt, gain, w, wo, *outs):
+        s = named(table, outs)
+        factors(s, None, s["left"])
+        stacked_map(bt, s["bhl"])
+        forward(x, s["bhl"], gain, w, wo, seg, s)
+
+    got = call(body, shapes(table), [], (x, seg, bt, gain, w, wo), FORWARD_COST, "forward_tick")
+    return named(table, got)
+
+
+ATTENTION = [e for e in SAVED if e[0] in ("coef", "proj", "scale", "qk", "weights")]
+
+
+def attention_tick(where, near, far, final, wo, saved, after):
+    def body(where, near0, near1, far0, far1, final, after, wo, *rest):
+        s = named(ATTENTION, rest)
+        g, right, sem = rest[len(ATTENTION) :]
+
+        def fetch(sources):
+            copies = [pltpu.make_async_copy(a, b, sem.at[k]) for k, (a, b) in enumerate(sources)]
+            for copy in copies:
+                copy.start()
+            for copy in copies:
+                copy.wait()
+
+        head = g.at[:, pl.ds(0, FRONT), :]
+        tail = g.at[:, pl.ds(FRONT, T - FRONT), :]
+
+        @pl.when(where[0] == 0)
+        def _():
+            fetch([(near0, head), (near1, tail)])
+
+        @pl.when(where[0] == 1)
+        def _():
+            fetch([(far0, head), (far1, tail)])
+
+        @pl.when(where[0] == 2)
+        def _():
+            fetch([(final, g)])
+
+        o = factors({}, right, None)
+        adjoint_rows(g, s, o["datt"])
+        attention_back(o["datt"], wo, s, o["dproj"])
+
+    args = (where, *near, *far, final, after, wo, *[saved[k] for k in names(ATTENTION)])
     return call(
         body,
-        shapes(BACK) + shapes(SAVED_OUT),
-        scratch(SAVED_IN) + scratch(TEMPS) + [pltpu.VMEM(BHL, BF16)],
-        (x, g, seg, bt, gain, w, wo),
-        4_000_000_000,
-        "whole_tick",
-    )
-
-
-def forward_tick(x, seg, bt, gain, w, wo):
-    def body(x, seg, bt, gain, w, wo, *outs):
-        bhl = outs[len(SAVED)]
-        stacked_map(bt, bhl)
-        forward(x, bhl, gain, w, wo, seg, named(SAVED, outs))
-
-    saved = call(
-        body,
-        shapes(SAVED) + [jax.ShapeDtypeStruct(BHL, BF16)],
-        [],
-        (x, seg, bt, gain, w, wo),
-        1_000_000_000,
-        "forward_tick",
-    )
-    return saved
-
-
-def fill_shards(first, second, out, n):
-    rows = D // n
-    normed = jnp.concatenate([first["normed"][...], second["normed"][...]], axis=0)
-    for at in range(6):
-        cols = slice(at * 256, at * 256 + 256)
-        right = jnp.concatenate([first["dproj"][:, cols], second["dproj"][:, cols]], axis=0)
-        product = dot(normed, right, TN).astype(BF16)
+        shapes(STREAMS) + [struct((T, RIGHT), BF16)],
+        [pltpu.SemaphoreType.DMA((2,))],
+        args,
+        5,
+        "attention_tick",
+        [SMEM] + [ANY] * 6 + [VMEM] * (1 + len(ATTENTION)),
+    )
+
+
+REST = [e for e in SAVED if e[0] in ("mc", "sink", "coef", "joined", "r", "att", "bhl")]
+
+
+def stream_tick(x, g, gain, w, right, saved, earlier, n, after):
+    def body(after, x, g, gain, w, right, *rest):
+        s = named(REST, rest)
+        rest = rest[len(REST) :]
+        first = named(MAP, rest)
+        dx, parts, *rest = rest[len(MAP) :]
+        o = named(MAP, rest)
+        factors(o, right, None)
+        t = named(TEMPS, rest[len(MAP) :])
+
+        def put_rows(block, j, value):
+            dx[j, pl.ds(pl.multiple_of(block * ROWS, ROWS), ROWS), :] = value
+
+        put = ((0, T // ROWS, put_rows),)
+        stream_back(x, g, s["bhl"], gain, w, s, o, t, put)
+        width = LANES * D // n
         for d in range(n):
-            part = product[d * rows : (d + 1) * rows]
-            if at < 4:
-                out[d, 0:rows, cols] = part
-            else:
-                left = (at - 4) * 256
-                half = rows // 2
-                out[d, QKV_TAIL : QKV_TAIL + half, left : left + 256] = part[0:half]
-                out[d, QKV_TAIL : QKV_TAIL + half, 512 + left : 768 + left] = part[half:]
-    ctx = jnp.concatenate([first["ctx"][...], second["ctx"][...]], axis=0)
-    rows = INNER // n
-    for at in range(4):
-        cols = slice(at * 256, at * 256 + 256)
-        right = jnp.concatenate([first["datt"][:, cols], second["datt"][:, cols]], axis=0)
-        product = dot(ctx, right, TN).astype(BF16)
-        for d in range(n):
-            out[d, OUT_AT : OUT_AT + rows, cols] = product[d * rows : (d + 1) * rows]
-    for d in range(n):
-        cols = slice(d * 512, d * 512 + 512)
-        proj = first["dproj_map"][:, cols] + second["dproj_map"][:, cols]
-        out[d, PROJ_AT : PROJ_AT + 16, 0:512] = proj[0:16].astype(BF16)
-        out[d, PROJ_AT : PROJ_AT + 16, 512:1024] = proj[16:32].astype(BF16)
-        gain = first["dgain"][:, d * 128 : d * 128 + 128] + second["dgain"][:, d * 128 : d * 128 + 128]
-        out[d, GAIN_AT : GAIN_AT + 16, 0:128] = jnp.broadcast_to(gain, (16, 128)).astype(BF16)
-        out[d, GAIN_AT : GAIN_AT + 16, 128:1024] = jnp.zeros((16, 896), BF16)
-
-
-EARLIER = ("dproj", "datt", "dproj_map", "dgain", "normed", "ctx")
-
-
-def backward_tick(x, g, gain, w, wo, saved, earlier, n):
-    def body(x, g, gain, w, wo, *rest):
-        s = named(SAVED, rest)
-        bhl = rest[len(SAVED)]
-        rest = rest[len(SAVED) + 1 :]
-        first = dict(zip(EARLIER, rest))
-        rest = rest[len(EARLIER) :]
-        o = {"dx": rest[0]}
-        out = rest[1]
-        rest = rest[2:]
-        o.update(named(BACK[1:], rest))
-        t = named(TEMPS, rest[len(BACK) - 1 :])
-        backward(x, g, bhl, gain, w, wo, s, o, t)
-        second = dict(o)
-        second["normed"] = s["normed"]
-        second["ctx"] = s["ctx"]
-        fill_shards(first, second, out, n)
+            cols = slice(d * width, d * width + width)
+            proj = first["dproj_map"][:, cols] + o["dproj_map"][:, cols]
+            lanes = slice(d * (D // n), (d + 1) * (D // n))
+            total = first["dgain"][:, lanes] + o["dgain"][:, lanes]
+            total = jnp.concatenate([total, jnp.zeros((1, width - D // n), F32)], axis=1)
+            total = jnp.broadcast_to(total, (8, width))
+            parts[d] = jnp.concatenate([proj[0:24], total], axis=0).astype(BF16)
 
     return call(
         body,
-        shapes(BACK[:1]) + [jax.ShapeDtypeStruct((n, SHARD_ROWS, D), BF16)],
-        scratch(BACK[1:]) + scratch(TEMPS),
-        (x, g, gain, w, wo, *saved, *[earlier[k] for k in EARLIER]),
-        4_000_000_000,
-        "backward_tick",
+        [struct((LANES, T, D), BF16), struct((n, 32, LANES * D // n), BF16)],
+        scratch(MAP) + scratch(TEMPS),
+        (
+            after,
+            x,
+            g,
+            gain,
+            w,
+            right,
+            *[saved[k] for k in names(REST)],
+            *[earlier[k] for k in names(MAP)],
+        ),
+        9,
+        "stream_tick",
+        [ANY] + [VMEM] * (5 + len(REST) + len(MAP)),
+    )
+
+
+STEPS = 4
+
+
+def turned_factors(place, first, second):
+    rows, few = D // (2 * STEPS), INNER // (2 * STEPS)
+
+    def body(place, *refs):
+        refs, (left, small) = refs[:STEPS], refs[STEPS:]
+        sides = [refs[k].at[:, pl.ds(RIGHT if k % 2 == 0 else 0, LEFT)] for k in range(STEPS)]
+        sides = [factors({}, None, side) for side in sides]
+        even = place[STEPS] == 0
+        for step in range(STEPS):
+            chip = place[step]
+            at = pl.multiple_of((2 * chip + place[STEPS]) * rows, rows)
+            near = pl.multiple_of(chip * rows, rows)
+            for k, side in enumerate(sides):
+                tokens = slice(k * T, k * T + T)
+                block = side["normed"][:, pl.ds(at, rows)].astype(F32).T
+                left[step * rows : (step + 1) * rows, tokens] = block.astype(BF16)
+                block = side["ctx"][:, pl.ds(near, rows)].astype(F32).T
+                block = jnp.where(even, block[0:few], block[few:rows])
+                small[step * few : (step + 1) * few, tokens] = block.astype(BF16)
+
+    return call(
+        body,
+        [struct((STEPS * rows, STEPS * T), BF16), struct((STEPS * few, STEPS * T), BF16)],
+        [],
+        (place, first[0], second[0], first[1], second[1]),
+        FORWARD_COST,
+        "turned_factors",
+        [SMEM] + [VMEM] * STEPS,
+    )
+
+
+PACKED = 3 * INNER + D // 2
+
+
+def terms(left, small, rights):
+    rows, few = D // (2 * STEPS), INNER // (2 * STEPS)
+
+    def body(left, small, *refs):
+        rights, outs = refs[:STEPS], refs[STEPS:]
+
+        def right(at):
+            return jnp.concatenate([r[:, at : at + 256] for r in rights], axis=0)
+
+        for at in range(0, 3 * INNER, 256):
+            product = dot(left[...], right(at))
+            for step in range(STEPS):
+                part = product[step * rows : (step + 1) * rows]
+                outs[step][:, at : at + 256] = part.astype(outs[step].dtype)
+        for at in range(0, D, 256):
+            product = dot(small[...], right(3 * INNER + at))
+            top = few * (at // (D // 2))
+            cols = 3 * INNER + at % (D // 2)
+            for step in range(STEPS):
+                part = product[step * few : (step + 1) * few]
+                outs[step][top : top + few, cols : cols + 256] = part.astype(outs[step].dtype)
+
+    own, *sends = call(
+        body,
+        [struct((rows, PACKED), F32)] + [struct((rows, PACKED), BF16)] * (STEPS - 1),
+        [],
+        (left, small, *rights),
+        4,
+        "terms",
+    )
+    return own, sends
+
+
+def finish_terms(terms):
+    few = INNER // (2 * STEPS)
+
+    def body(*refs):
+        *others, grad_qkv, grad_out = refs[1:]
+        total = refs[0][...]
+        for other in others:
+            total = total + other[...].astype(F32)
+        grad_qkv[...] = total[:, : 3 * INNER]
+        grad_out[:, : D // 2] = total[:few, 3 * INNER :]
+        grad_out[:, D // 2 :] = total[few:, 3 * INNER :]
+
+    rows = terms[0].shape[0]
+    outs = [struct((rows, 3 * INNER), F32), struct((few, D), F32)]
+    return call(body, outs, [], terms, FINISH_COST, "finish_terms")
+
+
+def finish_map(parts, n, after):
+    width = LANES * D // n
+
+    def body(parts, after, grad_map, grad_gain):
+        total = parts[0].astype(F32)
+        for d in range(1, n):
+            total = total + parts[d].astype(F32)
+        grad_map[...] = total[0:24]
+        grad_gain[...] = total[24:25, 0 : D // n]
+
+    return call(
+        body,
+        [struct((24, width), F32), struct((1, D // n), F32)],
+        [],
+        (parts, after),
+        1,
+        "finish_map",
+        [VMEM, ANY],
     )
 
 
@@ -472,7 +642,9 @@
 ):
     n = lax.axis_size("dp")
     layers = lax.axis_size("section")
-    last = lax.axis_index("section") == layers - 1
+    section = lax.axis_index("section")
+    replica = lax.axis_index("dp")
+    chip, core = replica // 2, replica % 2
     lanes_first = lambda a: jnp.transpose(a, (1, 0, 2))
     x0 = lanes_first(saved_entering_lanes[0, 0])
     x1 = lanes_first(saved_entering_lanes[0, 1])
@@ -482,32 +654,48 @@
     gain = rescale_amplitude
     w = attend_entry_maps[0]
     wo = attend_exit_map[0]
-    outs = whole_tick(x0, opening, document_labels[0, 0:1], bt, gain, w, wo)
-    earlier = dict(zip([e[0] for e in BACK] + [e[0] for e in SAVED_OUT], outs))
-    dx0 = earlier["dx"]
-    received = lax.ppermute(dx0, "section", [(i + 1, i) for i in range(layers - 1)])
+
+    def swap_cores(value):
+        return lax.ppermute(value, "dp", [(i, i ^ 1) for i in range(n)])
+
+    def along(value, *chips):
+        route = [(2 * a + c, 2 * b + c) for a, b in chips for c in range(2)]
+        return lax.ppermute(value, "dp", route)
+
+    first = whole_tick(x0, opening, document_labels[0, 0:1], bt, gain, w, wo)
+
+    near = [(s, s - 1) for s in range(1, layers) if s % RUN]
+    cross = range(RUN, layers, RUN)
+    hop = lax.ppermute(first["dx_back"], "section", near + [(s, s + RUN - 1) for s in cross])
+    front_far = lax.ppermute(first["dx_front"], "section", [(s, s - 1) for s in cross])
+    other = swap_cores(first["factors"])
     saved = forward_tick(x1, document_labels[0, 1:2], bt, gain, w, wo)
-    later = jnp.where(last, final, received)
-    dx1, terms = backward_tick(x1, later, gain, w, wo, saved, earlier, n)
-    mine = lax.psum_scatter(terms, "dp", scatter_dimension=0, tiled=False)
+    coming, later, _ = lax.optimization_barrier((hop, first["dx_front"], saved["coef"]))
+    far = lax.ppermute(coming, "section", [(s + RUN - 1, s - 1) for s in cross])
+    front_near = lax.ppermute(later, "section", near)
+    place = jnp.stack([chip ^ step for step in range(STEPS)] + [core])
+    left, small = turned_factors(
+        place, (first["factors"], other), (saved["left"], swap_cores(saved["left"]))
+    )
+    where = jnp.where(section == layers - 1, 2, jnp.where(section % RUN == RUN - 1, 1, 0))
+    g, right = attention_tick(
+        where[None], (front_near, hop), (front_far, far), final, wo, saved, left
+    )
+    own, sends = terms(left, small, [first["factors"], right, other, swap_cores(right)])
+    by_way = along(sends[2], (0, 1), (3, 2))
+    middle = along(sends[2], (1, 2), (2, 1))
+    beside = along(sends[0], (0, 1), (1, 0), (2, 3), (3, 2))
+    outer = along(sends[1], (0, 2), (3, 1))
+    dx1, parts = stream_tick(x1, g, gain, w, right, saved, first, n, own)
+    by_way, dx1, parts = lax.optimization_barrier((by_way, dx1, parts))
+    both = (sends[1].astype(F32) + by_way.astype(F32)).astype(BF16)
+    grads = [own, middle, beside, outer, along(both, (1, 3), (2, 0))]
+    parts = lax.all_to_all(parts, "dp", 0, 0)
+    grad_qkv, grad_out = finish_terms(grads)
+    grad_map, grad_gain = finish_map(parts, n, grad_qkv)
+    dx0 = jnp.concatenate([first["dx_front"], first["dx_back"]], axis=1)
     sent = jnp.stack([jnp.transpose(dx0, (1, 0, 2)), jnp.transpose(dx1, (1, 0, 2))])[None]
-    mine = mine.astype(F32)
-    rows = D // n
-    half = rows // 2
-    tail = mine[QKV_TAIL : QKV_TAIL + half]
-    tail = jnp.concatenate([tail[:, :512], tail[:, 512:]], axis=0)
-    grad_qkv = jnp.concatenate([mine[:rows], tail], axis=1)
-    grad_out = mine[OUT_AT : OUT_AT + INNER // n]
-    proj = jnp.concatenate(
-        [mine[PROJ_AT : PROJ_AT + 16, :512], mine[PROJ_AT : PROJ_AT + 8, 512:]], axis=0
-    )
-    return (
-        sent,
-        grad_qkv[None],
-        grad_out[None],
-        proj.T[None],
-        mine[GAIN_AT : GAIN_AT + 1, :rows],
-    )
+    return (sent, grad_qkv[None], grad_out[None], grad_map.T[None], grad_gain)
 
 
 def solution(mesh):

time: 186 us -> 151 us (0.81)
  waiting for transfers between devices: 101 us -> 41.7 us
  starting transfers between devices: 2.86 us -> 28.8 us
  Pallas kernels: 49.2 us -> 62.7 us
  between operations: 14.1 us -> 0.86 us
  other arithmetic: 4.77 us -> 0.39 us
    reduce_scatter x1 -> x0, waiting for transfers between devices: 75.5 us -> none  [shards(): mine = lax.psum_scatter(terms, 'dp', scatter_dimension=0, tiled=False)]
    ppermute x1 -> x12, starting transfers between devices: 2.82 us -> 24 us  [the longest x5 9.45 us: along(): return lax.ppermute(value, 'dp', route)]
    ppermute x1 -> x12, waiting for transfers between devices: 25.6 us -> 41.7 us  [the longest x5 22.2 us: along(): return lax.ppermute(value, 'dp', route)]
    pallas_call x3 -> x8, Pallas kernels: 49.2 us -> 62.7 us  [call(): pl.pallas_call(body, out_shape=outs, in_specs=specs or [VMEM] * len(args)...]
    all_to_all x0 -> x1, starting transfers between devices: none -> 4.85 us  [shards(): parts = lax.all_to_all(parts, 'dp', 0, 0)]
    unnamed x12 -> x31, local copies, waits for them, and re-layouts: 9.54 us -> 12.7 us
    slice x7 -> x1, local copies, waits for them, and re-layouts: 2.93 us -> 0.72 us  [shards(): x1 = lanes_first(saved_entering_lanes[0, 1])]
  transfers between devices with their start and end apart: 2 -> 13, of which waited for: 2 -> 5; matrix products, arithmetic and copies ran while one was open for 2% -> 4% of each run, Pallas kernels for 5% -> 18%
where the time goes in v1:
time: 151 us; the launch traced here: 150 us
  Pallas kernels  62.7 us (42%)
  waiting for transfers between devices  41.7 us (28%)
  starting transfers between devices  28.8 us (19%)
  local copies, waits for them, and re-layouts  15.5 us (10%)
    pallas_call x8, Pallas kernels, call(): pl.pallas_call(body, out_shape=outs, in_specs=specs or [VMEM] * len(args)...  62.7 us
    ppermute x5, waiting for transfers between devices, along(): return lax.ppermute(value, 'dp', route)  22.2 us
    unnamed x31, local copies, waits for them, and re-layouts  12.7 us
    ppermute x1, waiting for transfers between devices, shards(): far = lax.ppermute(coming, 'section', [(s + RUN - 1, s - 1) for s in cross])  11.7 us
    ppermute x5, starting transfers between devices, along(): return lax.ppermute(value, 'dp', route)  9.45 us
    ppermute x1, starting transfers between devices, shards(): far = lax.ppermute(coming, 'section', [(s + RUN - 1, s - 1) for s in cross])  8.39 us
    ppermute x1, waiting for transfers between devices, shards(): lax.ppermute(first['dx_back'], 'section', near + [(s, s + RUN - 1) for s...  5.48 us
    all_to_all x1, starting transfers between devices, shards(): parts = lax.all_to_all(parts, 'dp', 0, 0)  4.85 us
  transfers between devices with their start and end apart: 13, of which 5 were waited for; matrix products, arithmetic and copies ran while one was open for 4% of the time, Pallas kernels for 18%

profile of v1, /device:TPU:30, one launch (start us, length us, event | category | flops | bytes accessed | tf_op | source)
XLA Modules:
  0.0 149.9 jit_solution(7996451783515871745)
XLA Ops:
  0.6 0.0 copy-start
  0.6 1.4 slice_bitcast_fusion
  2.0 2.5 %copy.27 = bf16[1,128,4,1024]{3,1,2,0:T(8,128)(2,1)} copy(bf16[1,128,4,1024]{3,2,1,0:T(4,128)(2,1)} %param.9) | data formatting | bytes 2097152 | tf_op args[1]
  4.5 0.0 copy-done
  4.5 0.7 fusion
  5.2 1.3 copy.25
  6.5 20.9 %whole_tick.1 = (bf16[4,80,1024]{2,1,0:T(8,128)(2,1)}, bf16[4,48,1024]{2,1,0:T(8,128)(2,1)}, bf16[128,4096]{1,0:T(8,128)(2,1)}, f32[32,4096]{1,0:T(8,128)}, f32[1,1024]{1,0:T(1,128)}) custom-call(bf16[4,128,1024]{2,1,0:T(8,128)(2,1)} %bitcast.59, bf16[4,128,1024]{2,1,0:T(8,128)(2,1)} %bitcast.58, s32[1,128]{1,0:T(1,128)} %get-tuple-element.85.seg, ...), custom_call_target="tpu_custom_call" | custom-call | flops 20000000000 | bytes 40000000 | tf_op jit(solution)/shard_map/whole_tick/pallas_call | solution.py:351
  27.5 0.0 collective-permute-start
  27.5 2.6 %collective-permute-start.2 = (bf16[4,48,1024]{2,1,0:T(8,128)(2,1)}, bf16[4,48,1024]{2,1,0:T(8,128)(2,1)}, u32[]{:S(2)}, u32[]{:S(2)}) collective-permute-start(bf16[4,48,1024]{2,1,0:T(8,128)(2,1)} %get-tuple-element.42), channel_id=1, source_target_pairs={{8,0},{16,8},{24,16},{40,32},{48,40},{56,48},{72,64},{80,72},{88,8... | collective-permute-start | bytes 1179656 | tf_op jit(solution)/shard_map/ppermute | solution.py:669
  30.1 1.3 collective-permute-start.4
  31.4 1.3 copy.24
  32.7 0.0 copy-start.3
  32.7 0.0 copy-start.1
  32.7 9.6 %forward_tick.1 = (f32[32,128]{1,0:T(8,128)}, f32[20,13,8,128]{3,2,1,0:T(8,128)}, f32[128,128]{1,0:T(8,128)}, f32[128,1024]{1,0:T(8,128)}, f32[128,128]{1,0:T(8,...) custom-call(bf16[4,128,1024]{2,1,0:T(8,128)(2,1)} %bitcast.49, ...), custom_call_target="tpu_custom_call" | custom-call | flops 1000000000 | bytes 2000000 | tf_op jit(solution)/shard_map/forward_tick/pallas_call | solution.py:351
  42.3 5.5 %collective-permute-done.2.near1 = bf16[4,48,1024]{2,1,0:T(8,128)(2,1)} collective-permute-done((bf16[4,48,1024]{2,1,0:T(8,128)(2,1)}, bf16[4,48,1024]{2,1,0:T(8,128)(2,1)}, u32[]{:S(2)}, u32[]{:S(2)}) %collective-permute-start.2) | collective-permute-done | bytes 393248 | tf_op jit(solution)/shard_map/ppermute | solution.py:669
  47.8 0.0 copy-done.3
  47.8 2.1 %collective-permute-start.3 = (bf16[4,80,1024]{2,1,0:T(8,128)(2,1)S(1)}, bf16[4,80,1024]{2,1,0:T(8,128)(2,1)}, u32[]{:S(2)}, u32[]{:S(2)}) collective-permute-start(bf16[4,80,1024]{2,1,0:T(8,128)(2,1)S(1)} %copy-done.3), channel_id=1, source_target_pairs={{8,0},{16,8},{24,16},{40,32},{48,40},{56,48},{72,64},{80,72},{88,8... | collective-permute-start | bytes 1966088 | tf_op jit(solution)/shard_map/ppermute | solution.py:675
  49.9 0.0 collective-permute-start.1
  49.9 8.4 %collective-permute-start.5 = (bf16[4,48,1024]{2,1,0:T(8,128)(2,1)}, bf16[4,48,1024]{2,1,0:T(8,128)(2,1)}, u32[]{:S(2)}, u32[]{:S(2)}) collective-permute-start(bf16[4,48,1024]{2,1,0:T(8,128)(2,1)} %collective-permute-done.2.near1), channel_id=1, source_target_pairs={{56,24},{88,56},{120,88},{152,120},{184,152},{216,184},{248,216},{... | collective-permute-start | bytes 1179656 | tf_op jit(solution)/shard_map/ppermute | solution.py:674
  58.3 0.0 copy-done.1
  58.3 1.3 copy.26
  59.6 0.7 stack.33.place
  60.3 0.0 collective-permute-done.1.refs_3_
  60.3 0.0 collective-permute-done.refs_2_
  60.3 0.0 copy-start.7
  60.3 1.0 copy-done.7
  61.3 3.0 %turned_factors.1 = (bf16[512,512]{1,0:T(8,128)(2,1)}, bf16[256,512]{1,0:T(8,128)(2,1)}) custom-call(s32[5]{0:T(128)} %stack.33.place, bf16[128,4096]{1,0:T(8,128)(2,1)} %get-tuple-element.43.refs_0_, bf16[128,1536]{1,0:T(8,128)(2,1)} %get-tuple-element.44.refs_1_, bf16[128,4096]{1,0:T(8,128)(2,1)} %copy-done.7, bf16[128,1536]{1,0:T(8,128)(2,1)} %collective-permute-done.1.refs_3_), custom_call_target="tpu_custom_call" | custom-call | flops 1000000000 | bytes 2000000 | tf_op jit(solution)/shard_map/turned_factors/pallas_call | solution.py:351
  64.3 0.0 collective-permute-done.4.far0
  64.4 11.7 %collective-permute-done.5.far1 = bf16[4,48,1024]{2,1,0:T(8,128)(2,1)} collective-permute-done((bf16[4,48,1024]{2,1,0:T(8,128)(2,1)}, bf16[4,48,1024]{2,1,0:T(8,128)(2,1)}, u32[]{:S(2)}, u32[]{:S(2)}) %collective-permute-start.5) | collective-permute-done | bytes 393248 | tf_op jit(solution)/shard_map/ppermute | solution.py:674
  76.0 0.0 collective-permute-done.3.near0
  76.0 0.0 copy-done.8
  76.0 8.2 %attention_tick.1 = (bf16[4,128,1024]{2,1,0:T(8,128)(2,1)}, bf16[128,2560]{1,0:T(8,128)(2,1)}) custom-call(s32[1]{0:T(128)} %bitcast.20.where, bf16[4,80,1024]{2,1,0:T(8,128)(2,1)} %collective-permute-done.3.near0, bf16[4,48,1024]{2,1,0:T(8,128)(2,1)} %collective-permute-done.2.near1, bf16[4,80,1024]{2,1,0:T(8,128)(2,1)} %copy-done.8, ...), custom_call_target="tpu_custom_call" | custom-call | flops 5000000000 | bytes 10000000 | tf_op jit(solution)/shard_map/attention_tick/pallas_call | solution.py:351
  84.2 0.1 collective-permute-start.6
  84.3 2.3 %collective-permute-done.6.refs_3_ = bf16[128,2560]{1,0:T(8,128)(2,1)S(1)} collective-permute-done((bf16[128,2560]{1,0:T(8,128)(2,1)}, bf16[128,2560]{1,0:T(8,128)(2,1)S(1)}, u32[]{:S(2)}, u32[]{:S(2)}) %collective-permute-start.6) | collective-permute-done | bytes 655392 | tf_op jit(solution)/shard_map/ppermute | solution.py:659
  86.6 0.8 copy-done.9
  87.5 5.0 %terms.1 = (f32[128,2048]{1,0:T(8,128)}, bf16[128,2048]{1,0:T(8,128)(2,1)}, bf16[128,2048]{1,0:T(8,128)(2,1)}, bf16[128,2048]{1,0:T(8,128)(2,1)}) custom-call(bf16[512,512]{1,0:T(8,128)(2,1)} %get-tuple-element.45.after.left, bf16[256,512]{1,0:T(8,128)(2,1)} %get-tuple-element.46.small, bf16[128,4096]{1,0:T(8,128)(2,1)} %get-tuple-element.43.refs_0_, ...), custom_call_target="tpu_custom_call" | custom-call | flops 4000000000 | bytes 8000000 | tf_op jit(solution)/shard_map/terms/pallas_call | solution.py:351
  92.4 0.7 collective-permute-start.8
  93.1 1.3 collective-permute-start.7
  94.4 0.1 collective-permute-start.9
  94.5 5.9 %collective-permute-start.10 = (bf16[128,2048]{1,0:T(8,128)(2,1)}, bf16[128,2048]{1,0:T(8,128)(2,1)}, u32[]{:S(2)}, u32[]{:S(2)}) collective-permute-start(bf16[128,2048]{1,0:T(8,128)(2,1)} %get-tuple-element.70), channel_id=1, source_target_pairs={{0,4},{1,5},{6,2},{7,3},{8,12},{9,13},{14,10},{15,11},{16,20},{17,... | collective-permute-start | bytes 1572872 | tf_op jit(solution)/shard_map/ppermute | solution.py:663
  100.5 11.4 %stream_tick.1 = (bf16[4,128,1024]{2,1,0:T(8,128)(2,1)}, bf16[8,32,512]{2,1,0:T(8,128)(2,1)}) custom-call(f32[128,2048]{1,0:T(8,128)} %get-tuple-element.56.after.refs_0_, bf16[4,128,1024]{2,1,0:T(8,128)(2,1)} %bitcast.50, bf16[4,128,1024]{2,1,0:T(8,128)(2,1)} %get-tuple-element.57.g, f32[1,1024]{1,0:T(1,128)} %gain.5, bf16[1024,1536]{1,0:T(8,128)(2,1)} %bitcast.53, ...), custom_call_target="tpu_custom_call" | custom-call | flops 8999999488 | bytes 18000000 | tf_op jit(solution)/shard_map/stream_tick/pallas_call | solution.py:351
  111.9 0.0 collective-permute-done.7
  111.9 0.0 copy-done.4
  111.9 0.1 add_convert_fusion
  112.0 1.4 collective-permute-start.11
  113.5 0.0 copy-done.5
  113.5 0.1 maximum_bitcast_fusion.1
  113.6 0.0 copy-done.2
  113.6 0.2 maximum_bitcast_fusion
  113.8 2.9 %copy.17 = bf16[1,2,128,4,1024]{4,3,2,1,0:T(4,128)(2,1)} copy(bf16[1,2,128,4,1024]{4,2,3,1,0:T(8,128)(2,1)S(1)} %maximum_bitcast_fusion) | data formatting | bytes 4194304
  116.7 4.8 %all-to-all-start = ((bf16[8,32,512]{2,1,0:T(8,128)(2,1)}), bf16[8,32,512]{2,1,0:T(8,128)(2,1)S(1)}, u32[]{:S(2)}, u32[]{:S(2)}) async-start(bf16[8,32,512]{2,1,0:T(8,128)(2,1)} %get-tuple-element.74), calls=%async_computation | async-start | bytes 524288 | tf_op jit(solution)/shard_map/all_to_all | solution.py:693
  121.6 0.0 collective-permute-done.9.refs_2_
  121.6 0.0 copy-start.11
  121.6 0.0 collective-permute-done.8.refs_1_
  121.6 0.0 copy-start.10
  121.6 7.9 %collective-permute-done.10.refs_3_ = bf16[128,2048]{1,0:T(8,128)(2,1)} collective-permute-done((bf16[128,2048]{1,0:T(8,128)(2,1)}, bf16[128,2048]{1,0:T(8,128)(2,1)}, u32[]{:S(2)}, u32[]{:S(2)}) %collective-permute-start.10) | collective-permute-done | bytes 524320 | tf_op jit(solution)/shard_map/ppermute | solution.py:663
  129.5 14.4 %collective-permute-done.11.refs_4_ = bf16[128,2048]{1,0:T(8,128)(2,1)S(1)} collective-permute-done((bf16[128,2048]{1,0:T(8,128)(2,1)S(1)}, bf16[128,2048]{1,0:T(8,128)(2,1)S(1)}, u32[]{:S(2)}, u32[]{:S(2)}) %collective-permute-start.11) | collective-permute-done | bytes 524320 | tf_op jit(solution)/shard_map/ppermute | solution.py:663
  143.8 0.0 copy-done.11
  143.8 0.0 copy-done.10
  143.8 0.8 copy-done.12
  144.6 3.0 %finish_terms.1 = (f32[128,1536]{1,0:T(8,128)}, f32[64,1024]{1,0:T(8,128)}) custom-call(f32[128,2048]{1,0:T(8,128)} %get-tuple-element.56.after.refs_0_, bf16[128,2048]{1,0:T(8,128)(2,1)} %copy-done.10, bf16[128,2048]{1,0:T(8,128)(2,1)} %copy-done.11, bf16[128,2048]{1,0:T(8,128)(2,1)} %collective-permute-done.10.refs_3_, bf16[128,2048]{1,0:T(8,128)(2,1)} %copy-done.12), custom_call_target="tpu_custom_call" | custom-call | flops 99999997952 | bytes 200000000 | tf_op jit(solution)/shard_map/finish_terms/pallas_call | solution.py:351
  147.6 0.0 all-to-all-done.parts
  147.6 0.7 copy-done.6
  148.3 1.6 %finish_map.1 = (f32[24,512]{1,0:T(8,128)}, f32[1,128]{1,0:T(1,128)}) custom-call(bf16[8,32,512]{2,1,0:T(8,128)(2,1)} %copy-done.6, f32[128,1536]{1,0:T(8,128)} %get-tuple-element.72.after), custom_call_target="tpu_custom_call" | custom-call | flops 1000000000 | bytes 2000000 | tf_op jit(solution)/shard_map/finish_map/pallas_call | solution.py:351
  (7 shorter events, 0.0 us)
Async XLA Ops:
  0.6 3.9 %copy-start = (bf16[1,2,128,4,1024]{4,3,2,1,0:T(4,128)(2,1)S(1)}, bf16[1,2,128,4,1024]{4,3,2,1,0:T(4,128)(2,1)}, u32[]{:S(2)}) copy-start(bf16[1,2,128,4,1024]{4,3,2,1,0:T(4,128)(2,1)} %param.8) | copy-start | bytes 6291460
  27.5 32.8 %collective-permute-start = (bf16[128,4096]{1,0:T(8,128)(2,1)}, bf16[128,4096]{1,0:T(8,128)(2,1)S(1)}, u32[]{:S(2)}, u32[]{:S(2)}) collective-permute-start(bf16[128,4096]{1,0:T(8,128)(2,1)} %get-tuple-element.43.refs_0_), channel_id=1, source_target_pairs={{0,1},{1,0},{2,3},{3,2},{4,5},{5,4},{6,7},{7,6},{8,9},{9,8},{10,11... | collective-permute-start | bytes 3145736 | tf_op jit(solution)/shard_map/ppermute | solution.py:659
  27.5 20.3 %collective-permute-start.2 = (bf16[4,48,1024]{2,1,0:T(8,128)(2,1)}, bf16[4,48,1024]{2,1,0:T(8,128)(2,1)}, u32[]{:S(2)}, u32[]{:S(2)}) collective-permute-start(bf16[4,48,1024]{2,1,0:T(8,128)(2,1)} %get-tuple-element.42), channel_id=1, source_target_pairs={{8,0},{16,8},{24,16},{40,32},{48,40},{56,48},{72,64},{80,72},{88,8... | collective-permute-start | bytes 1179656 | tf_op jit(solution)/shard_map/ppermute | solution.py:669
  30.1 34.2 %collective-permute-start.4 = (bf16[4,80,1024]{2,1,0:T(8,128)(2,1)}, bf16[4,80,1024]{2,1,0:T(8,128)(2,1)S(1)}, u32[]{:S(2)}, u32[]{:S(2)}) collective-permute-start(bf16[4,80,1024]{2,1,0:T(8,128)(2,1)} %get-tuple-element.48), channel_id=1, source_target_pairs={{32,24},{64,56},{96,88},{128,120},{160,152},{192,184},{224,216},{3... | collective-permute-start | bytes 1966088 | tf_op jit(solution)/shard_map/ppermute | solution.py:670
  32.7 15.1 %copy-start.3 = (bf16[4,80,1024]{2,1,0:T(8,128)(2,1)S(1)}, bf16[4,80,1024]{2,1,0:T(8,128)(2,1)}, u32[]{:S(2)}) copy-start(bf16[4,80,1024]{2,1,0:T(8,128)(2,1)} %get-tuple-element.48) | copy-start | bytes 1966084
  32.7 25.6 %copy-start.1 = (bf16[1,128,4,1024]{3,2,1,0:T(4,128)(2,1)S(1)}, bf16[1,128,4,1024]{3,2,1,0:T(4,128)(2,1)}, u32[]{:S(2)}) copy-start(bf16[1,128,4,1024]{3,2,1,0:T(4,128)(2,1)} %param.10) | copy-start | bytes 3145732
  47.8 28.3 %collective-permute-start.3 = (bf16[4,80,1024]{2,1,0:T(8,128)(2,1)S(1)}, bf16[4,80,1024]{2,1,0:T(8,128)(2,1)}, u32[]{:S(2)}, u32[]{:S(2)}) collective-permute-start(bf16[4,80,1024]{2,1,0:T(8,128)(2,1)S(1)} %copy-done.3), channel_id=1, source_target_pairs={{8,0},{16,8},{24,16},{40,32},{48,40},{56,48},{72,64},{80,72},{88,8... | collective-permute-start | bytes 1966088 | tf_op jit(solution)/shard_map/ppermute | solution.py:675
  49.9 10.4 %collective-permute-start.1 = (bf16[128,1536]{1,0:T(8,128)(2,1)}, bf16[128,1536]{1,0:T(8,128)(2,1)}, u32[]{:S(2)}, u32[]{:S(2)}) collective-permute-start(bf16[128,1536]{1,0:T(8,128)(2,1)} %get-tuple-element.44.refs_1_), channel_id=1, source_target_pairs={{0,1},{1,0},{2,3},{3,2},{4,5},{5,4},{6,7},{7,6},{8,9},{9,8},{10,11... | collective-permute-start | bytes 1179656 | tf_op jit(solution)/shard_map/ppermute | solution.py:659
  49.9 26.1 %collective-permute-start.5 = (bf16[4,48,1024]{2,1,0:T(8,128)(2,1)}, bf16[4,48,1024]{2,1,0:T(8,128)(2,1)}, u32[]{:S(2)}, u32[]{:S(2)}) collective-permute-start(bf16[4,48,1024]{2,1,0:T(8,128)(2,1)} %collective-permute-done.2.near1), channel_id=1, source_target_pairs={{56,24},{88,56},{120,88},{152,120},{184,152},{216,184},{248,216},{... | collective-permute-start | bytes 1179656 | tf_op jit(solution)/shard_map/ppermute | solution.py:674
  60.3 1.0 copy-start.7
  64.3 11.7 %copy-start.8 = (bf16[4,80,1024]{2,1,0:T(8,128)(2,1)}, bf16[4,80,1024]{2,1,0:T(8,128)(2,1)S(1)}, u32[]{:S(2)}) copy-start(bf16[4,80,1024]{2,1,0:T(8,128)(2,1)S(1)} %collective-permute-done.4.far0) | copy-start | bytes 1966084
  84.2 2.4 %collective-permute-start.6 = (bf16[128,2560]{1,0:T(8,128)(2,1)}, bf16[128,2560]{1,0:T(8,128)(2,1)S(1)}, u32[]{:S(2)}, u32[]{:S(2)}) collective-permute-start(bf16[128,2560]{1,0:T(8,128)(2,1)} %get-tuple-element.54.refs_1_.right), channel_id=1, source_target_pairs={{0,1},{1,0},{2,3},{3,2},{4,5},{5,4},{6,7},{7,6},{8,9},{9,8},{10,11... | collective-permute-start | bytes 1966088 | tf_op jit(solution)/shard_map/ppermute | solution.py:659
  86.6 0.8 copy-start.9
  92.4 29.2 %collective-permute-start.8 = (bf16[128,2048]{1,0:T(8,128)(2,1)}, bf16[128,2048]{1,0:T(8,128)(2,1)S(1)}, u32[]{:S(2)}, u32[]{:S(2)}) collective-permute-start(bf16[128,2048]{1,0:T(8,128)(2,1)} %get-tuple-element.55), channel_id=1, source_target_pairs={{2,4},{3,5},{4,2},{5,3},{10,12},{11,13},{12,10},{13,11},{18,20},{1... | collective-permute-start | bytes 1572872 | tf_op jit(solution)/shard_map/ppermute | solution.py:663
  93.1 18.8 %collective-permute-start.7 = (bf16[128,2048]{1,0:T(8,128)(2,1)}, bf16[128,2048]{1,0:T(8,128)(2,1)S(1)}, u32[]{:S(2)}, u32[]{:S(2)}) collective-permute-start(bf16[128,2048]{1,0:T(8,128)(2,1)} %get-tuple-element.55), channel_id=1, source_target_pairs={{0,2},{1,3},{6,4},{7,5},{8,10},{9,11},{14,12},{15,13},{16,18},{17,... | collective-permute-start | bytes 1572872 | tf_op jit(solution)/shard_map/ppermute | solution.py:663
  94.4 27.1 %collective-permute-start.9 = (bf16[128,2048]{1,0:T(8,128)(2,1)}, bf16[128,2048]{1,0:T(8,128)(2,1)S(1)}, u32[]{:S(2)}, u32[]{:S(2)}) collective-permute-start(bf16[128,2048]{1,0:T(8,128)(2,1)} %get-tuple-element.69), channel_id=1, source_target_pairs={{0,2},{1,3},{2,0},{3,1},{4,6},{5,7},{6,4},{7,5},{8,10},{9,11},{10,... | collective-permute-start | bytes 1572872 | tf_op jit(solution)/shard_map/ppermute | solution.py:663
  94.5 34.9 %collective-permute-start.10 = (bf16[128,2048]{1,0:T(8,128)(2,1)}, bf16[128,2048]{1,0:T(8,128)(2,1)}, u32[]{:S(2)}, u32[]{:S(2)}) collective-permute-start(bf16[128,2048]{1,0:T(8,128)(2,1)} %get-tuple-element.70), channel_id=1, source_target_pairs={{0,4},{1,5},{6,2},{7,3},{8,12},{9,13},{14,10},{15,11},{16,20},{17,... | collective-permute-start | bytes 1572872 | tf_op jit(solution)/shard_map/ppermute | solution.py:663
  100.4 11.5 %copy-start.4 = (bf16[128,2048]{1,0:T(8,128)(2,1)S(1)}, bf16[128,2048]{1,0:T(8,128)(2,1)}, u32[]{:S(2)}) copy-start(bf16[128,2048]{1,0:T(8,128)(2,1)} %get-tuple-element.70) | copy-start | bytes 1572868
  100.5 13.0 %copy-start.5 = (bf16[4,48,1024]{2,1,0:T(8,128)(2,1)S(1)}, bf16[4,48,1024]{2,1,0:T(8,128)(2,1)}, u32[]{:S(2)}) copy-start(bf16[4,48,1024]{2,1,0:T(8,128)(2,1)} %get-tuple-element.42) | copy-start | bytes 1179652
  111.9 1.7 %copy-start.2 = (bf16[4,128,1024]{2,1,0:T(8,128)(2,1)S(1)}, bf16[4,128,1024]{2,1,0:T(8,128)(2,1)}, u32[]{:S(2)}) copy-start(bf16[4,128,1024]{2,1,0:T(8,128)(2,1)} %get-tuple-element.68) | copy-start | bytes 3145732
  112.0 31.8 %collective-permute-start.11 = (bf16[128,2048]{1,0:T(8,128)(2,1)S(1)}, bf16[128,2048]{1,0:T(8,128)(2,1)S(1)}, u32[]{:S(2)}, u32[]{:S(2)}) collective-permute-start(bf16[128,2048]{1,0:T(8,128)(2,1)S(1)} %add_convert_fusion), channel_id=1, source_target_pairs={{2,6},{3,7},{4,0},{5,1},{10,14},{11,15},{12,8},{13,9},{18,22},{19,... | collective-permute-start | bytes 1572872 | tf_op jit(solution)/shard_map/ppermute | solution.py:663
  116.7 30.9 %all-to-all-start = ((bf16[8,32,512]{2,1,0:T(8,128)(2,1)}), bf16[8,32,512]{2,1,0:T(8,128)(2,1)S(1)}, u32[]{:S(2)}, u32[]{:S(2)}) async-start(bf16[8,32,512]{2,1,0:T(8,128)(2,1)} %get-tuple-element.74), calls=%async_computation | async-start | bytes 524288 | tf_op jit(solution)/shard_map/all_to_all | solution.py:693
  121.6 22.3 %copy-start.11 = (bf16[128,2048]{1,0:T(8,128)(2,1)}, bf16[128,2048]{1,0:T(8,128)(2,1)S(1)}, u32[]{:S(2)}) copy-start(bf16[128,2048]{1,0:T(8,128)(2,1)S(1)} %collective-permute-done.9.refs_2_) | copy-start | bytes 1572868
  121.6 22.2 %copy-start.10 = (bf16[128,2048]{1,0:T(8,128)(2,1)}, bf16[128,2048]{1,0:T(8,128)(2,1)S(1)}, u32[]{:S(2)}) copy-start(bf16[128,2048]{1,0:T(8,128)(2,1)S(1)} %collective-permute-done.8.refs_1_) | copy-start | bytes 1572868
  143.8 0.8 copy-start.12
  147.6 0.7 copy-start.6

commit v2 on v1

--- a/solution.py
+++ b/solution.py
@@ -20,7 +20,6 @@
 ROWS = 16
 RUN = 4
 FORWARD_COST = 1
-FINISH_COST = 100
 RIGHT = 3 * INNER + D
 LEFT = D + INNER
 FRONT = 80
@@ -80,7 +79,7 @@
     bhl[32:64, :] = low
 
 
-def forward(x, bhl, gain, w, wo, seg, s):
+def forward(x, bhl, gain, w, wo, seg, s, wait):
     eye = iota((T, T), 0) == iota((T, T), 1)
     raw = jnp.zeros((64, T), F32)
     square = jnp.zeros((T, T), F32)
@@ -135,6 +134,7 @@
         return 0
 
     lax.fori_loop(0, T // ROWS, join_rows, 0)
+    wait("w")
     projected = dot(s["normed"][...], w[...]).astype(BF16)
     s["proj"][...] = projected
     ones = head_ones()
@@ -160,6 +160,7 @@
             s["weights"][2 * pair + half] = weights
             parts.append(dot(weights.astype(BF16), v))
         s["ctx"][:, lanes] = jnp.where(low, parts[0], parts[1]).astype(BF16)
+    wait("wo")
     s["att"][...] = dot(s["ctx"][...], wo[...]).astype(BF16)
 
 
@@ -220,7 +221,7 @@
         norm_back(jnp.where(low, dk[0], dk[1]), PAIRS + pair)
 
 
-def stream_back(x, g, bhl, gain, w, s, o, t, put):
+def stream_back(x, g, gain, w, s, o, t):
     eye = iota((T, T), 0) == iota((T, T), 1)
     t["dn"][...] = dot(o["dproj"][...], w[...], NT).astype(BF16)
 
@@ -273,14 +274,16 @@
     dot_mc = jnp.sum(dot_mc, axis=0, keepdims=True)
     kappa = inv * inv * dot_mc * (1.0 / (LANES * D))
     scaled = jnp.concatenate([a * inv for a in dmc] + [jnp.zeros((8, T), F32)], axis=0)
-    back = tokens_first(jnp.concatenate([scaled, scaled, kappa], axis=0))
-    t["back"][...] = back
-    lead = back[:, 0:64].astype(BF16)
+    t["back"][...] = tokens_first(jnp.concatenate([scaled, scaled, kappa], axis=0))
     rows_first = scaled.astype(BF16)
     for j in range(LANES):
-        cols = slice(j * D, (j + 1) * D)
-        o["dproj_map"][:, cols] = dot(rows_first, x[j])
-        t["f"][j] = dot(lead, bhl[:, cols])
+        o["dproj_map"][:, j * D : (j + 1) * D] = dot(rows_first, x[j])
+
+
+def stream_out(x, g, bhl, s, t, put):
+    lead = t["back"][:, 0:64].astype(BF16)
+    for j in range(LANES):
+        t["f"][j] = dot(lead, bhl[:, j * D : (j + 1) * D])
 
     def stream_rows(put, block, _):
         rows = pl.ds(pl.multiple_of(block * ROWS, ROWS), ROWS)
@@ -315,12 +318,10 @@
 )
 LEFT_OUT = (("left", (T, LEFT), BF16),)
 MAP = (("dproj_map", (32, LANES * D), F32), ("dgain", (1, D), F32))
-TEMPS = (
-    ("dn", (T, D), BF16),
-    ("dj", (T, D), F32),
-    ("back", (T, 128), F32),
-    ("f", (LANES, T, D), F32),
-)
+CARRIED = (("dj", (T, D), F32), ("back", (T, 128), F32))
+NORM = (("dn", (T, D), BF16),)
+MAPPED = (("f", (LANES, T, D), F32),)
+TEMPS = CARRIED + NORM + MAPPED
 STREAMS = (("g", (LANES, T, D), BF16),)
 VMEM = pl.BlockSpec(memory_space=pltpu.VMEM)
 ANY = pl.BlockSpec(memory_space=pl.ANY)
@@ -362,6 +363,34 @@
     )(*args)
 
 
+def brought(table, sources, rest, sem):
+    buffers = named(table, rest)
+    copies = {
+        name: pltpu.make_async_copy(source, buffers[name], sem.at[k])
+        for k, (name, source) in enumerate(zip(names(table), sources))
+    }
+    for copy in copies.values():
+        copy.start()
+    return buffers, lambda name: copies[name].wait()
+
+
+def bring_adjoint(where, near, far, final, g, sem):
+    parts = [g.at[:, pl.ds(0, FRONT), :], g.at[:, pl.ds(FRONT, T - FRONT), :]]
+    last = [final.at[:, pl.ds(0, FRONT), :], final.at[:, pl.ds(FRONT, T - FRONT), :]]
+    for case, sources in enumerate((near, far, last)):
+
+        @pl.when(where[0] == case)
+        def _(sources=sources):
+            for k in range(2):
+                pltpu.make_async_copy(sources[k], parts[k], sem.at[k]).start()
+
+    def wait():
+        for k in range(2):
+            pltpu.make_async_copy(near[k], parts[k], sem.at[k]).wait()
+
+    return wait
+
+
 def factors(refs, right, left):
     if right is not None:
         refs["dproj"] = right.at[:, pl.ds(0, 3 * INNER)]
@@ -372,24 +401,49 @@
     return refs
 
 
+WEIGHTS = (("w", (D, 3 * INNER), BF16), ("wo", (INNER, D), BF16))
+EARLY = (("x_rows", (T, LANES, D), BF16),)
+LATE = EARLY + WEIGHTS + (("g_rows", (T, LANES, D), BF16),)
+LANED = (("x", (LANES, T, D), BF16), ("g", (LANES, T, D), BF16))
+
+
+def lanes_apart(source, out):
+    def some_rows(block, _):
+        rows = pl.ds(pl.multiple_of(block * ROWS, ROWS), ROWS)
+        for j in range(LANES):
+            out[j, rows, :] = source[rows, j, :]
+        return 0
+
+    lax.fori_loop(0, T // ROWS, some_rows, 0)
+
+
 def whole_tick(x, g, seg, bt, gain, w, wo):
     outs = [
         ("dx_front", (LANES, FRONT, D), BF16),
         ("dx_back", (LANES, T - FRONT, D), BF16),
-        ("factors", (T, RIGHT + LEFT), BF16),
+        ("right", (T, RIGHT), BF16),
+        ("left", (T, LEFT), BF16),
         *MAP,
     ]
 
     def body(x, g, seg, bt, gain, w, wo, *rest):
         o = named(outs, rest)
-        right = o["factors"].at[:, pl.ds(0, RIGHT)]
-        s = factors({}, None, o["factors"].at[:, pl.ds(RIGHT, LEFT)])
-        factors(o, right, None)
+        s = factors({}, None, o["left"])
+        factors(o, o["right"], None)
         rest = rest[len(outs) :]
         s.update(named(SAVED, rest))
         t = named(TEMPS, rest[len(SAVED) :])
+        rest = rest[len(SAVED) + len(TEMPS) :]
+        buffers, wait = brought(LATE, (x.at[0], w, wo, g), rest, rest[-1])
+        x_rows, w, wo, g_rows = (buffers[k] for k in names(LATE))
+        laned = named(LANED, rest[len(LATE) :])
+        wait("x_rows")
+        lanes_apart(x_rows, laned["x"])
+        x, g = laned["x"], laned["g"]
         stacked_map(bt, s["bhl"])
-        forward(x, s["bhl"], gain, w, wo, seg, s)
+        forward(x, s["bhl"], gain, w, wo, seg.at[pl.ds(0, 1), :], s, wait)
+        wait("g_rows")
+        lanes_apart(g_rows, g)
         adjoint_rows(g, s, o["datt"])
         attention_back(o["datt"], wo, s, o["dproj"])
 
@@ -402,96 +456,105 @@
 
         cut = FRONT // ROWS
         put = ((0, cut, put_front), (cut, T // ROWS, put_back))
-        stream_back(x, g, s["bhl"], gain, w, s, o, t, put)
+        stream_back(x, g, gain, w, s, o, t)
+        stream_out(x, g, s["bhl"], s, t, put)
 
     got = call(
         body,
         shapes(outs),
-        scratch(SAVED) + scratch(TEMPS),
+        scratch(SAVED)
+        + scratch(TEMPS)
+        + scratch(LATE)
+        + scratch(LANED)
+        + [pltpu.SemaphoreType.DMA((len(LATE),))],
         (x, g, seg, bt, gain, w, wo),
         20,
         "whole_tick",
+        [ANY, ANY, VMEM, VMEM, VMEM, ANY, ANY],
     )
     return named(outs, got)
 
 
 def forward_tick(x, seg, bt, gain, w, wo):
-    table = SAVED + LEFT_OUT
-
-    def body(x, seg, bt, gain, w, wo, *outs):
-        s = named(table, outs)
+    table = SAVED + LEFT_OUT + LANED[:1]
+    late = EARLY + WEIGHTS
+
+    def body(x, seg, bt, gain, w, wo, *rest):
+        s = named(table, rest)
         factors(s, None, s["left"])
+        *rest, sem = rest[len(table) :]
+        buffers, wait = brought(late, (x.at[1], w, wo), rest, sem)
+        x_rows, w, wo = (buffers[k] for k in names(late))
         stacked_map(bt, s["bhl"])
-        forward(x, s["bhl"], gain, w, wo, seg, s)
-
-    got = call(body, shapes(table), [], (x, seg, bt, gain, w, wo), FORWARD_COST, "forward_tick")
+        wait("x_rows")
+        lanes_apart(x_rows, s["x"])
+        forward(s["x"], s["bhl"], gain, w, wo, seg.at[pl.ds(1, 1), :], s, wait)
+
+    got = call(
+        body,
+        shapes(table),
+        scratch(late) + [pltpu.SemaphoreType.DMA((len(late),))],
+        (x, seg, bt, gain, w, wo),
+        FORWARD_COST,
+        "forward_tick",
+        [ANY, VMEM, VMEM, VMEM, ANY, ANY],
+    )
     return named(table, got)
 
 
-ATTENTION = [e for e in SAVED if e[0] in ("coef", "proj", "scale", "qk", "weights")]
+ATTENTION = [e for e in SAVED if e[0] in ("proj", "scale", "qk", "weights")]
 
 
 def attention_tick(where, near, far, final, wo, saved, after):
-    def body(where, near0, near1, far0, far1, final, after, wo, *rest):
-        s = named(ATTENTION, rest)
-        g, right, sem = rest[len(ATTENTION) :]
-
-        def fetch(sources):
-            copies = [pltpu.make_async_copy(a, b, sem.at[k]) for k, (a, b) in enumerate(sources)]
-            for copy in copies:
-                copy.start()
-            for copy in copies:
-                copy.wait()
-
-        head = g.at[:, pl.ds(0, FRONT), :]
-        tail = g.at[:, pl.ds(FRONT, T - FRONT), :]
-
-        @pl.when(where[0] == 0)
-        def _():
-            fetch([(near0, head), (near1, tail)])
-
-        @pl.when(where[0] == 1)
-        def _():
-            fetch([(far0, head), (far1, tail)])
-
-        @pl.when(where[0] == 2)
-        def _():
-            fetch([(final, g)])
-
+    table = WEIGHTS[1:] + tuple(ATTENTION)
+
+    def body(where, near0, near1, far0, far1, final, after, coef, *rest):
+        sources, right, g = rest[: len(table)], rest[len(table)], rest[len(table) + 1]
+        *buffers, g_sem, sem = rest[len(table) + 2 :]
+        ready = bring_adjoint(where, (near0, near1), (far0, far1), final, g, g_sem)
+        s, wait = brought(table, sources, buffers, sem)
         o = factors({}, right, None)
-        adjoint_rows(g, s, o["datt"])
-        attention_back(o["datt"], wo, s, o["dproj"])
-
-    args = (where, *near, *far, final, after, wo, *[saved[k] for k in names(ATTENTION)])
+        ready()
+        adjoint_rows(g, {"coef": coef}, o["datt"])
+        for name in names(table):
+            wait(name)
+        attention_back(o["datt"], s["wo"], s, o["dproj"])
+
+    args = (where, *near, *far, final, after, saved["coef"], wo, *[saved[k] for k in names(ATTENTION)])
     return call(
         body,
-        shapes(STREAMS) + [struct((T, RIGHT), BF16)],
-        [pltpu.SemaphoreType.DMA((2,))],
+        [struct((T, RIGHT), BF16)],
+        scratch(STREAMS)
+        + scratch(table)
+        + [pltpu.SemaphoreType.DMA((2,)), pltpu.SemaphoreType.DMA((len(table),))],
         args,
         5,
         "attention_tick",
-        [SMEM] + [ANY] * 6 + [VMEM] * (1 + len(ATTENTION)),
-    )
-
-
-REST = [e for e in SAVED if e[0] in ("mc", "sink", "coef", "joined", "r", "att", "bhl")]
-
-
-def stream_tick(x, g, gain, w, right, saved, earlier, n, after):
-    def body(after, x, g, gain, w, right, *rest):
+        [SMEM] + [ANY] * 6 + [VMEM] + [ANY] * len(table),
+    )[0]
+
+
+REST = [e for e in SAVED if e[0] in ("mc", "sink", "joined", "r", "att")]
+
+
+def stream_tick(x, adjoint, gain, w, right, saved, earlier, n, after):
+    where, near, far, final = adjoint
+
+    def body(where, near0, near1, far0, far1, final, after, x, gain, w, right, *rest):
         s = named(REST, rest)
         rest = rest[len(REST) :]
         first = named(MAP, rest)
-        dx, parts, *rest = rest[len(MAP) :]
+        parts, *rest = rest[len(MAP) :]
+        t = named(CARRIED, rest)
+        rest = rest[len(CARRIED) :]
         o = named(MAP, rest)
         factors(o, right, None)
-        t = named(TEMPS, rest[len(MAP) :])
-
-        def put_rows(block, j, value):
-            dx[j, pl.ds(pl.multiple_of(block * ROWS, ROWS), ROWS), :] = value
-
-        put = ((0, T // ROWS, put_rows),)
-        stream_back(x, g, s["bhl"], gain, w, s, o, t, put)
+        rest = rest[len(MAP) :]
+        t.update(named(NORM, rest))
+        g, sem = rest[len(NORM) :]
+        ready = bring_adjoint(where, (near0, near1), (far0, far1), final, g, sem)
+        ready()
+        stream_back(x, g, gain, w, s, o, t)
         width = LANES * D // n
         for d in range(n):
             cols = slice(d * width, d * width + width)
@@ -502,36 +565,53 @@
             total = jnp.broadcast_to(total, (8, width))
             parts[d] = jnp.concatenate([proj[0:24], total], axis=0).astype(BF16)
 
+    args = (where, *near, *far, final, after, x, gain, w, right)
+    args += tuple(saved[k] for k in names(REST)) + tuple(earlier[k] for k in names(MAP))
     return call(
         body,
-        [struct((LANES, T, D), BF16), struct((n, 32, LANES * D // n), BF16)],
-        scratch(MAP) + scratch(TEMPS),
-        (
-            after,
-            x,
-            g,
-            gain,
-            w,
-            right,
-            *[saved[k] for k in names(REST)],
-            *[earlier[k] for k in names(MAP)],
-        ),
-        9,
+        [struct((n, 32, LANES * D // n), BF16)] + shapes(CARRIED),
+        scratch(MAP) + scratch(NORM) + scratch(STREAMS) + [pltpu.SemaphoreType.DMA((2,))],
+        args,
+        6,
         "stream_tick",
-        [ANY] + [VMEM] * (5 + len(REST) + len(MAP)),
-    )
+        [SMEM] + [ANY] * 6 + [VMEM] * (4 + len(REST) + len(MAP)),
+    )
+
+
+def output_tick(x, adjoint, coef, bhl, dj, back, after):
+    where, near, far, final = adjoint
+
+    def body(where, near0, near1, far0, far1, final, after, x, coef, bhl, dj, back, dx, *rest):
+        t = {"dj": dj, "back": back, "f": rest[0]}
+        g, sem = rest[1:]
+        ready = bring_adjoint(where, (near0, near1), (far0, far1), final, g, sem)
+        ready()
+
+        def put_rows(block, j, value):
+            dx[j, pl.ds(pl.multiple_of(block * ROWS, ROWS), ROWS), :] = value
+
+        stream_out(x, g, bhl, {"coef": coef}, t, ((0, T // ROWS, put_rows),))
+
+    return call(
+        body,
+        [struct((LANES, T, D), BF16)],
+        scratch(MAPPED) + scratch(STREAMS) + [pltpu.SemaphoreType.DMA((2,))],
+        (where, *near, *far, final, after, x, coef, bhl, dj, back),
+        5,
+        "output_tick",
+        [SMEM] + [ANY] * 6 + [VMEM] * 5,
+    )[0]
 
 
 STEPS = 4
 
 
-def turned_factors(place, first, second):
+def turned_factors(place, sides):
     rows, few = D // (2 * STEPS), INNER // (2 * STEPS)
 
     def body(place, *refs):
         refs, (left, small) = refs[:STEPS], refs[STEPS:]
-        sides = [refs[k].at[:, pl.ds(RIGHT if k % 2 == 0 else 0, LEFT)] for k in range(STEPS)]
-        sides = [factors({}, None, side) for side in sides]
+        sides = [factors({}, None, side) for side in refs]
         even = place[STEPS] == 0
         for step in range(STEPS):
             chip = place[step]
@@ -549,7 +629,7 @@
         body,
         [struct((STEPS * rows, STEPS * T), BF16), struct((STEPS * few, STEPS * T), BF16)],
         [],
-        (place, first[0], second[0], first[1], second[1]),
+        (place, *sides),
         FORWARD_COST,
         "turned_factors",
         [SMEM] + [VMEM] * STEPS,
@@ -592,11 +672,11 @@
     return own, sends
 
 
-def finish_terms(terms):
+def finish_terms(terms, after):
     few = INNER // (2 * STEPS)
 
     def body(*refs):
-        *others, grad_qkv, grad_out = refs[1:]
+        *others, _, grad_qkv, grad_out = refs[1:]
         total = refs[0][...]
         for other in others:
             total = total + other[...].astype(F32)
@@ -606,13 +686,14 @@
 
     rows = terms[0].shape[0]
     outs = [struct((rows, 3 * INNER), F32), struct((few, D), F32)]
-    return call(body, outs, [], terms, FINISH_COST, "finish_terms")
-
-
-def finish_map(parts, n, after):
+    specs = [VMEM] * len(terms) + [ANY]
+    return call(body, outs, [], (*terms, after), 2, "finish_terms", specs)
+
+
+def finish_map(parts, n):
     width = LANES * D // n
 
-    def body(parts, after, grad_map, grad_gain):
+    def body(parts, grad_map, grad_gain):
         total = parts[0].astype(F32)
         for d in range(1, n):
             total = total + parts[d].astype(F32)
@@ -623,10 +704,9 @@
         body,
         [struct((24, width), F32), struct((1, D // n), F32)],
         [],
-        (parts, after),
+        (parts,),
         1,
         "finish_map",
-        [VMEM, ANY],
     )
 
 
@@ -646,9 +726,8 @@
     replica = lax.axis_index("dp")
     chip, core = replica // 2, replica % 2
     lanes_first = lambda a: jnp.transpose(a, (1, 0, 2))
-    x0 = lanes_first(saved_entering_lanes[0, 0])
-    x1 = lanes_first(saved_entering_lanes[0, 1])
-    opening = lanes_first(opening_adjoint[0])
+    x = saved_entering_lanes[0]
+    opening = opening_adjoint[0]
     final = lanes_first(final_later_adjoint[0])
     bt = blend_linear_map[0].T
     gain = rescale_amplitude
@@ -662,37 +741,37 @@
         route = [(2 * a + c, 2 * b + c) for a, b in chips for c in range(2)]
         return lax.ppermute(value, "dp", route)
 
-    first = whole_tick(x0, opening, document_labels[0, 0:1], bt, gain, w, wo)
+    first = whole_tick(x, opening, document_labels[0], bt, gain, w, wo)
 
     near = [(s, s - 1) for s in range(1, layers) if s % RUN]
     cross = range(RUN, layers, RUN)
     hop = lax.ppermute(first["dx_back"], "section", near + [(s, s + RUN - 1) for s in cross])
     front_far = lax.ppermute(first["dx_front"], "section", [(s, s - 1) for s in cross])
-    other = swap_cores(first["factors"])
-    saved = forward_tick(x1, document_labels[0, 1:2], bt, gain, w, wo)
+    others_left, others_right = swap_cores(first["left"]), swap_cores(first["right"])
+    saved = forward_tick(x, document_labels[0], bt, gain, w, wo)
     coming, later, _ = lax.optimization_barrier((hop, first["dx_front"], saved["coef"]))
     far = lax.ppermute(coming, "section", [(s + RUN - 1, s - 1) for s in cross])
     front_near = lax.ppermute(later, "section", near)
     place = jnp.stack([chip ^ step for step in range(STEPS)] + [core])
     left, small = turned_factors(
-        place, (first["factors"], other), (saved["left"], swap_cores(saved["left"]))
+        place, (first["left"], saved["left"], others_left, swap_cores(saved["left"]))
     )
     where = jnp.where(section == layers - 1, 2, jnp.where(section % RUN == RUN - 1, 1, 0))
-    g, right = attention_tick(
-        where[None], (front_near, hop), (front_far, far), final, wo, saved, left
-    )
-    own, sends = terms(left, small, [first["factors"], right, other, swap_cores(right)])
+    adjoint = (where[None], (front_near, hop), (front_far, far), final)
+    right = attention_tick(*adjoint, wo, saved, left)
+    own, sends = terms(left, small, [first["right"], right, others_right, swap_cores(right)])
     by_way = along(sends[2], (0, 1), (3, 2))
     middle = along(sends[2], (1, 2), (2, 1))
     beside = along(sends[0], (0, 1), (1, 0), (2, 3), (3, 2))
     outer = along(sends[1], (0, 2), (3, 1))
-    dx1, parts = stream_tick(x1, g, gain, w, right, saved, first, n, own)
-    by_way, dx1, parts = lax.optimization_barrier((by_way, dx1, parts))
+    parts, dj, back = stream_tick(saved["x"], adjoint, gain, w, right, saved, first, n, own)
+    by_way, parts = lax.optimization_barrier((by_way, parts))
     both = (sends[1].astype(F32) + by_way.astype(F32)).astype(BF16)
     grads = [own, middle, beside, outer, along(both, (1, 3), (2, 0))]
+    dx1 = output_tick(saved["x"], adjoint, saved["coef"], saved["bhl"], dj, back, both)
     parts = lax.all_to_all(parts, "dp", 0, 0)
-    grad_qkv, grad_out = finish_terms(grads)
-    grad_map, grad_gain = finish_map(parts, n, grad_qkv)
+    grad_map, grad_gain = finish_map(parts, n)
+    grad_qkv, grad_out = finish_terms(grads, grad_map)
     dx0 = jnp.concatenate([first["dx_front"], first["dx_back"]], axis=1)
     sent = jnp.stack([jnp.transpose(dx0, (1, 0, 2)), jnp.transpose(dx1, (1, 0, 2))])[None]
     return (sent, grad_qkv[None], grad_out[None], grad_map.T[None], grad_gain)

time: 151 us -> 147 us (0.974)
  Pallas kernels: 62.7 us -> 71.4 us
  local copies, waits for them, and re-layouts: 15.5 us -> 7.33 us
  waiting for transfers between devices: 41.7 us -> 34.7 us
  starting transfers between devices: 28.8 us -> 30.4 us
    ppermute x5, waiting for transfers between devices: 22.2 us -> 8.72 us  [along(): return lax.ppermute(value, 'dp', route)]
    all_to_all x1, waiting for transfers between devices: 0.01 us -> 9.95 us  [shards(): parts = lax.all_to_all(parts, 'dp', 0, 0)]
    pallas_call x8 -> x9, Pallas kernels: 62.7 us -> 71.4 us  [call(): pl.pallas_call(body, out_shape=outs, in_specs=specs or [VMEM] * len(args)...]
    unnamed x31 -> x30, local copies, waits for them, and re-layouts: 12.7 us -> 6.65 us
    ppermute x5, starting transfers between devices: 9.45 us -> 11.9 us  [along(): return lax.ppermute(value, 'dp', route)]
    ppermute x1, waiting for transfers between devices: 5.48 us -> 3.19 us  [shards(): lax.ppermute(first['dx_back'], 'section', near + [(s, s + RUN - 1) for s...]
  transfers between devices with their start and end apart: 13 -> 14, of which waited for: 5 -> 5; matrix products, arithmetic and copies ran while one was open for 4% -> 4% of each run, Pallas kernels for 18% -> 27%
where the time goes in v2:
time: 147 us; the launch traced here: 146 us
  Pallas kernels  71.4 us (49%)
  waiting for transfers between devices  34.7 us (24%)
  starting transfers between devices  30.4 us (21%)
  local copies, waits for them, and re-layouts  7.33 us (5%)
  other arithmetic  1.62 us (1%)
    pallas_call x9, Pallas kernels, call(): pl.pallas_call(body, out_shape=outs, in_specs=specs or [VMEM] * len(args)...  71.4 us
    ppermute x5, starting transfers between devices, along(): return lax.ppermute(value, 'dp', route)  11.9 us
    ppermute x1, waiting for transfers between devices, shards(): far = lax.ppermute(coming, 'section', [(s + RUN - 1, s - 1) for s in cross])  10.6 us
    all_to_all x1, waiting for transfers between devices, shards(): parts = lax.all_to_all(parts, 'dp', 0, 0)  9.95 us
    ppermute x5, waiting for transfers between devices, along(): return lax.ppermute(value, 'dp', route)  8.72 us
    ppermute x1, starting transfers between devices, shards(): far = lax.ppermute(coming, 'section', [(s + RUN - 1, s - 1) for s in cross])  8.22 us
    unnamed x30, local copies, waits for them, and re-layouts  6.65 us
    all_to_all x1, starting transfers between devices, shards(): parts = lax.all_to_all(parts, 'dp', 0, 0)  4.18 us
  transfers between devices with their start and end apart: 14, of which 5 were waited for; matrix products, arithmetic and copies ran while one was open for 4% of the time, Pallas kernels for 27%

profile of v2, /device:TPU:30, one launch (start us, length us, event | category | flops | bytes accessed | tf_op | source)
XLA Modules:
  0.0 146.4 jit_solution(12090941283255077026)
XLA Ops:
  0.6 24.0 %whole_tick.1 = (bf16[4,80,1024]{2,1,0:T(8,128)(2,1)}, bf16[4,48,1024]{2,1,0:T(8,128)(2,1)}, bf16[128,2560]{1,0:T(8,128)(2,1)}, bf16[128,1536]{1,0:T(8,128)(2,1)...) custom-call(bf16[2,128,4,1024]{3,2,1,0:T(4,128)(2,1)} %bitcast.36, bf16[128,4,1024]{2,1,0:T(4,128)(2,1)} %bitcast.49, ...), custom_call_target="tpu_custom_call" | custom-call | flops 20000000000 | bytes 40000000 | tf_op jit(solution)/shard_map/whole_tick/pallas_call | solution.py:352
  24.6 2.7 %collective-permute-start = (bf16[4,48,1024]{2,1,0:T(8,128)(2,1)}, bf16[4,48,1024]{2,1,0:T(8,128)(2,1)S(1)}, u32[]{:S(2)}, u32[]{:S(2)}) collective-permute-start(bf16[4,48,1024]{2,1,0:T(8,128)(2,1)} %get-tuple-element.42), channel_id=1, source_target_pairs={{8,0},{16,8},{24,16},{40,32},{48,40},{56,48},{72,64},{80,72},{88,8... | collective-permute-start | bytes 1179656 | tf_op jit(solution)/shard_map/ppermute | solution.py:748
  27.3 0.0 copy-start.1
  27.3 0.0 copy-start
  27.3 1.4 collective-permute-start.2
  28.8 12.2 %forward_tick.1 = (f32[32,128]{1,0:T(8,128)}, f32[20,13,8,128]{3,2,1,0:T(8,128)}, f32[128,128]{1,0:T(8,128)}, f32[128,1024]{1,0:T(8,128)}, f32[128,128]{1,0:T(8,...) custom-call(bf16[2,128,4,1024]{3,2,1,0:T(4,128)(2,1)} %bitcast.37, ...), custom_call_target="tpu_custom_call" | custom-call | flops 1000000000 | bytes 2000000 | tf_op jit(solution)/shard_map/forward_tick/pallas_call | solution.py:352
  41.0 3.2 %collective-permute-done.near1 = bf16[4,48,1024]{2,1,0:T(8,128)(2,1)S(1)} collective-permute-done((bf16[4,48,1024]{2,1,0:T(8,128)(2,1)}, bf16[4,48,1024]{2,1,0:T(8,128)(2,1)S(1)}, u32[]{:S(2)}, u32[]{:S(2)}) %collective-permute-start) | collective-permute-done | bytes 393248 | tf_op jit(solution)/shard_map/ppermute | solution.py:748
  44.2 0.0 copy-done.1
  44.2 1.3 collective-permute-start.1
  45.5 0.1 collective-permute-start.4
  45.6 0.5 collective-permute-start.5
  46.1 8.2 %collective-permute-start.3 = (bf16[4,48,1024]{2,1,0:T(8,128)(2,1)S(1)}, bf16[4,48,1024]{2,1,0:T(8,128)(2,1)}, u32[]{:S(2)}, u32[]{:S(2)}) collective-permute-start(bf16[4,48,1024]{2,1,0:T(8,128)(2,1)S(1)} %collective-permute-done.near1), channel_id=1, source_target_pairs={{56,24},{88,56},{120,88},{152,120},{184,152},{216,184},{248,216},{... | collective-permute-start | bytes 1179656 | tf_op jit(solution)/shard_map/ppermute | solution.py:753
  54.4 0.0 copy-done
  54.4 1.3 copy.16
  55.6 0.7 stack.33.place
  56.3 0.0 collective-permute-done.4.refs_2_
  56.3 0.0 collective-permute-start.6
  56.3 0.0 collective-permute-done.5.refs_3_
  56.3 2.6 %turned_factors.1 = (bf16[512,512]{1,0:T(8,128)(2,1)}, bf16[256,512]{1,0:T(8,128)(2,1)}) custom-call(s32[5]{0:T(128)} %stack.33.place, bf16[128,1536]{1,0:T(8,128)(2,1)} %get-tuple-element.46.refs_0_, bf16[128,1536]{1,0:T(8,128)(2,1)} %get-tuple-element.47.refs_1_, bf16[128,1536]{1,0:T(8,128)(2,1)} %collective-permute-done.4.refs_2_, ...), custom_call_target="tpu_custom_call" | custom-call | flops 1000000000 | bytes 2000000 | tf_op jit(solution)/shard_map/turned_factors/pallas_call | solution.py:352
  58.9 0.0 copy-done.13
  58.9 0.0 collective-permute-done.2.far0
  58.9 0.0 copy-start.6
  59.0 10.6 %collective-permute-done.3.far1 = bf16[4,48,1024]{2,1,0:T(8,128)(2,1)} collective-permute-done((bf16[4,48,1024]{2,1,0:T(8,128)(2,1)S(1)}, bf16[4,48,1024]{2,1,0:T(8,128)(2,1)}, u32[]{:S(2)}, u32[]{:S(2)}) %collective-permute-start.3) | collective-permute-done | bytes 393248 | tf_op jit(solution)/shard_map/ppermute | solution.py:753
  69.6 0.0 collective-permute-done.1.near0
  69.6 0.0 copy-done.6
  69.6 0.8 copy-done.7
  70.4 7.8 %attention_tick.1.refs_1_.right = bf16[128,2560]{1,0:T(8,128)(2,1)} custom-call(s32[1]{0:T(128)} %bitcast.9.where, bf16[4,80,1024]{2,1,0:T(8,128)(2,1)} %copy-done.7, bf16[4,48,1024]{2,1,0:T(8,128)(2,1)} %copy-done.13, bf16[4,80,1024]{2,1,0:T(8,128)(2,1)} %copy-done.6, bf16[4,48,1024]{2,1,0:T(8,128)(2,1)} %collective-permute-done.3.far1, ...), custom_call_target="tpu_custom_call" | custom-call | flops 5000000000 | bytes 10000000 | tf_op jit(solution)/shard_map/attention_tick/pallas_call | solution.py:352
  78.2 0.1 collective-permute-start.7
  78.3 0.0 copy-done.4
  78.3 0.1 maximum_bitcast_fusion.1
  78.4 0.0 collective-permute-done.6.refs_2_
  78.4 0.0 copy-start.8
  78.4 2.2 %collective-permute-done.7.refs_3_ = bf16[128,2560]{1,0:T(8,128)(2,1)S(1)} collective-permute-done((bf16[128,2560]{1,0:T(8,128)(2,1)}, bf16[128,2560]{1,0:T(8,128)(2,1)S(1)}, u32[]{:S(2)}, u32[]{:S(2)}) %collective-permute-start.7) | collective-permute-done | bytes 655392 | tf_op jit(solution)/shard_map/ppermute | solution.py:738
  80.6 0.0 copy-done.8
  80.6 0.8 copy-done.9
  81.5 4.7 %terms.1 = (f32[128,2048]{1,0:T(8,128)}, bf16[128,2048]{1,0:T(8,128)(2,1)}, bf16[128,2048]{1,0:T(8,128)(2,1)}, bf16[128,2048]{1,0:T(8,128)(2,1)}) custom-call(bf16[512,512]{1,0:T(8,128)(2,1)} %get-tuple-element.48.after.left, bf16[256,512]{1,0:T(8,128)(2,1)} %get-tuple-element.49.small, bf16[128,2560]{1,0:T(8,128)(2,1)} %get-tuple-element.50.refs_0_, ...), custom_call_target="tpu_custom_call" | custom-call | flops 4000000000 | bytes 8000000 | tf_op jit(solution)/shard_map/terms/pallas_call | solution.py:352
  86.1 0.7 collective-permute-start.9
  86.8 6.5 %collective-permute-start.8 = (bf16[128,2048]{1,0:T(8,128)(2,1)}, bf16[128,2048]{1,0:T(8,128)(2,1)S(1)}, u32[]{:S(2)}, u32[]{:S(2)}) collective-permute-start(bf16[128,2048]{1,0:T(8,128)(2,1)} %get-tuple-element.56), channel_id=1, source_target_pairs={{0,2},{1,3},{6,4},{7,5},{8,10},{9,11},{14,12},{15,13},{16,18},{17,... | collective-permute-start | bytes 1572872 | tf_op jit(solution)/shard_map/ppermute | solution.py:742
  93.3 0.1 collective-permute-start.10
  93.4 3.4 %collective-permute-start.11 = (bf16[128,2048]{1,0:T(8,128)(2,1)}, bf16[128,2048]{1,0:T(8,128)(2,1)S(1)}, u32[]{:S(2)}, u32[]{:S(2)}) collective-permute-start(bf16[128,2048]{1,0:T(8,128)(2,1)} %get-tuple-element.55), channel_id=1, source_target_pairs={{0,4},{1,5},{6,2},{7,3},{8,12},{9,13},{14,10},{15,11},{16,20},{17,... | collective-permute-start | bytes 1572872 | tf_op jit(solution)/shard_map/ppermute | solution.py:742
  96.8 0.0 copy-start.2
  96.8 9.9 %stream_tick.1 = (bf16[8,32,512]{2,1,0:T(8,128)(2,1)}, f32[128,1024]{1,0:T(8,128)}, f32[128,128]{1,0:T(8,128)}) custom-call(s32[1]{0:T(128)} %bitcast.9.where, bf16[4,80,1024]{2,1,0:T(8,128)(2,1)} %copy-done.7, bf16[4,48,1024]{2,1,0:T(8,128)(2,1)} %copy-done.13, bf16[4,80,1024]{2,1,0:T(8,128)(2,1)} %copy-done.6, ...), custom_call_target="tpu_custom_call" | custom-call | flops 6000000000 | bytes 12000000 | tf_op jit(solution)/shard_map/stream_tick/pallas_call | solution.py:352
  106.7 0.0 collective-permute-done.8
  106.7 0.0 copy-done.2
  106.8 0.1 add_convert_fusion.after
  106.9 0.0 copy-start.3
  106.9 4.2 %all-to-all-start = ((bf16[8,32,512]{2,1,0:T(8,128)(2,1)}), bf16[8,32,512]{2,1,0:T(8,128)(2,1)S(1)}, u32[]{:S(2)}, u32[]{:S(2)}) async-start(bf16[8,32,512]{2,1,0:T(8,128)(2,1)} %get-tuple-element.72), calls=%async_computation | async-start | bytes 524288 | tf_op jit(solution)/shard_map/all_to_all | solution.py:772
  111.1 1.3 collective-permute-start.12
  112.4 0.0 copy-done.3
  112.4 5.6 %output_tick.1 = bf16[4,128,1024]{2,1,0:T(8,128)(2,1)} custom-call(s32[1]{0:T(128)} %bitcast.9.where, bf16[4,80,1024]{2,1,0:T(8,128)(2,1)} %copy-done.7, bf16[4,48,1024]{2,1,0:T(8,128)(2,1)} %copy-done.13, bf16[4,80,1024]{2,1,0:T(8,128)(2,1)} %copy-done.6, bf16[4,48,1024]{2,1,0:T(8,128)(2,1)} %collective-permute-done.3.far1, bf16[4,128,1024]{2,1,0:T(8,128)(2,1)} %bitcast.43, ...), custom_call_target="tpu_custom_call" | custom-call | flops 5000000000 | bytes 10000000 | tf_op jit(solution)/shard_map/output_tick/pallas_call | solution.py:352
  118.0 1.4 maximum_bitcast_fusion
  119.5 2.9 %copy.14 = bf16[1,2,128,4,1024]{4,3,2,1,0:T(4,128)(2,1)} copy(bf16[1,2,128,4,1024]{4,2,3,1,0:T(8,128)(2,1)S(1)} %maximum_bitcast_fusion) | data formatting | bytes 4194304
  122.4 9.9 %all-to-all-done.parts = bf16[8,32,512]{2,1,0:T(8,128)(2,1)S(1)} async-done(((bf16[8,32,512]{2,1,0:T(8,128)(2,1)}), bf16[8,32,512]{2,1,0:T(8,128)(2,1)S(1)}, u32[]{:S(2)}, u32[]{:S(2)}) %all-to-all-start) | async-done | bytes 262176 | tf_op jit(solution)/shard_map/all_to_all | solution.py:772
  132.3 0.7 copy-done.5
  133.0 1.6 %finish_map.1 = (f32[24,512]{1,0:T(8,128)}, f32[1,128]{1,0:T(1,128)}) custom-call(bf16[8,32,512]{2,1,0:T(8,128)(2,1)} %copy-done.5), custom_call_target="tpu_custom_call" | custom-call | flops 1000000000 | bytes 2000000 | tf_op jit(solution)/shard_map/finish_map/pallas_call | solution.py:352
  134.6 0.0 collective-permute-done.10.refs_2_
  134.7 0.0 collective-permute-done.11.refs_3_
  134.7 0.0 copy-start.12
  134.7 0.0 collective-permute-done.9.refs_1_
  134.7 0.0 copy-start.10
  134.7 8.7 %collective-permute-done.12.refs_4_ = bf16[128,2048]{1,0:T(8,128)(2,1)} collective-permute-done((bf16[128,2048]{1,0:T(8,128)(2,1)S(1)}, bf16[128,2048]{1,0:T(8,128)(2,1)}, u32[]{:S(2)}, u32[]{:S(2)}) %collective-permute-start.12) | collective-permute-done | bytes 524320 | tf_op jit(solution)/shard_map/ppermute | solution.py:742
  143.4 0.0 copy-done.11
  143.4 0.0 copy-done.12
  143.4 3.0 %finish_terms.1 = (f32[128,1536]{1,0:T(8,128)}, f32[64,1024]{1,0:T(8,128)}) custom-call(f32[128,2048]{1,0:T(8,128)} %get-tuple-element.57.after.refs_0_, bf16[128,2048]{1,0:T(8,128)(2,1)} %copy-done.10, bf16[128,2048]{1,0:T(8,128)(2,1)} %copy-done.11, bf16[128,2048]{1,0:T(8,128)(2,1)} %copy-done.12, bf16[128,2048]{1,0:T(8,128)(2,1)} %collective-permute-done.12.refs_4_, ...), custom_call_target="tpu_custom_call" | custom-call | flops 2000000000 | bytes 4000000 | tf_op jit(solution)/shard_map/finish_terms/pallas_call | solution.py:352
  (7 shorter events, 0.0 us)
Async XLA Ops:
  24.6 19.5 %collective-permute-start = (bf16[4,48,1024]{2,1,0:T(8,128)(2,1)}, bf16[4,48,1024]{2,1,0:T(8,128)(2,1)S(1)}, u32[]{:S(2)}, u32[]{:S(2)}) collective-permute-start(bf16[4,48,1024]{2,1,0:T(8,128)(2,1)} %get-tuple-element.42), channel_id=1, source_target_pairs={{8,0},{16,8},{24,16},{40,32},{48,40},{56,48},{72,64},{80,72},{88,8... | collective-permute-start | bytes 1179656 | tf_op jit(solution)/shard_map/ppermute | solution.py:748
  27.3 16.9 %copy-start.1 = (bf16[4,80,1024]{2,1,0:T(8,128)(2,1)S(1)}, bf16[4,80,1024]{2,1,0:T(8,128)(2,1)}, u32[]{:S(2)}) copy-start(bf16[4,80,1024]{2,1,0:T(8,128)(2,1)} %get-tuple-element.44) | copy-start | bytes 1966084
  27.3 27.0 %copy-start = (bf16[1,128,4,1024]{3,2,1,0:T(4,128)(2,1)S(1)}, bf16[1,128,4,1024]{3,2,1,0:T(4,128)(2,1)}, u32[]{:S(2)}) copy-start(bf16[1,128,4,1024]{3,2,1,0:T(4,128)(2,1)} %param.10) | copy-start | bytes 3145732
  27.3 31.6 %collective-permute-start.2 = (bf16[4,80,1024]{2,1,0:T(8,128)(2,1)}, bf16[4,80,1024]{2,1,0:T(8,128)(2,1)S(1)}, u32[]{:S(2)}, u32[]{:S(2)}) collective-permute-start(bf16[4,80,1024]{2,1,0:T(8,128)(2,1)} %get-tuple-element.44), channel_id=1, source_target_pairs={{32,24},{64,56},{96,88},{128,120},{160,152},{192,184},{224,216},{3... | collective-permute-start | bytes 1966088 | tf_op jit(solution)/shard_map/ppermute | solution.py:749
  44.2 14.8 %copy-start.13 = (bf16[4,48,1024]{2,1,0:T(8,128)(2,1)}, bf16[4,48,1024]{2,1,0:T(8,128)(2,1)S(1)}, u32[]{:S(2)}) copy-start(bf16[4,48,1024]{2,1,0:T(8,128)(2,1)S(1)} %collective-permute-done.near1) | copy-start | bytes 1179652
  44.2 25.4 %collective-permute-start.1 = (bf16[4,80,1024]{2,1,0:T(8,128)(2,1)S(1)}, bf16[4,80,1024]{2,1,0:T(8,128)(2,1)S(1)}, u32[]{:S(2)}, u32[]{:S(2)}) collective-permute-start(bf16[4,80,1024]{2,1,0:T(8,128)(2,1)S(1)} %copy-done.1), channel_id=1, source_target_pairs={{8,0},{16,8},{24,16},{40,32},{48,40},{56,48},{72,64},{80,72},{88,8... | collective-permute-start | bytes 1966088 | tf_op jit(solution)/shard_map/ppermute | solution.py:754
  45.5 10.8 %collective-permute-start.4 = (bf16[128,1536]{1,0:T(8,128)(2,1)}, bf16[128,1536]{1,0:T(8,128)(2,1)}, u32[]{:S(2)}, u32[]{:S(2)}) collective-permute-start(bf16[128,1536]{1,0:T(8,128)(2,1)} %get-tuple-element.46.refs_0_), channel_id=1, source_target_pairs={{0,1},{1,0},{2,3},{3,2},{4,5},{5,4},{6,7},{7,6},{8,9},{9,8},{10,11... | collective-permute-start | bytes 1179656 | tf_op jit(solution)/shard_map/ppermute | solution.py:738
  45.6 10.7 %collective-permute-start.5 = (bf16[128,1536]{1,0:T(8,128)(2,1)}, bf16[128,1536]{1,0:T(8,128)(2,1)}, u32[]{:S(2)}, u32[]{:S(2)}) collective-permute-start(bf16[128,1536]{1,0:T(8,128)(2,1)} %get-tuple-element.47.refs_1_), channel_id=1, source_target_pairs={{0,1},{1,0},{2,3},{3,2},{4,5},{5,4},{6,7},{7,6},{8,9},{9,8},{10,11... | collective-permute-start | bytes 1179656 | tf_op jit(solution)/shard_map/ppermute | solution.py:738
  46.1 23.5 %collective-permute-start.3 = (bf16[4,48,1024]{2,1,0:T(8,128)(2,1)S(1)}, bf16[4,48,1024]{2,1,0:T(8,128)(2,1)}, u32[]{:S(2)}, u32[]{:S(2)}) collective-permute-start(bf16[4,48,1024]{2,1,0:T(8,128)(2,1)S(1)} %collective-permute-done.near1), channel_id=1, source_target_pairs={{56,24},{88,56},{120,88},{152,120},{184,152},{216,184},{248,216},{... | collective-permute-start | bytes 1179656 | tf_op jit(solution)/shard_map/ppermute | solution.py:753
  56.3 22.1 %collective-permute-start.6 = (bf16[128,2560]{1,0:T(8,128)(2,1)}, bf16[128,2560]{1,0:T(8,128)(2,1)S(1)}, u32[]{:S(2)}, u32[]{:S(2)}) collective-permute-start(bf16[128,2560]{1,0:T(8,128)(2,1)} %get-tuple-element.50.refs_0_), channel_id=1, source_target_pairs={{0,1},{1,0},{2,3},{3,2},{4,5},{5,4},{6,7},{7,6},{8,9},{9,8},{10,11... | collective-permute-start | bytes 1966088 | tf_op jit(solution)/shard_map/ppermute | solution.py:738
  58.9 10.7 %copy-start.6 = (bf16[4,80,1024]{2,1,0:T(8,128)(2,1)}, bf16[4,80,1024]{2,1,0:T(8,128)(2,1)S(1)}, u32[]{:S(2)}) copy-start(bf16[4,80,1024]{2,1,0:T(8,128)(2,1)S(1)} %collective-permute-done.2.far0) | copy-start | bytes 1966084
  69.6 0.8 copy-start.7
  70.4 7.9 %copy-start.4 = (bf16[4,48,1024]{2,1,0:T(8,128)(2,1)S(1)}, bf16[4,48,1024]{2,1,0:T(8,128)(2,1)}, u32[]{:S(2)}) copy-start(bf16[4,48,1024]{2,1,0:T(8,128)(2,1)} %get-tuple-element.42) | copy-start | bytes 1179652
  78.2 2.4 %collective-permute-start.7 = (bf16[128,2560]{1,0:T(8,128)(2,1)}, bf16[128,2560]{1,0:T(8,128)(2,1)S(1)}, u32[]{:S(2)}, u32[]{:S(2)}) collective-permute-start(bf16[128,2560]{1,0:T(8,128)(2,1)} %attention_tick.1.refs_1_.right), channel_id=1, source_target_pairs={{0,1},{1,0},{2,3},{3,2},{4,5},{5,4},{6,7},{7,6},{8,9},{9,8},{10,11... | collective-permute-start | bytes 1966088 | tf_op jit(solution)/shard_map/ppermute | solution.py:738
  78.4 2.2 %copy-start.8 = (bf16[128,2560]{1,0:T(8,128)(2,1)}, bf16[128,2560]{1,0:T(8,128)(2,1)S(1)}, u32[]{:S(2)}) copy-start(bf16[128,2560]{1,0:T(8,128)(2,1)S(1)} %collective-permute-done.6.refs_2_) | copy-start | bytes 1966084
  80.6 0.9 copy-start.9
  86.1 48.5 %collective-permute-start.9 = (bf16[128,2048]{1,0:T(8,128)(2,1)}, bf16[128,2048]{1,0:T(8,128)(2,1)S(1)}, u32[]{:S(2)}, u32[]{:S(2)}) collective-permute-start(bf16[128,2048]{1,0:T(8,128)(2,1)} %get-tuple-element.56), channel_id=1, source_target_pairs={{2,4},{3,5},{4,2},{5,3},{10,12},{11,13},{12,10},{13,11},{18,20},{1... | collective-permute-start | bytes 1572872 | tf_op jit(solution)/shard_map/ppermute | solution.py:742
  86.8 19.9 %collective-permute-start.8 = (bf16[128,2048]{1,0:T(8,128)(2,1)}, bf16[128,2048]{1,0:T(8,128)(2,1)S(1)}, u32[]{:S(2)}, u32[]{:S(2)}) collective-permute-start(bf16[128,2048]{1,0:T(8,128)(2,1)} %get-tuple-element.56), channel_id=1, source_target_pairs={{0,2},{1,3},{6,4},{7,5},{8,10},{9,11},{14,12},{15,13},{16,18},{17,... | collective-permute-start | bytes 1572872 | tf_op jit(solution)/shard_map/ppermute | solution.py:742
  93.3 41.3 %collective-permute-start.10 = (bf16[128,2048]{1,0:T(8,128)(2,1)}, bf16[128,2048]{1,0:T(8,128)(2,1)S(1)}, u32[]{:S(2)}, u32[]{:S(2)}) collective-permute-start(bf16[128,2048]{1,0:T(8,128)(2,1)} %get-tuple-element.71), channel_id=1, source_target_pairs={{0,2},{1,3},{2,0},{3,1},{4,6},{5,7},{6,4},{7,5},{8,10},{9,11},{10,... | collective-permute-start | bytes 1572872 | tf_op jit(solution)/shard_map/ppermute | solution.py:742
  93.4 41.2 %collective-permute-start.11 = (bf16[128,2048]{1,0:T(8,128)(2,1)}, bf16[128,2048]{1,0:T(8,128)(2,1)S(1)}, u32[]{:S(2)}, u32[]{:S(2)}) collective-permute-start(bf16[128,2048]{1,0:T(8,128)(2,1)} %get-tuple-element.55), channel_id=1, source_target_pairs={{0,4},{1,5},{6,2},{7,3},{8,12},{9,13},{14,10},{15,11},{16,20},{17,... | collective-permute-start | bytes 1572872 | tf_op jit(solution)/shard_map/ppermute | solution.py:742
  96.8 9.9 %copy-start.2 = (bf16[128,2048]{1,0:T(8,128)(2,1)S(1)}, bf16[128,2048]{1,0:T(8,128)(2,1)}, u32[]{:S(2)}) copy-start(bf16[128,2048]{1,0:T(8,128)(2,1)} %get-tuple-element.55) | copy-start | bytes 1572868
  106.9 5.5 %copy-start.3 = (bf16[128,2048]{1,0:T(8,128)(2,1)}, bf16[128,2048]{1,0:T(8,128)(2,1)S(1)}, u32[]{:S(2)}) copy-start(bf16[128,2048]{1,0:T(8,128)(2,1)S(1)} %add_convert_fusion.after) | copy-start | bytes 1572868
  106.9 25.4 %all-to-all-start = ((bf16[8,32,512]{2,1,0:T(8,128)(2,1)}), bf16[8,32,512]{2,1,0:T(8,128)(2,1)S(1)}, u32[]{:S(2)}, u32[]{:S(2)}) async-start(bf16[8,32,512]{2,1,0:T(8,128)(2,1)} %get-tuple-element.72), calls=%async_computation | async-start | bytes 524288 | tf_op jit(solution)/shard_map/all_to_all | solution.py:772
  111.1 32.3 %collective-permute-start.12 = (bf16[128,2048]{1,0:T(8,128)(2,1)S(1)}, bf16[128,2048]{1,0:T(8,128)(2,1)}, u32[]{:S(2)}, u32[]{:S(2)}) collective-permute-start(bf16[128,2048]{1,0:T(8,128)(2,1)S(1)} %add_convert_fusion.after), channel_id=1, source_target_pairs={{2,6},{3,7},{4,0},{5,1},{10,14},{11,15},{12,8},{13,9},{18,22},{19,... | collective-permute-start | bytes 1572872 | tf_op jit(solution)/shard_map/ppermute | solution.py:742
  132.3 0.7 copy-start.5
  134.6 8.8 %copy-start.11 = (bf16[128,2048]{1,0:T(8,128)(2,1)}, bf16[128,2048]{1,0:T(8,128)(2,1)S(1)}, u32[]{:S(2)}) copy-start(bf16[128,2048]{1,0:T(8,128)(2,1)S(1)} %collective-permute-done.10.refs_2_) | copy-start | bytes 1572868
  134.7 8.7 %copy-start.12 = (bf16[128,2048]{1,0:T(8,128)(2,1)}, bf16[128,2048]{1,0:T(8,128)(2,1)S(1)}, u32[]{:S(2)}) copy-start(bf16[128,2048]{1,0:T(8,128)(2,1)S(1)} %collective-permute-done.11.refs_3_) | copy-start | bytes 1572868
  134.7 8.7 %copy-start.10 = (bf16[128,2048]{1,0:T(8,128)(2,1)}, bf16[128,2048]{1,0:T(8,128)(2,1)S(1)}, u32[]{:S(2)}) copy-start(bf16[128,2048]{1,0:T(8,128)(2,1)S(1)} %collective-permute-done.9.refs_1_) | copy-start | bytes 1572868

commit v3 on v2

--- a/solution.py
+++ b/solution.py
@@ -769,6 +769,7 @@
     both = (sends[1].astype(F32) + by_way.astype(F32)).astype(BF16)
     grads = [own, middle, beside, outer, along(both, (1, 3), (2, 0))]
     dx1 = output_tick(saved["x"], adjoint, saved["coef"], saved["bhl"], dj, back, both)
+    parts, dx1 = lax.optimization_barrier((parts, dx1))
     parts = lax.all_to_all(parts, "dp", 0, 0)
     grad_map, grad_gain = finish_map(parts, n)
     grad_qkv, grad_out = finish_terms(grads, grad_map)

time: 147 us -> 160 us (1.088)
  waiting for transfers between devices: 34.7 us -> 45.7 us
  starting transfers between devices: 30.4 us -> 33.1 us
    ppermute x5, waiting for transfers between devices: 8.72 us -> 29.5 us  [along(): return lax.ppermute(value, 'dp', route)]
    all_to_all x1, waiting for transfers between devices: 9.95 us -> 0.01 us  [shards(): parts = lax.all_to_all(parts, 'dp', 0, 0)]
    unnamed x30 -> x26, local copies, waits for them, and re-layouts: 6.65 us -> 6.66 us
  transfers between devices with their start and end apart: 14 -> 14, of which waited for: 5 -> 7; matrix products, arithmetic and copies ran while one was open for 4% -> 3% of each run, Pallas kernels for 27% -> 21%
where the time goes in v3:
time: 160 us
  Pallas kernels  71.4 us (45%)
  waiting for transfers between devices  45.7 us (29%)
  starting transfers between devices  33.1 us (21%)
  local copies, waits for them, and re-layouts  7.32 us (5%)
    pallas_call x9, Pallas kernels, call(): pl.pallas_call(body, out_shape=outs, in_specs=specs or [VMEM] * len(args)...  71.4 us
    ppermute x5, waiting for transfers between devices, along(): return lax.ppermute(value, 'dp', route)  29.5 us
    ppermute x5, starting transfers between devices, along(): return lax.ppermute(value, 'dp', route)  13.5 us
    ppermute x1, waiting for transfers between devices, shards(): far = lax.ppermute(coming, 'section', [(s + RUN - 1, s - 1) for s in cross])  10.6 us
    ppermute x1, starting transfers between devices, shards(): far = lax.ppermute(coming, 'section', [(s + RUN - 1, s - 1) for s in cross])  8.22 us
    unnamed x26, local copies, waits for them, and re-layouts  6.66 us
    all_to_all x1, starting transfers between devices, shards(): parts = lax.all_to_all(parts, 'dp', 0, 0)  5.27 us
    ppermute x1, waiting for transfers between devices, shards(): lax.ppermute(first['dx_back'], 'section', near + [(s, s + RUN - 1) for s...  3.21 us
  transfers between devices with their start and end apart: 14, of which 7 were waited for; matrix products, arithmetic and copies ran while one was open for 3% of the time, Pallas kernels for 21%

profile of v3, /device:TPU:30, one launch (start us, length us, event | category | flops | bytes accessed | tf_op | source)
XLA Modules:
  0.0 159.6 jit_solution(3079832874411468448)
XLA Ops:
  0.6 24.0 %whole_tick.1 = (bf16[4,80,1024]{2,1,0:T(8,128)(2,1)}, bf16[4,48,1024]{2,1,0:T(8,128)(2,1)}, bf16[128,2560]{1,0:T(8,128)(2,1)}, bf16[128,1536]{1,0:T(8,128)(2,1)...) custom-call(bf16[2,128,4,1024]{3,2,1,0:T(4,128)(2,1)} %bitcast.36, bf16[128,4,1024]{2,1,0:T(4,128)(2,1)} %bitcast.49, ...), custom_call_target="tpu_custom_call" | custom-call | flops 20000000000 | bytes 40000000 | tf_op jit(solution)/shard_map/whole_tick/pallas_call | solution.py:352
  24.6 2.7 %collective-permute-start.2 = (bf16[4,48,1024]{2,1,0:T(8,128)(2,1)}, bf16[4,48,1024]{2,1,0:T(8,128)(2,1)S(1)}, u32[]{:S(2)}, u32[]{:S(2)}) collective-permute-start(bf16[4,48,1024]{2,1,0:T(8,128)(2,1)} %get-tuple-element.44), channel_id=1, source_target_pairs={{8,0},{16,8},{24,16},{40,32},{48,40},{56,48},{72,64},{80,72},{88,8... | collective-permute-start | bytes 1179656 | tf_op jit(solution)/shard_map/ppermute | solution.py:748
  27.3 0.0 copy-start.2
  27.3 0.0 copy-start
  27.3 1.4 collective-permute-start.4
  28.8 12.2 %forward_tick.1 = (f32[32,128]{1,0:T(8,128)}, f32[20,13,8,128]{3,2,1,0:T(8,128)}, f32[128,128]{1,0:T(8,128)}, f32[128,1024]{1,0:T(8,128)}, f32[128,128]{1,0:T(8,...) custom-call(bf16[2,128,4,1024]{3,2,1,0:T(4,128)(2,1)} %bitcast.37, ...), custom_call_target="tpu_custom_call" | custom-call | flops 1000000000 | bytes 2000000 | tf_op jit(solution)/shard_map/forward_tick/pallas_call | solution.py:352
  41.0 3.2 %collective-permute-done.2.near1 = bf16[4,48,1024]{2,1,0:T(8,128)(2,1)S(1)} collective-permute-done((bf16[4,48,1024]{2,1,0:T(8,128)(2,1)}, bf16[4,48,1024]{2,1,0:T(8,128)(2,1)S(1)}, u32[]{:S(2)}, u32[]{:S(2)}) %collective-permute-start.2) | collective-permute-done | bytes 393248 | tf_op jit(solution)/shard_map/ppermute | solution.py:748
  44.2 0.0 copy-start.11
  44.2 0.0 copy-done.2
  44.2 1.3 collective-permute-start.3
  45.5 0.1 collective-permute-start
  45.6 0.5 collective-permute-start.1
  46.1 8.2 %collective-permute-start.5 = (bf16[4,48,1024]{2,1,0:T(8,128)(2,1)S(1)}, bf16[4,48,1024]{2,1,0:T(8,128)(2,1)}, u32[]{:S(2)}, u32[]{:S(2)}) collective-permute-start(bf16[4,48,1024]{2,1,0:T(8,128)(2,1)S(1)} %collective-permute-done.2.near1), channel_id=1, source_target_pairs={{56,24},{88,56},{120,88},{152,120},{184,152},{216,184},{248,216},{... | collective-permute-start | bytes 1179656 | tf_op jit(solution)/shard_map/ppermute | solution.py:753
  54.4 0.0 copy-done
  54.4 1.3 copy.16
  55.6 0.7 stack.33.place
  56.3 0.0 collective-permute-done.refs_2_
  56.3 0.0 collective-permute-start.6
  56.3 0.0 collective-permute-done.1.refs_3_
  56.3 2.6 %turned_factors.1 = (bf16[512,512]{1,0:T(8,128)(2,1)}, bf16[256,512]{1,0:T(8,128)(2,1)}) custom-call(s32[5]{0:T(128)} %stack.33.place, bf16[128,1536]{1,0:T(8,128)(2,1)} %get-tuple-element.45.refs_0_, bf16[128,1536]{1,0:T(8,128)(2,1)} %get-tuple-element.46.refs_1_, bf16[128,1536]{1,0:T(8,128)(2,1)} %collective-permute-done.refs_2_, ...), custom_call_target="tpu_custom_call" | custom-call | flops 1000000000 | bytes 2000000 | tf_op jit(solution)/shard_map/turned_factors/pallas_call | solution.py:352
  58.9 0.0 copy-done.11
  58.9 0.0 collective-permute-done.4.far0
  58.9 0.0 copy-start.7
  59.0 10.6 %collective-permute-done.5.far1 = bf16[4,48,1024]{2,1,0:T(8,128)(2,1)} collective-permute-done((bf16[4,48,1024]{2,1,0:T(8,128)(2,1)S(1)}, bf16[4,48,1024]{2,1,0:T(8,128)(2,1)}, u32[]{:S(2)}, u32[]{:S(2)}) %collective-permute-start.5) | collective-permute-done | bytes 393248 | tf_op jit(solution)/shard_map/ppermute | solution.py:753
  69.6 0.0 collective-permute-done.3.near0
  69.6 0.0 copy-start.8
  69.6 0.0 copy-done.7
  69.6 0.8 copy-done.8
  70.4 7.7 %attention_tick.1.refs_1_.right = bf16[128,2560]{1,0:T(8,128)(2,1)} custom-call(s32[1]{0:T(128)} %bitcast.15.where, bf16[4,80,1024]{2,1,0:T(8,128)(2,1)} %copy-done.8, bf16[4,48,1024]{2,1,0:T(8,128)(2,1)} %copy-done.11, bf16[4,80,1024]{2,1,0:T(8,128)(2,1)} %copy-done.7, bf16[4,48,1024]{2,1,0:T(8,128)(2,1)} %collective-permute-done.5.far1, ...), custom_call_target="tpu_custom_call" | custom-call | flops 5000000000 | bytes 10000000 | tf_op jit(solution)/shard_map/attention_tick/pallas_call | solution.py:352
  78.2 0.1 collective-permute-start.7
  78.3 0.0 collective-permute-done.6.refs_2_
  78.3 0.0 copy-start.9
  78.3 2.3 %collective-permute-done.7.refs_3_ = bf16[128,2560]{1,0:T(8,128)(2,1)S(1)} collective-permute-done((bf16[128,2560]{1,0:T(8,128)(2,1)}, bf16[128,2560]{1,0:T(8,128)(2,1)S(1)}, u32[]{:S(2)}, u32[]{:S(2)}) %collective-permute-start.7) | collective-permute-done | bytes 655392 | tf_op jit(solution)/shard_map/ppermute | solution.py:738
  80.5 0.0 copy-start.10
  80.5 0.0 copy-done.9
  80.6 0.9 copy-done.10
  81.4 4.7 %terms.1 = (f32[128,2048]{1,0:T(8,128)}, bf16[128,2048]{1,0:T(8,128)(2,1)}, bf16[128,2048]{1,0:T(8,128)(2,1)}, bf16[128,2048]{1,0:T(8,128)(2,1)}) custom-call(bf16[512,512]{1,0:T(8,128)(2,1)} %get-tuple-element.47.after.left, bf16[256,512]{1,0:T(8,128)(2,1)} %get-tuple-element.48.small, bf16[128,2560]{1,0:T(8,128)(2,1)} %get-tuple-element.49.refs_0_, ...), custom_call_target="tpu_custom_call" | custom-call | flops 4000000000 | bytes 8000000 | tf_op jit(solution)/shard_map/terms/pallas_call | solution.py:352
  86.1 3.2 %collective-permute-start.8 = (bf16[128,2048]{1,0:T(8,128)(2,1)}, bf16[128,2048]{1,0:T(8,128)(2,1)S(1)}, u32[]{:S(2)}, u32[]{:S(2)}) collective-permute-start(bf16[128,2048]{1,0:T(8,128)(2,1)} %get-tuple-element.57), channel_id=1, source_target_pairs={{0,2},{1,3},{6,4},{7,5},{8,10},{9,11},{14,12},{15,13},{16,18},{17,... | collective-permute-start | bytes 1572872 | tf_op jit(solution)/shard_map/ppermute | solution.py:742
  89.3 0.0 copy-start.3
  89.3 9.9 %stream_tick.1 = (bf16[8,32,512]{2,1,0:T(8,128)(2,1)}, f32[128,1024]{1,0:T(8,128)}, f32[128,128]{1,0:T(8,128)}) custom-call(s32[1]{0:T(128)} %bitcast.15.where, bf16[4,80,1024]{2,1,0:T(8,128)(2,1)} %copy-done.8, bf16[4,48,1024]{2,1,0:T(8,128)(2,1)} %copy-done.11, bf16[4,80,1024]{2,1,0:T(8,128)(2,1)} %copy-done.7, ...), custom_call_target="tpu_custom_call" | custom-call | flops 6000000000 | bytes 12000000 | tf_op jit(solution)/shard_map/stream_tick/pallas_call | solution.py:352
  99.2 1.8 %collective-permute-done.8 = bf16[128,2048]{1,0:T(8,128)(2,1)S(1)} collective-permute-done((bf16[128,2048]{1,0:T(8,128)(2,1)}, bf16[128,2048]{1,0:T(8,128)(2,1)S(1)}, u32[]{:S(2)}, u32[]{:S(2)}) %collective-permute-start.8) | collective-permute-done | bytes 524320 | tf_op jit(solution)/shard_map/ppermute | solution.py:742
  101.1 0.0 copy-done.3
  101.1 1.0 add_convert_fusion.after
  102.1 5.7 %output_tick.1 = bf16[4,128,1024]{2,1,0:T(8,128)(2,1)} custom-call(s32[1]{0:T(128)} %bitcast.15.where, bf16[4,80,1024]{2,1,0:T(8,128)(2,1)} %copy-done.8, bf16[4,48,1024]{2,1,0:T(8,128)(2,1)} %copy-done.11, bf16[4,80,1024]{2,1,0:T(8,128)(2,1)} %copy-done.7, bf16[4,48,1024]{2,1,0:T(8,128)(2,1)} %collective-permute-done.5.far1, ...), custom_call_target="tpu_custom_call" | custom-call | flops 5000000000 | bytes 10000000 | tf_op jit(solution)/shard_map/output_tick/pallas_call | solution.py:352
  107.8 0.0 copy-start.1
  107.8 5.3 %all-to-all-start = ((bf16[8,32,512]{2,1,0:T(8,128)(2,1)}), bf16[8,32,512]{2,1,0:T(8,128)(2,1)S(1)}, u32[]{:S(2)}, u32[]{:S(2)}) async-start(bf16[8,32,512]{2,1,0:T(8,128)(2,1)} %get-tuple-element.76), calls=%async_computation | async-start | bytes 524288 | tf_op jit(solution)/shard_map/all_to_all | solution.py:773
  113.1 2.0 %collective-permute-start.10 = (bf16[128,2048]{1,0:T(8,128)(2,1)}, bf16[128,2048]{1,0:T(8,128)(2,1)}, u32[]{:S(2)}, u32[]{:S(2)}) collective-permute-start(bf16[128,2048]{1,0:T(8,128)(2,1)} %get-tuple-element.75), channel_id=1, source_target_pairs={{0,2},{1,3},{2,0},{3,1},{4,6},{5,7},{6,4},{7,5},{8,10},{9,11},{10,... | collective-permute-start | bytes 1572872 | tf_op jit(solution)/shard_map/ppermute | solution.py:742
  115.1 1.4 collective-permute-start.9
  116.5 5.5 %collective-permute-start.11 = (bf16[128,2048]{1,0:T(8,128)(2,1)S(1)}, bf16[128,2048]{1,0:T(8,128)(2,1)}, u32[]{:S(2)}, u32[]{:S(2)}) collective-permute-start(bf16[128,2048]{1,0:T(8,128)(2,1)S(1)} %copy-done.3), channel_id=1, source_target_pairs={{0,4},{1,5},{6,2},{7,3},{8,12},{9,13},{14,10},{15,11},{16,20},{17,... | collective-permute-start | bytes 1572872 | tf_op jit(solution)/shard_map/ppermute | solution.py:742
  122.1 0.0 copy-done.4
  122.1 1.3 collective-permute-start.12
  123.4 0.0 copy-done.5
  123.4 0.1 maximum_bitcast_fusion.1
  123.5 0.0 copy-done.1
  123.5 0.2 maximum_bitcast_fusion
  123.7 2.9 %copy.14 = bf16[1,2,128,4,1024]{4,3,2,1,0:T(4,128)(2,1)} copy(bf16[1,2,128,4,1024]{4,2,3,1,0:T(8,128)(2,1)S(1)} %maximum_bitcast_fusion) | data formatting | bytes 4194304
  126.6 0.0 all-to-all-done.parts
  126.6 0.7 copy-done.6
  127.3 1.6 %finish_map.1 = (f32[24,512]{1,0:T(8,128)}, f32[1,128]{1,0:T(1,128)}) custom-call(bf16[8,32,512]{2,1,0:T(8,128)(2,1)} %copy-done.6), custom_call_target="tpu_custom_call" | custom-call | flops 1000000000 | bytes 2000000 | tf_op jit(solution)/shard_map/finish_map/pallas_call | solution.py:352
  128.9 2.9 %collective-permute-done.10.refs_2_ = bf16[128,2048]{1,0:T(8,128)(2,1)} collective-permute-done((bf16[128,2048]{1,0:T(8,128)(2,1)}, bf16[128,2048]{1,0:T(8,128)(2,1)}, u32[]{:S(2)}, u32[]{:S(2)}) %collective-permute-start.10) | collective-permute-done | bytes 524320 | tf_op jit(solution)/shard_map/ppermute | solution.py:742
  131.8 0.0 collective-permute-done.9.refs_1_
  131.8 9.0 %collective-permute-done.11.refs_3_ = bf16[128,2048]{1,0:T(8,128)(2,1)} collective-permute-done((bf16[128,2048]{1,0:T(8,128)(2,1)S(1)}, bf16[128,2048]{1,0:T(8,128)(2,1)}, u32[]{:S(2)}, u32[]{:S(2)}) %collective-permute-start.11) | collective-permute-done | bytes 524320 | tf_op jit(solution)/shard_map/ppermute | solution.py:742
  140.9 15.7 %collective-permute-done.12.refs_4_ = bf16[128,2048]{1,0:T(8,128)(2,1)} collective-permute-done((bf16[128,2048]{1,0:T(8,128)(2,1)S(1)}, bf16[128,2048]{1,0:T(8,128)(2,1)}, u32[]{:S(2)}, u32[]{:S(2)}) %collective-permute-start.12) | collective-permute-done | bytes 524320 | tf_op jit(solution)/shard_map/ppermute | solution.py:742
  156.6 3.0 %finish_terms.1 = (f32[128,1536]{1,0:T(8,128)}, f32[64,1024]{1,0:T(8,128)}) custom-call(f32[128,2048]{1,0:T(8,128)} %get-tuple-element.58.after.refs_0_, bf16[128,2048]{1,0:T(8,128)(2,1)} %collective-permute-done.9.refs_1_, bf16[128,2048]{1,0:T(8,128)(2,1)} %collective-permute-done.10.refs_2_, bf16[128,2048]{1,0:T(8,128)(2,1)} %collective-permute-done.11.refs_3_, ...), custom_call_target="tpu_custom_call" | custom-call | flops 2000000000 | bytes 4000000 | tf_op jit(solution)/shard_map/finish_terms/pallas_call | solution.py:352
  (3 shorter events, 0.0 us)
Async XLA Ops:
  24.6 19.5 %collective-permute-start.2 = (bf16[4,48,1024]{2,1,0:T(8,128)(2,1)}, bf16[4,48,1024]{2,1,0:T(8,128)(2,1)S(1)}, u32[]{:S(2)}, u32[]{:S(2)}) collective-permute-start(bf16[4,48,1024]{2,1,0:T(8,128)(2,1)} %get-tuple-element.44), channel_id=1, source_target_pairs={{8,0},{16,8},{24,16},{40,32},{48,40},{56,48},{72,64},{80,72},{88,8... | collective-permute-start | bytes 1179656 | tf_op jit(solution)/shard_map/ppermute | solution.py:748
  27.3 16.9 %copy-start.2 = (bf16[4,80,1024]{2,1,0:T(8,128)(2,1)S(1)}, bf16[4,80,1024]{2,1,0:T(8,128)(2,1)}, u32[]{:S(2)}) copy-start(bf16[4,80,1024]{2,1,0:T(8,128)(2,1)} %get-tuple-element.51) | copy-start | bytes 1966084
  27.3 27.0 %copy-start = (bf16[1,128,4,1024]{3,2,1,0:T(4,128)(2,1)S(1)}, bf16[1,128,4,1024]{3,2,1,0:T(4,128)(2,1)}, u32[]{:S(2)}) copy-start(bf16[1,128,4,1024]{3,2,1,0:T(4,128)(2,1)} %param.10) | copy-start | bytes 3145732
  27.3 31.6 %collective-permute-start.4 = (bf16[4,80,1024]{2,1,0:T(8,128)(2,1)}, bf16[4,80,1024]{2,1,0:T(8,128)(2,1)S(1)}, u32[]{:S(2)}, u32[]{:S(2)}) collective-permute-start(bf16[4,80,1024]{2,1,0:T(8,128)(2,1)} %get-tuple-element.51), channel_id=1, source_target_pairs={{32,24},{64,56},{96,88},{128,120},{160,152},{192,184},{224,216},{3... | collective-permute-start | bytes 1966088 | tf_op jit(solution)/shard_map/ppermute | solution.py:749
  44.2 14.8 %copy-start.11 = (bf16[4,48,1024]{2,1,0:T(8,128)(2,1)}, bf16[4,48,1024]{2,1,0:T(8,128)(2,1)S(1)}, u32[]{:S(2)}) copy-start(bf16[4,48,1024]{2,1,0:T(8,128)(2,1)S(1)} %collective-permute-done.2.near1) | copy-start | bytes 1179652
  44.2 25.4 %collective-permute-start.3 = (bf16[4,80,1024]{2,1,0:T(8,128)(2,1)S(1)}, bf16[4,80,1024]{2,1,0:T(8,128)(2,1)S(1)}, u32[]{:S(2)}, u32[]{:S(2)}) collective-permute-start(bf16[4,80,1024]{2,1,0:T(8,128)(2,1)S(1)} %copy-done.2), channel_id=1, source_target_pairs={{8,0},{16,8},{24,16},{40,32},{48,40},{56,48},{72,64},{80,72},{88,8... | collective-permute-start | bytes 1966088 | tf_op jit(solution)/shard_map/ppermute | solution.py:754
  45.5 10.8 %collective-permute-start = (bf16[128,1536]{1,0:T(8,128)(2,1)}, bf16[128,1536]{1,0:T(8,128)(2,1)}, u32[]{:S(2)}, u32[]{:S(2)}) collective-permute-start(bf16[128,1536]{1,0:T(8,128)(2,1)} %get-tuple-element.45.refs_0_), channel_id=1, source_target_pairs={{0,1},{1,0},{2,3},{3,2},{4,5},{5,4},{6,7},{7,6},{8,9},{9,8},{10,11... | collective-permute-start | bytes 1179656 | tf_op jit(solution)/shard_map/ppermute | solution.py:738
  45.6 10.7 %collective-permute-start.1 = (bf16[128,1536]{1,0:T(8,128)(2,1)}, bf16[128,1536]{1,0:T(8,128)(2,1)}, u32[]{:S(2)}, u32[]{:S(2)}) collective-permute-start(bf16[128,1536]{1,0:T(8,128)(2,1)} %get-tuple-element.46.refs_1_), channel_id=1, source_target_pairs={{0,1},{1,0},{2,3},{3,2},{4,5},{5,4},{6,7},{7,6},{8,9},{9,8},{10,11... | collective-permute-start | bytes 1179656 | tf_op jit(solution)/shard_map/ppermute | solution.py:738
  46.1 23.5 %collective-permute-start.5 = (bf16[4,48,1024]{2,1,0:T(8,128)(2,1)S(1)}, bf16[4,48,1024]{2,1,0:T(8,128)(2,1)}, u32[]{:S(2)}, u32[]{:S(2)}) collective-permute-start(bf16[4,48,1024]{2,1,0:T(8,128)(2,1)S(1)} %collective-permute-done.2.near1), channel_id=1, source_target_pairs={{56,24},{88,56},{120,88},{152,120},{184,152},{216,184},{248,216},{... | collective-permute-start | bytes 1179656 | tf_op jit(solution)/shard_map/ppermute | solution.py:753
  56.3 21.9 %collective-permute-start.6 = (bf16[128,2560]{1,0:T(8,128)(2,1)}, bf16[128,2560]{1,0:T(8,128)(2,1)S(1)}, u32[]{:S(2)}, u32[]{:S(2)}) collective-permute-start(bf16[128,2560]{1,0:T(8,128)(2,1)} %get-tuple-element.49.refs_0_), channel_id=1, source_target_pairs={{0,1},{1,0},{2,3},{3,2},{4,5},{5,4},{6,7},{7,6},{8,9},{9,8},{10,11... | collective-permute-start | bytes 1966088 | tf_op jit(solution)/shard_map/ppermute | solution.py:738
  58.9 10.7 %copy-start.7 = (bf16[4,80,1024]{2,1,0:T(8,128)(2,1)}, bf16[4,80,1024]{2,1,0:T(8,128)(2,1)S(1)}, u32[]{:S(2)}) copy-start(bf16[4,80,1024]{2,1,0:T(8,128)(2,1)S(1)} %collective-permute-done.4.far0) | copy-start | bytes 1966084
  69.6 0.8 copy-start.8
  78.2 2.4 %collective-permute-start.7 = (bf16[128,2560]{1,0:T(8,128)(2,1)}, bf16[128,2560]{1,0:T(8,128)(2,1)S(1)}, u32[]{:S(2)}, u32[]{:S(2)}) collective-permute-start(bf16[128,2560]{1,0:T(8,128)(2,1)} %attention_tick.1.refs_1_.right), channel_id=1, source_target_pairs={{0,1},{1,0},{2,3},{3,2},{4,5},{5,4},{6,7},{7,6},{8,9},{9,8},{10,11... | collective-permute-start | bytes 1966088 | tf_op jit(solution)/shard_map/ppermute | solution.py:738
  78.3 2.3 %copy-start.9 = (bf16[128,2560]{1,0:T(8,128)(2,1)}, bf16[128,2560]{1,0:T(8,128)(2,1)S(1)}, u32[]{:S(2)}) copy-start(bf16[128,2560]{1,0:T(8,128)(2,1)S(1)} %collective-permute-done.6.refs_2_) | copy-start | bytes 1966084
  80.5 0.9 copy-start.10
  86.1 15.0 %collective-permute-start.8 = (bf16[128,2048]{1,0:T(8,128)(2,1)}, bf16[128,2048]{1,0:T(8,128)(2,1)S(1)}, u32[]{:S(2)}, u32[]{:S(2)}) collective-permute-start(bf16[128,2048]{1,0:T(8,128)(2,1)} %get-tuple-element.57), channel_id=1, source_target_pairs={{0,2},{1,3},{6,4},{7,5},{8,10},{9,11},{14,12},{15,13},{16,18},{17,... | collective-permute-start | bytes 1572872 | tf_op jit(solution)/shard_map/ppermute | solution.py:742
  89.3 11.8 %copy-start.3 = (bf16[128,2048]{1,0:T(8,128)(2,1)S(1)}, bf16[128,2048]{1,0:T(8,128)(2,1)}, u32[]{:S(2)}) copy-start(bf16[128,2048]{1,0:T(8,128)(2,1)} %get-tuple-element.69) | copy-start | bytes 1572868
  102.0 20.0 %copy-start.4 = (bf16[128,2048]{1,0:T(8,128)(2,1)S(1)}, bf16[128,2048]{1,0:T(8,128)(2,1)}, u32[]{:S(2)}) copy-start(bf16[128,2048]{1,0:T(8,128)(2,1)} %add_convert_fusion.after) | copy-start | bytes 1572868
  102.1 21.3 %copy-start.5 = (bf16[4,48,1024]{2,1,0:T(8,128)(2,1)S(1)}, bf16[4,48,1024]{2,1,0:T(8,128)(2,1)}, u32[]{:S(2)}) copy-start(bf16[4,48,1024]{2,1,0:T(8,128)(2,1)} %get-tuple-element.44) | copy-start | bytes 1179652
  107.8 15.7 %copy-start.1 = (bf16[4,128,1024]{2,1,0:T(8,128)(2,1)S(1)}, bf16[4,128,1024]{2,1,0:T(8,128)(2,1)}, u32[]{:S(2)}) copy-start(bf16[4,128,1024]{2,1,0:T(8,128)(2,1)} %output_tick.1) | copy-start | bytes 3145732
  107.8 18.8 %all-to-all-start = ((bf16[8,32,512]{2,1,0:T(8,128)(2,1)}), bf16[8,32,512]{2,1,0:T(8,128)(2,1)S(1)}, u32[]{:S(2)}, u32[]{:S(2)}) async-start(bf16[8,32,512]{2,1,0:T(8,128)(2,1)} %get-tuple-element.76), calls=%async_computation | async-start | bytes 524288 | tf_op jit(solution)/shard_map/all_to_all | solution.py:773
  113.1 18.8 %collective-permute-start.10 = (bf16[128,2048]{1,0:T(8,128)(2,1)}, bf16[128,2048]{1,0:T(8,128)(2,1)}, u32[]{:S(2)}, u32[]{:S(2)}) collective-permute-start(bf16[128,2048]{1,0:T(8,128)(2,1)} %get-tuple-element.75), channel_id=1, source_target_pairs={{0,2},{1,3},{2,0},{3,1},{4,6},{5,7},{6,4},{7,5},{8,10},{9,11},{10,... | collective-permute-start | bytes 1572872 | tf_op jit(solution)/shard_map/ppermute | solution.py:742
  115.1 16.8 %collective-permute-start.9 = (bf16[128,2048]{1,0:T(8,128)(2,1)}, bf16[128,2048]{1,0:T(8,128)(2,1)}, u32[]{:S(2)}, u32[]{:S(2)}) collective-permute-start(bf16[128,2048]{1,0:T(8,128)(2,1)} %get-tuple-element.57), channel_id=1, source_target_pairs={{2,4},{3,5},{4,2},{5,3},{10,12},{11,13},{12,10},{13,11},{18,20},{1... | collective-permute-start | bytes 1572872 | tf_op jit(solution)/shard_map/ppermute | solution.py:742
  116.5 24.4 %collective-permute-start.11 = (bf16[128,2048]{1,0:T(8,128)(2,1)S(1)}, bf16[128,2048]{1,0:T(8,128)(2,1)}, u32[]{:S(2)}, u32[]{:S(2)}) collective-permute-start(bf16[128,2048]{1,0:T(8,128)(2,1)S(1)} %copy-done.3), channel_id=1, source_target_pairs={{0,4},{1,5},{6,2},{7,3},{8,12},{9,13},{14,10},{15,11},{16,20},{17,... | collective-permute-start | bytes 1572872 | tf_op jit(solution)/shard_map/ppermute | solution.py:742
  122.1 34.5 %collective-permute-start.12 = (bf16[128,2048]{1,0:T(8,128)(2,1)S(1)}, bf16[128,2048]{1,0:T(8,128)(2,1)}, u32[]{:S(2)}, u32[]{:S(2)}) collective-permute-start(bf16[128,2048]{1,0:T(8,128)(2,1)S(1)} %copy-done.4), channel_id=1, source_target_pairs={{2,6},{3,7},{4,0},{5,1},{10,14},{11,15},{12,8},{13,9},{18,22},{19,... | collective-permute-start | bytes 1572872 | tf_op jit(solution)/shard_map/ppermute | solution.py:742
  126.6 0.7 copy-start.6

commit v4 on v2

--- a/solution.py
+++ b/solution.py
@@ -20,6 +20,7 @@
 ROWS = 16
 RUN = 4
 FORWARD_COST = 1
+FINISH_COST = 100
 RIGHT = 3 * INNER + D
 LEFT = D + INNER
 FRONT = 80
@@ -672,11 +673,11 @@
     return own, sends
 
 
-def finish_terms(terms, after):
+def finish_terms(terms):
     few = INNER // (2 * STEPS)
 
     def body(*refs):
-        *others, _, grad_qkv, grad_out = refs[1:]
+        *others, grad_qkv, grad_out = refs[1:]
         total = refs[0][...]
         for other in others:
             total = total + other[...].astype(F32)
@@ -686,14 +687,13 @@
 
     rows = terms[0].shape[0]
     outs = [struct((rows, 3 * INNER), F32), struct((few, D), F32)]
-    specs = [VMEM] * len(terms) + [ANY]
-    return call(body, outs, [], (*terms, after), 2, "finish_terms", specs)
-
-
-def finish_map(parts, n):
+    return call(body, outs, [], terms, FINISH_COST, "finish_terms")
+
+
+def finish_map(parts, n, after):
     width = LANES * D // n
 
-    def body(parts, grad_map, grad_gain):
+    def body(parts, after, grad_map, grad_gain):
         total = parts[0].astype(F32)
         for d in range(1, n):
             total = total + parts[d].astype(F32)
@@ -704,9 +704,10 @@
         body,
         [struct((24, width), F32), struct((1, D // n), F32)],
         [],
-        (parts,),
+        (parts, after),
         1,
         "finish_map",
+        [VMEM, ANY],
     )
 
 
@@ -770,8 +771,8 @@
     grads = [own, middle, beside, outer, along(both, (1, 3), (2, 0))]
     dx1 = output_tick(saved["x"], adjoint, saved["coef"], saved["bhl"], dj, back, both)
     parts = lax.all_to_all(parts, "dp", 0, 0)
-    grad_map, grad_gain = finish_map(parts, n)
-    grad_qkv, grad_out = finish_terms(grads, grad_map)
+    grad_qkv, grad_out = finish_terms(grads)
+    grad_map, grad_gain = finish_map(parts, n, grad_qkv)
     dx0 = jnp.concatenate([first["dx_front"], first["dx_back"]], axis=1)
     sent = jnp.stack([jnp.transpose(dx0, (1, 0, 2)), jnp.transpose(dx1, (1, 0, 2))])[None]
     return (sent, grad_qkv[None], grad_out[None], grad_map.T[None], grad_gain)

time: 147 us -> 145 us (0.986)
  waiting for transfers between devices: 34.7 us -> 30 us
  starting transfers between devices: 30.4 us -> 33.2 us
    all_to_all x1, waiting for transfers between devices: 9.95 us -> 0.01 us  [shards(): parts = lax.all_to_all(parts, 'dp', 0, 0)]
    ppermute x5, waiting for transfers between devices: 8.72 us -> 14 us  [along(): return lax.ppermute(value, 'dp', route)]
    all_to_all x1, starting transfers between devices: 4.18 us -> 6.2 us  [shards(): parts = lax.all_to_all(parts, 'dp', 0, 0)]
    unnamed x30 -> x28, local copies, waits for them, and re-layouts: 6.65 us -> 6.64 us
  transfers between devices with their start and end apart: 14 -> 14, of which waited for: 5 -> 5; matrix products, arithmetic and copies ran while one was open for 4% -> 4% of each run, Pallas kernels for 27% -> 28%
where the time goes in v4:
time: 145 us; the launch traced here: 144 us
  Pallas kernels  71.4 us (49%)
  starting transfers between devices  33.2 us (23%)
  waiting for transfers between devices  30 us (21%)
  local copies, waits for them, and re-layouts  7.29 us (5%)
  other arithmetic  1.62 us (1%)
    pallas_call x9, Pallas kernels, call(): pl.pallas_call(body, out_shape=outs, in_specs=specs or [VMEM] * len(args)...  71.4 us
    ppermute x5, waiting for transfers between devices, along(): return lax.ppermute(value, 'dp', route)  14 us
    ppermute x5, starting transfers between devices, along(): return lax.ppermute(value, 'dp', route)  12.7 us
    ppermute x1, waiting for transfers between devices, shards(): far = lax.ppermute(coming, 'section', [(s + RUN - 1, s - 1) for s in cross])  10.7 us
    ppermute x1, starting transfers between devices, shards(): far = lax.ppermute(coming, 'section', [(s + RUN - 1, s - 1) for s in cross])  8.22 us
    unnamed x28, local copies, waits for them, and re-layouts  6.64 us
    all_to_all x1, starting transfers between devices, shards(): parts = lax.all_to_all(parts, 'dp', 0, 0)  6.2 us
    ppermute x1, waiting for transfers between devices, shards(): lax.ppermute(first['dx_back'], 'section', near + [(s, s + RUN - 1) for s...  3.2 us
  transfers between devices with their start and end apart: 14, of which 5 were waited for; matrix products, arithmetic and copies ran while one was open for 4% of the time, Pallas kernels for 28%

profile of v4, /device:TPU:30, one launch (start us, length us, event | category | flops | bytes accessed | tf_op | source)
XLA Modules:
  0.0 144.5 jit_solution(1229568747895665732)
XLA Ops:
  0.6 24.0 %whole_tick.1 = (bf16[4,80,1024]{2,1,0:T(8,128)(2,1)}, bf16[4,48,1024]{2,1,0:T(8,128)(2,1)}, bf16[128,2560]{1,0:T(8,128)(2,1)}, bf16[128,1536]{1,0:T(8,128)(2,1)...) custom-call(bf16[2,128,4,1024]{3,2,1,0:T(4,128)(2,1)} %bitcast.36, bf16[128,4,1024]{2,1,0:T(4,128)(2,1)} %bitcast.49, ...), custom_call_target="tpu_custom_call" | custom-call | flops 20000000000 | bytes 40000000 | tf_op jit(solution)/shard_map/whole_tick/pallas_call | solution.py:353
  24.6 2.7 %collective-permute-start = (bf16[4,48,1024]{2,1,0:T(8,128)(2,1)}, bf16[4,48,1024]{2,1,0:T(8,128)(2,1)S(1)}, u32[]{:S(2)}, u32[]{:S(2)}) collective-permute-start(bf16[4,48,1024]{2,1,0:T(8,128)(2,1)} %get-tuple-element.42), channel_id=1, source_target_pairs={{8,0},{16,8},{24,16},{40,32},{48,40},{56,48},{72,64},{80,72},{88,8... | collective-permute-start | bytes 1179656 | tf_op jit(solution)/shard_map/ppermute | solution.py:749
  27.3 0.0 copy-start.1
  27.3 0.0 copy-start
  27.3 1.4 collective-permute-start.2
  28.8 12.2 %forward_tick.1 = (f32[32,128]{1,0:T(8,128)}, f32[20,13,8,128]{3,2,1,0:T(8,128)}, f32[128,128]{1,0:T(8,128)}, f32[128,1024]{1,0:T(8,128)}, f32[128,128]{1,0:T(8,...) custom-call(bf16[2,128,4,1024]{3,2,1,0:T(4,128)(2,1)} %bitcast.37, ...), custom_call_target="tpu_custom_call" | custom-call | flops 1000000000 | bytes 2000000 | tf_op jit(solution)/shard_map/forward_tick/pallas_call | solution.py:353
  41.0 3.2 %collective-permute-done.near1 = bf16[4,48,1024]{2,1,0:T(8,128)(2,1)S(1)} collective-permute-done((bf16[4,48,1024]{2,1,0:T(8,128)(2,1)}, bf16[4,48,1024]{2,1,0:T(8,128)(2,1)S(1)}, u32[]{:S(2)}, u32[]{:S(2)}) %collective-permute-start) | collective-permute-done | bytes 393248 | tf_op jit(solution)/shard_map/ppermute | solution.py:749
  44.2 0.0 copy-start.12
  44.2 0.0 copy-done.1
  44.2 1.3 collective-permute-start.1
  45.5 0.1 collective-permute-start.4
  45.6 0.5 collective-permute-start.5
  46.1 8.2 %collective-permute-start.3 = (bf16[4,48,1024]{2,1,0:T(8,128)(2,1)S(1)}, bf16[4,48,1024]{2,1,0:T(8,128)(2,1)}, u32[]{:S(2)}, u32[]{:S(2)}) collective-permute-start(bf16[4,48,1024]{2,1,0:T(8,128)(2,1)S(1)} %collective-permute-done.near1), channel_id=1, source_target_pairs={{56,24},{88,56},{120,88},{152,120},{184,152},{216,184},{248,216},{... | collective-permute-start | bytes 1179656 | tf_op jit(solution)/shard_map/ppermute | solution.py:754
  54.4 0.0 copy-done
  54.4 1.3 copy.16
  55.6 0.7 stack.33.place
  56.3 0.0 collective-permute-done.4.refs_2_
  56.3 0.0 collective-permute-start.6
  56.3 0.0 collective-permute-done.5.refs_3_
  56.3 2.6 %turned_factors.1 = (bf16[512,512]{1,0:T(8,128)(2,1)}, bf16[256,512]{1,0:T(8,128)(2,1)}) custom-call(s32[5]{0:T(128)} %stack.33.place, bf16[128,1536]{1,0:T(8,128)(2,1)} %get-tuple-element.46.refs_0_, bf16[128,1536]{1,0:T(8,128)(2,1)} %get-tuple-element.47.refs_1_, bf16[128,1536]{1,0:T(8,128)(2,1)} %collective-permute-done.4.refs_2_, ...), custom_call_target="tpu_custom_call" | custom-call | flops 1000000000 | bytes 2000000 | tf_op jit(solution)/shard_map/turned_factors/pallas_call | solution.py:353
  58.9 0.0 copy-done.12
  58.9 0.0 collective-permute-done.2.far0
  58.9 0.0 copy-start.6
  58.9 10.7 %collective-permute-done.3.far1 = bf16[4,48,1024]{2,1,0:T(8,128)(2,1)} collective-permute-done((bf16[4,48,1024]{2,1,0:T(8,128)(2,1)S(1)}, bf16[4,48,1024]{2,1,0:T(8,128)(2,1)}, u32[]{:S(2)}, u32[]{:S(2)}) %collective-permute-start.3) | collective-permute-done | bytes 393248 | tf_op jit(solution)/shard_map/ppermute | solution.py:754
  69.6 0.0 collective-permute-done.1.near0
  69.6 0.0 copy-start.7
  69.6 0.0 copy-done.6
  69.6 0.8 copy-done.7
  70.4 7.8 %attention_tick.1.refs_1_.right = bf16[128,2560]{1,0:T(8,128)(2,1)} custom-call(s32[1]{0:T(128)} %bitcast.9.where, bf16[4,80,1024]{2,1,0:T(8,128)(2,1)} %copy-done.7, bf16[4,48,1024]{2,1,0:T(8,128)(2,1)} %copy-done.12, bf16[4,80,1024]{2,1,0:T(8,128)(2,1)} %copy-done.6, bf16[4,48,1024]{2,1,0:T(8,128)(2,1)} %collective-permute-done.3.far1, ...), custom_call_target="tpu_custom_call" | custom-call | flops 5000000000 | bytes 10000000 | tf_op jit(solution)/shard_map/attention_tick/pallas_call | solution.py:353
  78.2 0.1 collective-permute-start.7
  78.3 0.0 copy-done.4
  78.3 0.1 maximum_bitcast_fusion.1
  78.4 0.0 collective-permute-done.6.refs_2_
  78.4 0.0 copy-start.8
  78.4 2.2 %collective-permute-done.7.refs_3_ = bf16[128,2560]{1,0:T(8,128)(2,1)S(1)} collective-permute-done((bf16[128,2560]{1,0:T(8,128)(2,1)}, bf16[128,2560]{1,0:T(8,128)(2,1)S(1)}, u32[]{:S(2)}, u32[]{:S(2)}) %collective-permute-start.7) | collective-permute-done | bytes 655392 | tf_op jit(solution)/shard_map/ppermute | solution.py:739
  80.6 0.0 copy-done.8
  80.6 0.9 copy-done.9
  81.5 4.7 %terms.1 = (f32[128,2048]{1,0:T(8,128)}, bf16[128,2048]{1,0:T(8,128)(2,1)}, bf16[128,2048]{1,0:T(8,128)(2,1)}, bf16[128,2048]{1,0:T(8,128)(2,1)}) custom-call(bf16[512,512]{1,0:T(8,128)(2,1)} %get-tuple-element.48.after.left, bf16[256,512]{1,0:T(8,128)(2,1)} %get-tuple-element.49.small, bf16[128,2560]{1,0:T(8,128)(2,1)} %get-tuple-element.50.refs_0_, ...), custom_call_target="tpu_custom_call" | custom-call | flops 4000000000 | bytes 8000000 | tf_op jit(solution)/shard_map/terms/pallas_call | solution.py:353
  86.1 0.7 collective-permute-start.9
  86.8 6.5 %collective-permute-start.8 = (bf16[128,2048]{1,0:T(8,128)(2,1)}, bf16[128,2048]{1,0:T(8,128)(2,1)S(1)}, u32[]{:S(2)}, u32[]{:S(2)}) collective-permute-start(bf16[128,2048]{1,0:T(8,128)(2,1)} %get-tuple-element.56), channel_id=1, source_target_pairs={{0,2},{1,3},{6,4},{7,5},{8,10},{9,11},{14,12},{15,13},{16,18},{17,... | collective-permute-start | bytes 1572872 | tf_op jit(solution)/shard_map/ppermute | solution.py:743
  93.3 0.1 collective-permute-start.10
  93.4 4.2 %collective-permute-start.11 = (bf16[128,2048]{1,0:T(8,128)(2,1)}, bf16[128,2048]{1,0:T(8,128)(2,1)}, u32[]{:S(2)}, u32[]{:S(2)}) collective-permute-start(bf16[128,2048]{1,0:T(8,128)(2,1)} %get-tuple-element.55), channel_id=1, source_target_pairs={{0,4},{1,5},{6,2},{7,3},{8,12},{9,13},{14,10},{15,11},{16,20},{17,... | collective-permute-start | bytes 1572872 | tf_op jit(solution)/shard_map/ppermute | solution.py:743
  97.6 9.9 %stream_tick.1 = (bf16[8,32,512]{2,1,0:T(8,128)(2,1)}, f32[128,1024]{1,0:T(8,128)}, f32[128,128]{1,0:T(8,128)}) custom-call(s32[1]{0:T(128)} %bitcast.9.where, bf16[4,80,1024]{2,1,0:T(8,128)(2,1)} %copy-done.7, bf16[4,48,1024]{2,1,0:T(8,128)(2,1)} %copy-done.12, bf16[4,80,1024]{2,1,0:T(8,128)(2,1)} %copy-done.6, ...), custom_call_target="tpu_custom_call" | custom-call | flops 6000000000 | bytes 12000000 | tf_op jit(solution)/shard_map/stream_tick/pallas_call | solution.py:353
  107.5 0.0 collective-permute-done.8
  107.5 0.0 copy-done.2
  107.5 0.1 add_convert_fusion.after
  107.6 0.0 copy-start.3
  107.6 1.3 collective-permute-start.12
  108.9 0.0 copy-done.3
  108.9 5.7 %output_tick.1 = bf16[4,128,1024]{2,1,0:T(8,128)(2,1)} custom-call(s32[1]{0:T(128)} %bitcast.9.where, bf16[4,80,1024]{2,1,0:T(8,128)(2,1)} %copy-done.7, bf16[4,48,1024]{2,1,0:T(8,128)(2,1)} %copy-done.12, bf16[4,80,1024]{2,1,0:T(8,128)(2,1)} %copy-done.6, bf16[4,48,1024]{2,1,0:T(8,128)(2,1)} %collective-permute-done.3.far1, bf16[4,128,1024]{2,1,0:T(8,128)(2,1)} %bitcast.43, ...), custom_call_target="tpu_custom_call" | custom-call | flops 5000000000 | bytes 10000000 | tf_op jit(solution)/shard_map/output_tick/pallas_call | solution.py:353
  114.6 1.4 maximum_bitcast_fusion
  116.0 2.9 %copy.14 = bf16[1,2,128,4,1024]{4,3,2,1,0:T(4,128)(2,1)} copy(bf16[1,2,128,4,1024]{4,2,3,1,0:T(8,128)(2,1)S(1)} %maximum_bitcast_fusion) | data formatting | bytes 4194304
  119.0 6.2 %all-to-all-start = ((bf16[8,32,512]{2,1,0:T(8,128)(2,1)}), bf16[8,32,512]{2,1,0:T(8,128)(2,1)S(1)}, u32[]{:S(2)}, u32[]{:S(2)}) async-start(bf16[8,32,512]{2,1,0:T(8,128)(2,1)} %get-tuple-element.74), calls=%async_computation | async-start | bytes 524288 | tf_op jit(solution)/shard_map/all_to_all | solution.py:773
  125.2 0.0 collective-permute-done.10.refs_2_
  125.2 0.0 copy-start.11
  125.2 2.9 %collective-permute-done.11.refs_3_ = bf16[128,2048]{1,0:T(8,128)(2,1)} collective-permute-done((bf16[128,2048]{1,0:T(8,128)(2,1)}, bf16[128,2048]{1,0:T(8,128)(2,1)}, u32[]{:S(2)}, u32[]{:S(2)}) %collective-permute-start.11) | collective-permute-done | bytes 524320 | tf_op jit(solution)/shard_map/ppermute | solution.py:743
  128.1 0.0 collective-permute-done.9.refs_1_
  128.1 11.0 %collective-permute-done.12.refs_4_ = bf16[128,2048]{1,0:T(8,128)(2,1)} collective-permute-done((bf16[128,2048]{1,0:T(8,128)(2,1)S(1)}, bf16[128,2048]{1,0:T(8,128)(2,1)}, u32[]{:S(2)}, u32[]{:S(2)}) %collective-permute-start.12) | collective-permute-done | bytes 524320 | tf_op jit(solution)/shard_map/ppermute | solution.py:743
  139.1 0.0 copy-done.11
  139.2 0.0 copy-done.10
  139.2 3.0 %finish_terms.1 = (f32[128,1536]{1,0:T(8,128)}, f32[64,1024]{1,0:T(8,128)}) custom-call(f32[128,2048]{1,0:T(8,128)} %get-tuple-element.57.after.refs_0_, bf16[128,2048]{1,0:T(8,128)(2,1)} %copy-done.10, bf16[128,2048]{1,0:T(8,128)(2,1)} %copy-done.11, bf16[128,2048]{1,0:T(8,128)(2,1)} %collective-permute-done.11.refs_3_, ...), custom_call_target="tpu_custom_call" | custom-call | flops 99999997952 | bytes 200000000 | tf_op jit(solution)/shard_map/finish_terms/pallas_call | solution.py:353
  142.2 0.0 all-to-all-done.parts
  142.2 0.7 copy-done.5
  142.9 1.6 %finish_map.1 = (f32[24,512]{1,0:T(8,128)}, f32[1,128]{1,0:T(1,128)}) custom-call(bf16[8,32,512]{2,1,0:T(8,128)(2,1)} %copy-done.5, f32[128,1536]{1,0:T(8,128)} %get-tuple-element.72.after), custom_call_target="tpu_custom_call" | custom-call | flops 1000000000 | bytes 2000000 | tf_op jit(solution)/shard_map/finish_map/pallas_call | solution.py:353
  (5 shorter events, 0.0 us)
Async XLA Ops:
  24.6 19.5 %collective-permute-start = (bf16[4,48,1024]{2,1,0:T(8,128)(2,1)}, bf16[4,48,1024]{2,1,0:T(8,128)(2,1)S(1)}, u32[]{:S(2)}, u32[]{:S(2)}) collective-permute-start(bf16[4,48,1024]{2,1,0:T(8,128)(2,1)} %get-tuple-element.42), channel_id=1, source_target_pairs={{8,0},{16,8},{24,16},{40,32},{48,40},{56,48},{72,64},{80,72},{88,8... | collective-permute-start | bytes 1179656 | tf_op jit(solution)/shard_map/ppermute | solution.py:749
  27.3 16.9 %copy-start.1 = (bf16[4,80,1024]{2,1,0:T(8,128)(2,1)S(1)}, bf16[4,80,1024]{2,1,0:T(8,128)(2,1)}, u32[]{:S(2)}) copy-start(bf16[4,80,1024]{2,1,0:T(8,128)(2,1)} %get-tuple-element.44) | copy-start | bytes 1966084
  27.3 27.0 %copy-start = (bf16[1,128,4,1024]{3,2,1,0:T(4,128)(2,1)S(1)}, bf16[1,128,4,1024]{3,2,1,0:T(4,128)(2,1)}, u32[]{:S(2)}) copy-start(bf16[1,128,4,1024]{3,2,1,0:T(4,128)(2,1)} %param.10) | copy-start | bytes 3145732
  27.3 31.6 %collective-permute-start.2 = (bf16[4,80,1024]{2,1,0:T(8,128)(2,1)}, bf16[4,80,1024]{2,1,0:T(8,128)(2,1)S(1)}, u32[]{:S(2)}, u32[]{:S(2)}) collective-permute-start(bf16[4,80,1024]{2,1,0:T(8,128)(2,1)} %get-tuple-element.44), channel_id=1, source_target_pairs={{32,24},{64,56},{96,88},{128,120},{160,152},{192,184},{224,216},{3... | collective-permute-start | bytes 1966088 | tf_op jit(solution)/shard_map/ppermute | solution.py:750
  44.2 14.8 %copy-start.12 = (bf16[4,48,1024]{2,1,0:T(8,128)(2,1)}, bf16[4,48,1024]{2,1,0:T(8,128)(2,1)S(1)}, u32[]{:S(2)}) copy-start(bf16[4,48,1024]{2,1,0:T(8,128)(2,1)S(1)} %collective-permute-done.near1) | copy-start | bytes 1179652
  44.2 25.4 %collective-permute-start.1 = (bf16[4,80,1024]{2,1,0:T(8,128)(2,1)S(1)}, bf16[4,80,1024]{2,1,0:T(8,128)(2,1)S(1)}, u32[]{:S(2)}, u32[]{:S(2)}) collective-permute-start(bf16[4,80,1024]{2,1,0:T(8,128)(2,1)S(1)} %copy-done.1), channel_id=1, source_target_pairs={{8,0},{16,8},{24,16},{40,32},{48,40},{56,48},{72,64},{80,72},{88,8... | collective-permute-start | bytes 1966088 | tf_op jit(solution)/shard_map/ppermute | solution.py:755
  45.5 10.8 %collective-permute-start.4 = (bf16[128,1536]{1,0:T(8,128)(2,1)}, bf16[128,1536]{1,0:T(8,128)(2,1)}, u32[]{:S(2)}, u32[]{:S(2)}) collective-permute-start(bf16[128,1536]{1,0:T(8,128)(2,1)} %get-tuple-element.46.refs_0_), channel_id=1, source_target_pairs={{0,1},{1,0},{2,3},{3,2},{4,5},{5,4},{6,7},{7,6},{8,9},{9,8},{10,11... | collective-permute-start | bytes 1179656 | tf_op jit(solution)/shard_map/ppermute | solution.py:739
  45.6 10.7 %collective-permute-start.5 = (bf16[128,1536]{1,0:T(8,128)(2,1)}, bf16[128,1536]{1,0:T(8,128)(2,1)}, u32[]{:S(2)}, u32[]{:S(2)}) collective-permute-start(bf16[128,1536]{1,0:T(8,128)(2,1)} %get-tuple-element.47.refs_1_), channel_id=1, source_target_pairs={{0,1},{1,0},{2,3},{3,2},{4,5},{5,4},{6,7},{7,6},{8,9},{9,8},{10,11... | collective-permute-start | bytes 1179656 | tf_op jit(solution)/shard_map/ppermute | solution.py:739
  46.1 23.5 %collective-permute-start.3 = (bf16[4,48,1024]{2,1,0:T(8,128)(2,1)S(1)}, bf16[4,48,1024]{2,1,0:T(8,128)(2,1)}, u32[]{:S(2)}, u32[]{:S(2)}) collective-permute-start(bf16[4,48,1024]{2,1,0:T(8,128)(2,1)S(1)} %collective-permute-done.near1), channel_id=1, source_target_pairs={{56,24},{88,56},{120,88},{152,120},{184,152},{216,184},{248,216},{... | collective-permute-start | bytes 1179656 | tf_op jit(solution)/shard_map/ppermute | solution.py:754
  56.3 22.1 %collective-permute-start.6 = (bf16[128,2560]{1,0:T(8,128)(2,1)}, bf16[128,2560]{1,0:T(8,128)(2,1)S(1)}, u32[]{:S(2)}, u32[]{:S(2)}) collective-permute-start(bf16[128,2560]{1,0:T(8,128)(2,1)} %get-tuple-element.50.refs_0_), channel_id=1, source_target_pairs={{0,1},{1,0},{2,3},{3,2},{4,5},{5,4},{6,7},{7,6},{8,9},{9,8},{10,11... | collective-permute-start | bytes 1966088 | tf_op jit(solution)/shard_map/ppermute | solution.py:739
  58.9 10.7 %copy-start.6 = (bf16[4,80,1024]{2,1,0:T(8,128)(2,1)}, bf16[4,80,1024]{2,1,0:T(8,128)(2,1)S(1)}, u32[]{:S(2)}) copy-start(bf16[4,80,1024]{2,1,0:T(8,128)(2,1)S(1)} %collective-permute-done.2.far0) | copy-start | bytes 1966084
  69.6 0.8 copy-start.7
  70.4 7.9 %copy-start.4 = (bf16[4,48,1024]{2,1,0:T(8,128)(2,1)S(1)}, bf16[4,48,1024]{2,1,0:T(8,128)(2,1)}, u32[]{:S(2)}) copy-start(bf16[4,48,1024]{2,1,0:T(8,128)(2,1)} %get-tuple-element.42) | copy-start | bytes 1179652
  78.2 2.4 %collective-permute-start.7 = (bf16[128,2560]{1,0:T(8,128)(2,1)}, bf16[128,2560]{1,0:T(8,128)(2,1)S(1)}, u32[]{:S(2)}, u32[]{:S(2)}) collective-permute-start(bf16[128,2560]{1,0:T(8,128)(2,1)} %attention_tick.1.refs_1_.right), channel_id=1, source_target_pairs={{0,1},{1,0},{2,3},{3,2},{4,5},{5,4},{6,7},{7,6},{8,9},{9,8},{10,11... | collective-permute-start | bytes 1966088 | tf_op jit(solution)/shard_map/ppermute | solution.py:739
  78.4 2.2 %copy-start.8 = (bf16[128,2560]{1,0:T(8,128)(2,1)}, bf16[128,2560]{1,0:T(8,128)(2,1)S(1)}, u32[]{:S(2)}) copy-start(bf16[128,2560]{1,0:T(8,128)(2,1)S(1)} %collective-permute-done.6.refs_2_) | copy-start | bytes 1966084
  80.6 0.9 copy-start.9
  86.1 42.0 %collective-permute-start.9 = (bf16[128,2048]{1,0:T(8,128)(2,1)}, bf16[128,2048]{1,0:T(8,128)(2,1)S(1)}, u32[]{:S(2)}, u32[]{:S(2)}) collective-permute-start(bf16[128,2048]{1,0:T(8,128)(2,1)} %get-tuple-element.56), channel_id=1, source_target_pairs={{2,4},{3,5},{4,2},{5,3},{10,12},{11,13},{12,10},{13,11},{18,20},{1... | collective-permute-start | bytes 1572872 | tf_op jit(solution)/shard_map/ppermute | solution.py:743
  86.8 20.7 %collective-permute-start.8 = (bf16[128,2048]{1,0:T(8,128)(2,1)}, bf16[128,2048]{1,0:T(8,128)(2,1)S(1)}, u32[]{:S(2)}, u32[]{:S(2)}) collective-permute-start(bf16[128,2048]{1,0:T(8,128)(2,1)} %get-tuple-element.56), channel_id=1, source_target_pairs={{0,2},{1,3},{6,4},{7,5},{8,10},{9,11},{14,12},{15,13},{16,18},{17,... | collective-permute-start | bytes 1572872 | tf_op jit(solution)/shard_map/ppermute | solution.py:743
  93.3 31.9 %collective-permute-start.10 = (bf16[128,2048]{1,0:T(8,128)(2,1)}, bf16[128,2048]{1,0:T(8,128)(2,1)S(1)}, u32[]{:S(2)}, u32[]{:S(2)}) collective-permute-start(bf16[128,2048]{1,0:T(8,128)(2,1)} %get-tuple-element.71), channel_id=1, source_target_pairs={{0,2},{1,3},{2,0},{3,1},{4,6},{5,7},{6,4},{7,5},{8,10},{9,11},{10,... | collective-permute-start | bytes 1572872 | tf_op jit(solution)/shard_map/ppermute | solution.py:743
  93.4 34.7 %collective-permute-start.11 = (bf16[128,2048]{1,0:T(8,128)(2,1)}, bf16[128,2048]{1,0:T(8,128)(2,1)}, u32[]{:S(2)}, u32[]{:S(2)}) collective-permute-start(bf16[128,2048]{1,0:T(8,128)(2,1)} %get-tuple-element.55), channel_id=1, source_target_pairs={{0,4},{1,5},{6,2},{7,3},{8,12},{9,13},{14,10},{15,11},{16,20},{17,... | collective-permute-start | bytes 1572872 | tf_op jit(solution)/shard_map/ppermute | solution.py:743
  97.6 9.9 %copy-start.2 = (bf16[128,2048]{1,0:T(8,128)(2,1)S(1)}, bf16[128,2048]{1,0:T(8,128)(2,1)}, u32[]{:S(2)}) copy-start(bf16[128,2048]{1,0:T(8,128)(2,1)} %get-tuple-element.55) | copy-start | bytes 1572868
  107.6 1.3 copy-start.3
  107.6 31.5 %collective-permute-start.12 = (bf16[128,2048]{1,0:T(8,128)(2,1)S(1)}, bf16[128,2048]{1,0:T(8,128)(2,1)}, u32[]{:S(2)}, u32[]{:S(2)}) collective-permute-start(bf16[128,2048]{1,0:T(8,128)(2,1)S(1)} %add_convert_fusion.after), channel_id=1, source_target_pairs={{2,6},{3,7},{4,0},{5,1},{10,14},{11,15},{12,8},{13,9},{18,22},{19,... | collective-permute-start | bytes 1572872 | tf_op jit(solution)/shard_map/ppermute | solution.py:743
  119.0 23.2 %all-to-all-start = ((bf16[8,32,512]{2,1,0:T(8,128)(2,1)}), bf16[8,32,512]{2,1,0:T(8,128)(2,1)S(1)}, u32[]{:S(2)}, u32[]{:S(2)}) async-start(bf16[8,32,512]{2,1,0:T(8,128)(2,1)} %get-tuple-element.74), calls=%async_computation | async-start | bytes 524288 | tf_op jit(solution)/shard_map/all_to_all | solution.py:773
  125.2 14.0 %copy-start.11 = (bf16[128,2048]{1,0:T(8,128)(2,1)}, bf16[128,2048]{1,0:T(8,128)(2,1)S(1)}, u32[]{:S(2)}) copy-start(bf16[128,2048]{1,0:T(8,128)(2,1)S(1)} %collective-permute-done.10.refs_2_) | copy-start | bytes 1572868
  128.1 11.0 %copy-start.10 = (bf16[128,2048]{1,0:T(8,128)(2,1)}, bf16[128,2048]{1,0:T(8,128)(2,1)S(1)}, u32[]{:S(2)}) copy-start(bf16[128,2048]{1,0:T(8,128)(2,1)S(1)} %collective-permute-done.9.refs_1_) | copy-start | bytes 1572868
  142.2 0.7 copy-start.5

commit v5 on v4

--- a/solution.py
+++ b/solution.py
@@ -664,7 +664,7 @@
 
     own, *sends = call(
         body,
-        [struct((rows, PACKED), F32)] + [struct((rows, PACKED), BF16)] * (STEPS - 1),
+        [struct((rows, PACKED), BF16)] * STEPS,
         [],
         (left, small, *rights),
         4,
@@ -678,7 +678,7 @@
 
     def body(*refs):
         *others, grad_qkv, grad_out = refs[1:]
-        total = refs[0][...]
+        total = refs[0][...].astype(F32)
         for other in others:
             total = total + other[...].astype(F32)
         grad_qkv[...] = total[:, : 3 * INNER]

time: 145 us -> 145 us (level)
  no operation moved by 1% of the time
where the time goes in v5:
time: 145 us; the launch traced here: 144 us
  Pallas kernels  71.1 us (49%)
  starting transfers between devices  33.2 us (23%)
  waiting for transfers between devices  30.1 us (21%)
  local copies, waits for them, and re-layouts  7.27 us (5%)
  other arithmetic  1.62 us (1%)
    pallas_call x9, Pallas kernels, call(): pl.pallas_call(body, out_shape=outs, in_specs=specs or [VMEM] * len(args)...  71.1 us
    ppermute x5, waiting for transfers between devices, along(): return lax.ppermute(value, 'dp', route)  14 us
    ppermute x5, starting transfers between devices, along(): return lax.ppermute(value, 'dp', route)  12.8 us
    ppermute x1, waiting for transfers between devices, shards(): far = lax.ppermute(coming, 'section', [(s + RUN - 1, s - 1) for s in cross])  10.7 us
    ppermute x1, starting transfers between devices, shards(): far = lax.ppermute(coming, 'section', [(s + RUN - 1, s - 1) for s in cross])  8.22 us
    unnamed x28, local copies, waits for them, and re-layouts  6.66 us
    all_to_all x1, starting transfers between devices, shards(): parts = lax.all_to_all(parts, 'dp', 0, 0)  6.06 us
    ppermute x1, waiting for transfers between devices, shards(): lax.ppermute(first['dx_back'], 'section', near + [(s, s + RUN - 1) for s...  3.17 us
  transfers between devices with their start and end apart: 14, of which 5 were waited for; matrix products, arithmetic and copies ran while one was open for 4% of the time, Pallas kernels for 28%

profile of v5, /device:TPU:30, one launch (start us, length us, event | category | flops | bytes accessed | tf_op | source)
XLA Modules:
  0.0 144.2 jit_solution(15576144994068562288)
XLA Ops:
  0.6 24.0 %whole_tick.1 = (bf16[4,80,1024]{2,1,0:T(8,128)(2,1)}, bf16[4,48,1024]{2,1,0:T(8,128)(2,1)}, bf16[128,2560]{1,0:T(8,128)(2,1)}, bf16[128,1536]{1,0:T(8,128)(2,1)...) custom-call(bf16[2,128,4,1024]{3,2,1,0:T(4,128)(2,1)} %bitcast.36, bf16[128,4,1024]{2,1,0:T(4,128)(2,1)} %bitcast.49, ...), custom_call_target="tpu_custom_call" | custom-call | flops 20000000000 | bytes 40000000 | tf_op jit(solution)/shard_map/whole_tick/pallas_call | solution.py:353
  24.6 2.7 %collective-permute-start = (bf16[4,48,1024]{2,1,0:T(8,128)(2,1)}, bf16[4,48,1024]{2,1,0:T(8,128)(2,1)S(1)}, u32[]{:S(2)}, u32[]{:S(2)}) collective-permute-start(bf16[4,48,1024]{2,1,0:T(8,128)(2,1)} %get-tuple-element.42), channel_id=1, source_target_pairs={{8,0},{16,8},{24,16},{40,32},{48,40},{56,48},{72,64},{80,72},{88,8... | collective-permute-start | bytes 1179656 | tf_op jit(solution)/shard_map/ppermute | solution.py:749
  27.3 0.0 copy-start.1
  27.3 0.0 copy-start
  27.3 1.4 collective-permute-start.2
  28.7 12.2 %forward_tick.1 = (f32[32,128]{1,0:T(8,128)}, f32[20,13,8,128]{3,2,1,0:T(8,128)}, f32[128,128]{1,0:T(8,128)}, f32[128,1024]{1,0:T(8,128)}, f32[128,128]{1,0:T(8,...) custom-call(bf16[2,128,4,1024]{3,2,1,0:T(4,128)(2,1)} %bitcast.37, ...), custom_call_target="tpu_custom_call" | custom-call | flops 1000000000 | bytes 2000000 | tf_op jit(solution)/shard_map/forward_tick/pallas_call | solution.py:353
  41.0 3.2 %collective-permute-done.near1 = bf16[4,48,1024]{2,1,0:T(8,128)(2,1)S(1)} collective-permute-done((bf16[4,48,1024]{2,1,0:T(8,128)(2,1)}, bf16[4,48,1024]{2,1,0:T(8,128)(2,1)S(1)}, u32[]{:S(2)}, u32[]{:S(2)}) %collective-permute-start) | collective-permute-done | bytes 393248 | tf_op jit(solution)/shard_map/ppermute | solution.py:749
  44.2 0.0 copy-start.12
  44.2 0.0 copy-done.1
  44.2 1.3 collective-permute-start.1
  45.5 0.1 collective-permute-start.4
  45.6 0.5 collective-permute-start.5
  46.1 8.2 %collective-permute-start.3 = (bf16[4,48,1024]{2,1,0:T(8,128)(2,1)S(1)}, bf16[4,48,1024]{2,1,0:T(8,128)(2,1)}, u32[]{:S(2)}, u32[]{:S(2)}) collective-permute-start(bf16[4,48,1024]{2,1,0:T(8,128)(2,1)S(1)} %collective-permute-done.near1), channel_id=1, source_target_pairs={{56,24},{88,56},{120,88},{152,120},{184,152},{216,184},{248,216},{... | collective-permute-start | bytes 1179656 | tf_op jit(solution)/shard_map/ppermute | solution.py:754
  54.3 0.0 copy-done
  54.4 1.3 copy.16
  55.6 0.6 stack.33.place
  56.2 0.0 collective-permute-done.4.refs_2_
  56.3 0.0 collective-permute-start.6
  56.3 0.0 collective-permute-done.5.refs_3_
  56.3 2.6 %turned_factors.1 = (bf16[512,512]{1,0:T(8,128)(2,1)}, bf16[256,512]{1,0:T(8,128)(2,1)}) custom-call(s32[5]{0:T(128)} %stack.33.place, bf16[128,1536]{1,0:T(8,128)(2,1)} %get-tuple-element.46.refs_0_, bf16[128,1536]{1,0:T(8,128)(2,1)} %get-tuple-element.47.refs_1_, bf16[128,1536]{1,0:T(8,128)(2,1)} %collective-permute-done.4.refs_2_, ...), custom_call_target="tpu_custom_call" | custom-call | flops 1000000000 | bytes 2000000 | tf_op jit(solution)/shard_map/turned_factors/pallas_call | solution.py:353
  58.9 0.0 copy-done.12
  58.9 0.0 collective-permute-done.2.far0
  58.9 0.0 copy-start.6
  58.9 10.7 %collective-permute-done.3.far1 = bf16[4,48,1024]{2,1,0:T(8,128)(2,1)} collective-permute-done((bf16[4,48,1024]{2,1,0:T(8,128)(2,1)S(1)}, bf16[4,48,1024]{2,1,0:T(8,128)(2,1)}, u32[]{:S(2)}, u32[]{:S(2)}) %collective-permute-start.3) | collective-permute-done | bytes 393248 | tf_op jit(solution)/shard_map/ppermute | solution.py:754
  69.6 0.0 collective-permute-done.1.near0
  69.6 0.0 copy-start.7
  69.6 0.0 copy-done.6
  69.6 0.8 copy-done.7
  70.5 7.7 %attention_tick.1.refs_1_.right = bf16[128,2560]{1,0:T(8,128)(2,1)} custom-call(s32[1]{0:T(128)} %bitcast.9.where, bf16[4,80,1024]{2,1,0:T(8,128)(2,1)} %copy-done.7, bf16[4,48,1024]{2,1,0:T(8,128)(2,1)} %copy-done.12, bf16[4,80,1024]{2,1,0:T(8,128)(2,1)} %copy-done.6, bf16[4,48,1024]{2,1,0:T(8,128)(2,1)} %collective-permute-done.3.far1, ...), custom_call_target="tpu_custom_call" | custom-call | flops 5000000000 | bytes 10000000 | tf_op jit(solution)/shard_map/attention_tick/pallas_call | solution.py:353
  78.2 0.1 collective-permute-start.7
  78.3 0.0 copy-done.4
  78.3 0.1 maximum_bitcast_fusion.1
  78.4 0.0 collective-permute-done.6.refs_2_
  78.4 0.0 copy-start.8
  78.4 2.2 %collective-permute-done.7.refs_3_ = bf16[128,2560]{1,0:T(8,128)(2,1)S(1)} collective-permute-done((bf16[128,2560]{1,0:T(8,128)(2,1)}, bf16[128,2560]{1,0:T(8,128)(2,1)S(1)}, u32[]{:S(2)}, u32[]{:S(2)}) %collective-permute-start.7) | collective-permute-done | bytes 655392 | tf_op jit(solution)/shard_map/ppermute | solution.py:739
  80.6 0.0 copy-done.8
  80.6 0.9 copy-done.9
  81.5 4.5 %terms.1 = (bf16[128,2048]{1,0:T(8,128)(2,1)}, bf16[128,2048]{1,0:T(8,128)(2,1)}, bf16[128,2048]{1,0:T(8,128)(2,1)}, bf16[128,2048]{1,0:T(8,128)(2,1)}) custom-call(bf16[512,512]{1,0:T(8,128)(2,1)} %get-tuple-element.48.after.left, bf16[256,512]{1,0:T(8,128)(2,1)} %get-tuple-element.49.small, bf16[128,2560]{1,0:T(8,128)(2,1)} %get-tuple-element.50.refs_0_, ...), custom_call_target="tpu_custom_call" | custom-call | flops 4000000000 | bytes 8000000 | tf_op jit(solution)/shard_map/terms/pallas_call | solution.py:353
  86.0 0.7 collective-permute-start.9
  86.7 6.5 %collective-permute-start.8 = (bf16[128,2048]{1,0:T(8,128)(2,1)}, bf16[128,2048]{1,0:T(8,128)(2,1)S(1)}, u32[]{:S(2)}, u32[]{:S(2)}) collective-permute-start(bf16[128,2048]{1,0:T(8,128)(2,1)} %get-tuple-element.56), channel_id=1, source_target_pairs={{0,2},{1,3},{6,4},{7,5},{8,10},{9,11},{14,12},{15,13},{16,18},{17,... | collective-permute-start | bytes 1572872 | tf_op jit(solution)/shard_map/ppermute | solution.py:743
  93.2 0.1 collective-permute-start.10
  93.3 4.3 %collective-permute-start.11 = (bf16[128,2048]{1,0:T(8,128)(2,1)}, bf16[128,2048]{1,0:T(8,128)(2,1)}, u32[]{:S(2)}, u32[]{:S(2)}) collective-permute-start(bf16[128,2048]{1,0:T(8,128)(2,1)} %get-tuple-element.55), channel_id=1, source_target_pairs={{0,4},{1,5},{6,2},{7,3},{8,12},{9,13},{14,10},{15,11},{16,20},{17,... | collective-permute-start | bytes 1572872 | tf_op jit(solution)/shard_map/ppermute | solution.py:743
  97.5 9.9 %stream_tick.1 = (bf16[8,32,512]{2,1,0:T(8,128)(2,1)}, f32[128,1024]{1,0:T(8,128)}, f32[128,128]{1,0:T(8,128)}) custom-call(s32[1]{0:T(128)} %bitcast.9.where, bf16[4,80,1024]{2,1,0:T(8,128)(2,1)} %copy-done.7, bf16[4,48,1024]{2,1,0:T(8,128)(2,1)} %copy-done.12, bf16[4,80,1024]{2,1,0:T(8,128)(2,1)} %copy-done.6, ...), custom_call_target="tpu_custom_call" | custom-call | flops 6000000000 | bytes 12000000 | tf_op jit(solution)/shard_map/stream_tick/pallas_call | solution.py:353
  107.4 0.0 collective-permute-done.8
  107.4 0.0 copy-done.2
  107.4 0.1 add_convert_fusion.after
  107.6 0.0 copy-start.3
  107.6 1.3 collective-permute-start.12
  108.9 0.0 copy-done.3
  108.9 5.7 %output_tick.1 = bf16[4,128,1024]{2,1,0:T(8,128)(2,1)} custom-call(s32[1]{0:T(128)} %bitcast.9.where, bf16[4,80,1024]{2,1,0:T(8,128)(2,1)} %copy-done.7, bf16[4,48,1024]{2,1,0:T(8,128)(2,1)} %copy-done.12, bf16[4,80,1024]{2,1,0:T(8,128)(2,1)} %copy-done.6, bf16[4,48,1024]{2,1,0:T(8,128)(2,1)} %collective-permute-done.3.far1, bf16[4,128,1024]{2,1,0:T(8,128)(2,1)} %bitcast.43, ...), custom_call_target="tpu_custom_call" | custom-call | flops 5000000000 | bytes 10000000 | tf_op jit(solution)/shard_map/output_tick/pallas_call | solution.py:353
  114.6 1.4 maximum_bitcast_fusion
  116.0 2.9 %copy.14 = bf16[1,2,128,4,1024]{4,3,2,1,0:T(4,128)(2,1)} copy(bf16[1,2,128,4,1024]{4,2,3,1,0:T(8,128)(2,1)S(1)} %maximum_bitcast_fusion) | data formatting | bytes 4194304
  118.9 6.1 %all-to-all-start = ((bf16[8,32,512]{2,1,0:T(8,128)(2,1)}), bf16[8,32,512]{2,1,0:T(8,128)(2,1)S(1)}, u32[]{:S(2)}, u32[]{:S(2)}) async-start(bf16[8,32,512]{2,1,0:T(8,128)(2,1)} %get-tuple-element.74), calls=%async_computation | async-start | bytes 524288 | tf_op jit(solution)/shard_map/all_to_all | solution.py:773
  125.0 0.0 collective-permute-done.10.refs_2_
  125.0 0.0 copy-start.11
  125.0 3.1 %collective-permute-done.11.refs_3_ = bf16[128,2048]{1,0:T(8,128)(2,1)} collective-permute-done((bf16[128,2048]{1,0:T(8,128)(2,1)}, bf16[128,2048]{1,0:T(8,128)(2,1)}, u32[]{:S(2)}, u32[]{:S(2)}) %collective-permute-start.11) | collective-permute-done | bytes 524320 | tf_op jit(solution)/shard_map/ppermute | solution.py:743
  128.0 0.0 collective-permute-done.9.refs_1_
  128.1 11.0 %collective-permute-done.12.refs_4_ = bf16[128,2048]{1,0:T(8,128)(2,1)} collective-permute-done((bf16[128,2048]{1,0:T(8,128)(2,1)S(1)}, bf16[128,2048]{1,0:T(8,128)(2,1)}, u32[]{:S(2)}, u32[]{:S(2)}) %collective-permute-start.12) | collective-permute-done | bytes 524320 | tf_op jit(solution)/shard_map/ppermute | solution.py:743
  139.0 0.0 copy-done.11
  139.0 0.0 copy-done.10
  139.0 2.9 %finish_terms.1 = (f32[128,1536]{1,0:T(8,128)}, f32[64,1024]{1,0:T(8,128)}) custom-call(bf16[128,2048]{1,0:T(8,128)(2,1)} %get-tuple-element.57.after.refs_0_, bf16[128,2048]{1,0:T(8,128)(2,1)} %copy-done.10, bf16[128,2048]{1,0:T(8,128)(2,1)} %copy-done.11, bf16[128,2048]{1,0:T(8,128)(2,1)} %collective-permute-done.11.refs_3_, ...), custom_call_target="tpu_custom_call" | custom-call | flops 99999997952 | bytes 200000000 | tf_op jit(solution)/shard_map/finish_terms/pallas_call | solution.py:353
  141.9 0.0 all-to-all-done.parts
  141.9 0.7 copy-done.5
  142.6 1.6 %finish_map.1 = (f32[24,512]{1,0:T(8,128)}, f32[1,128]{1,0:T(1,128)}) custom-call(bf16[8,32,512]{2,1,0:T(8,128)(2,1)} %copy-done.5, f32[128,1536]{1,0:T(8,128)} %get-tuple-element.72.after), custom_call_target="tpu_custom_call" | custom-call | flops 1000000000 | bytes 2000000 | tf_op jit(solution)/shard_map/finish_map/pallas_call | solution.py:353
  (5 shorter events, 0.0 us)
Async XLA Ops:
  24.6 19.5 %collective-permute-start = (bf16[4,48,1024]{2,1,0:T(8,128)(2,1)}, bf16[4,48,1024]{2,1,0:T(8,128)(2,1)S(1)}, u32[]{:S(2)}, u32[]{:S(2)}) collective-permute-start(bf16[4,48,1024]{2,1,0:T(8,128)(2,1)} %get-tuple-element.42), channel_id=1, source_target_pairs={{8,0},{16,8},{24,16},{40,32},{48,40},{56,48},{72,64},{80,72},{88,8... | collective-permute-start | bytes 1179656 | tf_op jit(solution)/shard_map/ppermute | solution.py:749
  27.3 16.9 %copy-start.1 = (bf16[4,80,1024]{2,1,0:T(8,128)(2,1)S(1)}, bf16[4,80,1024]{2,1,0:T(8,128)(2,1)}, u32[]{:S(2)}) copy-start(bf16[4,80,1024]{2,1,0:T(8,128)(2,1)} %get-tuple-element.44) | copy-start | bytes 1966084
  27.3 27.0 %copy-start = (bf16[1,128,4,1024]{3,2,1,0:T(4,128)(2,1)S(1)}, bf16[1,128,4,1024]{3,2,1,0:T(4,128)(2,1)}, u32[]{:S(2)}) copy-start(bf16[1,128,4,1024]{3,2,1,0:T(4,128)(2,1)} %param.10) | copy-start | bytes 3145732
  27.3 31.6 %collective-permute-start.2 = (bf16[4,80,1024]{2,1,0:T(8,128)(2,1)}, bf16[4,80,1024]{2,1,0:T(8,128)(2,1)S(1)}, u32[]{:S(2)}, u32[]{:S(2)}) collective-permute-start(bf16[4,80,1024]{2,1,0:T(8,128)(2,1)} %get-tuple-element.44), channel_id=1, source_target_pairs={{32,24},{64,56},{96,88},{128,120},{160,152},{192,184},{224,216},{3... | collective-permute-start | bytes 1966088 | tf_op jit(solution)/shard_map/ppermute | solution.py:750
  44.2 14.7 %copy-start.12 = (bf16[4,48,1024]{2,1,0:T(8,128)(2,1)}, bf16[4,48,1024]{2,1,0:T(8,128)(2,1)S(1)}, u32[]{:S(2)}) copy-start(bf16[4,48,1024]{2,1,0:T(8,128)(2,1)S(1)} %collective-permute-done.near1) | copy-start | bytes 1179652
  44.2 25.5 %collective-permute-start.1 = (bf16[4,80,1024]{2,1,0:T(8,128)(2,1)S(1)}, bf16[4,80,1024]{2,1,0:T(8,128)(2,1)S(1)}, u32[]{:S(2)}, u32[]{:S(2)}) collective-permute-start(bf16[4,80,1024]{2,1,0:T(8,128)(2,1)S(1)} %copy-done.1), channel_id=1, source_target_pairs={{8,0},{16,8},{24,16},{40,32},{48,40},{56,48},{72,64},{80,72},{88,8... | collective-permute-start | bytes 1966088 | tf_op jit(solution)/shard_map/ppermute | solution.py:755
  45.5 10.8 %collective-permute-start.4 = (bf16[128,1536]{1,0:T(8,128)(2,1)}, bf16[128,1536]{1,0:T(8,128)(2,1)}, u32[]{:S(2)}, u32[]{:S(2)}) collective-permute-start(bf16[128,1536]{1,0:T(8,128)(2,1)} %get-tuple-element.46.refs_0_), channel_id=1, source_target_pairs={{0,1},{1,0},{2,3},{3,2},{4,5},{5,4},{6,7},{7,6},{8,9},{9,8},{10,11... | collective-permute-start | bytes 1179656 | tf_op jit(solution)/shard_map/ppermute | solution.py:739
  45.6 10.7 %collective-permute-start.5 = (bf16[128,1536]{1,0:T(8,128)(2,1)}, bf16[128,1536]{1,0:T(8,128)(2,1)}, u32[]{:S(2)}, u32[]{:S(2)}) collective-permute-start(bf16[128,1536]{1,0:T(8,128)(2,1)} %get-tuple-element.47.refs_1_), channel_id=1, source_target_pairs={{0,1},{1,0},{2,3},{3,2},{4,5},{5,4},{6,7},{7,6},{8,9},{9,8},{10,11... | collective-permute-start | bytes 1179656 | tf_op jit(solution)/shard_map/ppermute | solution.py:739
  46.1 23.5 %collective-permute-start.3 = (bf16[4,48,1024]{2,1,0:T(8,128)(2,1)S(1)}, bf16[4,48,1024]{2,1,0:T(8,128)(2,1)}, u32[]{:S(2)}, u32[]{:S(2)}) collective-permute-start(bf16[4,48,1024]{2,1,0:T(8,128)(2,1)S(1)} %collective-permute-done.near1), channel_id=1, source_target_pairs={{56,24},{88,56},{120,88},{152,120},{184,152},{216,184},{248,216},{... | collective-permute-start | bytes 1179656 | tf_op jit(solution)/shard_map/ppermute | solution.py:754
  56.3 22.1 %collective-permute-start.6 = (bf16[128,2560]{1,0:T(8,128)(2,1)}, bf16[128,2560]{1,0:T(8,128)(2,1)S(1)}, u32[]{:S(2)}, u32[]{:S(2)}) collective-permute-start(bf16[128,2560]{1,0:T(8,128)(2,1)} %get-tuple-element.50.refs_0_), channel_id=1, source_target_pairs={{0,1},{1,0},{2,3},{3,2},{4,5},{5,4},{6,7},{7,6},{8,9},{9,8},{10,11... | collective-permute-start | bytes 1966088 | tf_op jit(solution)/shard_map/ppermute | solution.py:739
  58.9 10.7 %copy-start.6 = (bf16[4,80,1024]{2,1,0:T(8,128)(2,1)}, bf16[4,80,1024]{2,1,0:T(8,128)(2,1)S(1)}, u32[]{:S(2)}) copy-start(bf16[4,80,1024]{2,1,0:T(8,128)(2,1)S(1)} %collective-permute-done.2.far0) | copy-start | bytes 1966084
  69.6 0.8 copy-start.7
  70.5 7.8 %copy-start.4 = (bf16[4,48,1024]{2,1,0:T(8,128)(2,1)S(1)}, bf16[4,48,1024]{2,1,0:T(8,128)(2,1)}, u32[]{:S(2)}) copy-start(bf16[4,48,1024]{2,1,0:T(8,128)(2,1)} %get-tuple-element.42) | copy-start | bytes 1179652
  78.2 2.4 %collective-permute-start.7 = (bf16[128,2560]{1,0:T(8,128)(2,1)}, bf16[128,2560]{1,0:T(8,128)(2,1)S(1)}, u32[]{:S(2)}, u32[]{:S(2)}) collective-permute-start(bf16[128,2560]{1,0:T(8,128)(2,1)} %attention_tick.1.refs_1_.right), channel_id=1, source_target_pairs={{0,1},{1,0},{2,3},{3,2},{4,5},{5,4},{6,7},{7,6},{8,9},{9,8},{10,11... | collective-permute-start | bytes 1966088 | tf_op jit(solution)/shard_map/ppermute | solution.py:739
  78.4 2.2 %copy-start.8 = (bf16[128,2560]{1,0:T(8,128)(2,1)}, bf16[128,2560]{1,0:T(8,128)(2,1)S(1)}, u32[]{:S(2)}) copy-start(bf16[128,2560]{1,0:T(8,128)(2,1)S(1)} %collective-permute-done.6.refs_2_) | copy-start | bytes 1966084
  80.6 0.9 copy-start.9
  86.0 42.1 %collective-permute-start.9 = (bf16[128,2048]{1,0:T(8,128)(2,1)}, bf16[128,2048]{1,0:T(8,128)(2,1)S(1)}, u32[]{:S(2)}, u32[]{:S(2)}) collective-permute-start(bf16[128,2048]{1,0:T(8,128)(2,1)} %get-tuple-element.56), channel_id=1, source_target_pairs={{2,4},{3,5},{4,2},{5,3},{10,12},{11,13},{12,10},{13,11},{18,20},{1... | collective-permute-start | bytes 1572872 | tf_op jit(solution)/shard_map/ppermute | solution.py:743
  86.7 20.7 %collective-permute-start.8 = (bf16[128,2048]{1,0:T(8,128)(2,1)}, bf16[128,2048]{1,0:T(8,128)(2,1)S(1)}, u32[]{:S(2)}, u32[]{:S(2)}) collective-permute-start(bf16[128,2048]{1,0:T(8,128)(2,1)} %get-tuple-element.56), channel_id=1, source_target_pairs={{0,2},{1,3},{6,4},{7,5},{8,10},{9,11},{14,12},{15,13},{16,18},{17,... | collective-permute-start | bytes 1572872 | tf_op jit(solution)/shard_map/ppermute | solution.py:743
  93.2 31.8 %collective-permute-start.10 = (bf16[128,2048]{1,0:T(8,128)(2,1)}, bf16[128,2048]{1,0:T(8,128)(2,1)S(1)}, u32[]{:S(2)}, u32[]{:S(2)}) collective-permute-start(bf16[128,2048]{1,0:T(8,128)(2,1)} %get-tuple-element.71), channel_id=1, source_target_pairs={{0,2},{1,3},{2,0},{3,1},{4,6},{5,7},{6,4},{7,5},{8,10},{9,11},{10,... | collective-permute-start | bytes 1572872 | tf_op jit(solution)/shard_map/ppermute | solution.py:743
  93.3 34.8 %collective-permute-start.11 = (bf16[128,2048]{1,0:T(8,128)(2,1)}, bf16[128,2048]{1,0:T(8,128)(2,1)}, u32[]{:S(2)}, u32[]{:S(2)}) collective-permute-start(bf16[128,2048]{1,0:T(8,128)(2,1)} %get-tuple-element.55), channel_id=1, source_target_pairs={{0,4},{1,5},{6,2},{7,3},{8,12},{9,13},{14,10},{15,11},{16,20},{17,... | collective-permute-start | bytes 1572872 | tf_op jit(solution)/shard_map/ppermute | solution.py:743
  97.5 9.9 %copy-start.2 = (bf16[128,2048]{1,0:T(8,128)(2,1)S(1)}, bf16[128,2048]{1,0:T(8,128)(2,1)}, u32[]{:S(2)}) copy-start(bf16[128,2048]{1,0:T(8,128)(2,1)} %get-tuple-element.55) | copy-start | bytes 1572868
  107.6 1.3 copy-start.3
  107.6 31.4 %collective-permute-start.12 = (bf16[128,2048]{1,0:T(8,128)(2,1)S(1)}, bf16[128,2048]{1,0:T(8,128)(2,1)}, u32[]{:S(2)}, u32[]{:S(2)}) collective-permute-start(bf16[128,2048]{1,0:T(8,128)(2,1)S(1)} %add_convert_fusion.after), channel_id=1, source_target_pairs={{2,6},{3,7},{4,0},{5,1},{10,14},{11,15},{12,8},{13,9},{18,22},{19,... | collective-permute-start | bytes 1572872 | tf_op jit(solution)/shard_map/ppermute | solution.py:743
  118.9 23.0 %all-to-all-start = ((bf16[8,32,512]{2,1,0:T(8,128)(2,1)}), bf16[8,32,512]{2,1,0:T(8,128)(2,1)S(1)}, u32[]{:S(2)}, u32[]{:S(2)}) async-start(bf16[8,32,512]{2,1,0:T(8,128)(2,1)} %get-tuple-element.74), calls=%async_computation | async-start | bytes 524288 | tf_op jit(solution)/shard_map/all_to_all | solution.py:773
  125.0 14.0 %copy-start.11 = (bf16[128,2048]{1,0:T(8,128)(2,1)}, bf16[128,2048]{1,0:T(8,128)(2,1)S(1)}, u32[]{:S(2)}) copy-start(bf16[128,2048]{1,0:T(8,128)(2,1)S(1)} %collective-permute-done.10.refs_2_) | copy-start | bytes 1572868
  128.1 11.0 %copy-start.10 = (bf16[128,2048]{1,0:T(8,128)(2,1)}, bf16[128,2048]{1,0:T(8,128)(2,1)S(1)}, u32[]{:S(2)}) copy-start(bf16[128,2048]{1,0:T(8,128)(2,1)S(1)} %collective-permute-done.9.refs_1_) | copy-start | bytes 1572868
  141.9 0.7 copy-start.5
